TPU v7x, 128 devices: a whole 4x4x4 slice. The times are simulated.
128 devices in a mesh: row: 8 (over x, core), col: 16 (over z, y).
Axes of the slice: x: 4, y: 4, z: 4, core: 2. Of those that a mesh axis runs over, the one named last changes fastest.
Arguments:
- out_grad: bfloat16 [4096, 7, 7, 256], P(('row', 'col')), may hold values from -6 to 6
- saved: bfloat16 [2, 4096, 7, 7, 256], P(None, ('row', 'col')), may hold values from -6 to 6
- conv_weight: bfloat16 [2, 9, 256, 256], replicated, may hold values from -0.125 to 0.125
- conv_bias: float32 [2, 256], replicated, may hold values from -3 to 3
- tile_ids: int32 [4096, 4], P(('row', 'col')), may hold values from 0 to 127, all different within a row; in each aligned block of 32 rows (0 to 31, 32 to 63, ...) at most 2 rows name the same one
- corner_rows: int32 [4096, 4, 7], P(('row', 'col')), may hold values from 0 to 62
- corner_cols: int32 [4096, 4, 7], P(('row', 'col')), may hold values from 0 to 62
- row_weight: bfloat16 [4096, 4, 7, 2], P(('row', 'col')), may hold values from 0 to 1
- col_weight: bfloat16 [4096, 4, 7, 2], P(('row', 'col')), may hold values from 0 to 1
Outputs:
- weight_grad: float32 [2, 2304, 256], replicated
- bias_grad: float32 [2, 256], replicated
- feature_grad: float32 [512, 1024, 256], P('row', 'col')
Inputs may be any that keep to these rules, and one draw needn't show every extreme that they name: `tile_ids`: each box names 4 different tiles. Among the boxes of one device (aligned blocks of 32 boxes) no tile is named more than 2 times, and in some device's boxes some tile is named exactly 2 times.
All inputs are finite; a program needn't handle non-finite values.
Results may differ from a plain program's by a relative error of at most 0.015.
Values may be sent and summed in bfloat16 or wider, within the bound.
No kernel may reach another device: no remote copies, remote signals or barrier semaphores. Data moves between devices by JAX's collectives and lax.ppermute only.
A program may use at most 128 MiB of HBM per device.

v0:
```python
import functools
import math

import jax
import jax.numpy as jnp
from jax import lax
from jax.experimental import pallas as pl
from jax.experimental.pallas import tpu as pltpu
from jax.sharding import PartitionSpec as P

TILE = 64
SLOT_ROWS = 104
GROUP = 32
UNROLL = 8
VMEM = pltpu.MemorySpace.VMEM
SMEM = pltpu.MemorySpace.SMEM
AXES = ("row", "col")


def params(megabytes):
    return pltpu.CompilerParams(vmem_limit_bytes=megabytes * 1024 * 1024)


def gelu_slope(pre_act):
    normal_cdf = 0.5 * (1.0 + lax.erf(pre_act * 0.7071067811865476))
    return normal_cdf + pre_act * jnp.exp(-0.5 * pre_act * pre_act) * 0.3989422804014327


def chain_kernel(
    grad_ref, saved_ref, weight_ref, bias_ref, slope_ref, crops_ref, biases_ref, padded, slopes, flow
):
    extent, boxes, channels = grad_ref.shape[0], grad_ref.shape[2], grad_ref.shape[3]
    rows = extent * boxes
    padded[...] = jnp.zeros_like(padded)
    slopes[...] = jnp.zeros_like(slopes)
    for layer in (1, 0):
        padded[1 : extent + 1, 1 : extent + 1] = saved_ref[layer]

        def forward(i, sums, layer=layer):
            pieces = [
                padded[i + a, b : b + extent].reshape(rows, channels)
                for a in range(3)
                for b in range(3)
            ]
            pre = jnp.dot(
                jnp.concatenate(pieces, axis=1),
                weight_ref[layer].reshape(9 * channels, channels),
                preferred_element_type=jnp.float32,
            )
            pre = pre + bias_ref[layer : layer + 1, :]
            upper = grad_ref[i] if layer == 1 else flow[i]
            upper = upper.reshape(rows, channels).astype(jnp.float32)
            slope = (upper * gelu_slope(pre)).astype(jnp.bfloat16)
            slopes[i + 1, 1 : extent + 1] = slope.reshape(extent, boxes, channels)
            slope_ref[layer, i] = slope.reshape(extent, boxes, channels)
            return sums + jnp.sum(
                slope.astype(jnp.float32).reshape(rows // 8, 8, channels), axis=0
            )

        sums = lax.fori_loop(0, extent, forward, jnp.zeros((8, channels), jnp.float32))
        biases_ref[layer : layer + 1, :] = jnp.sum(sums, axis=0, keepdims=True)

        def backward(i, carry, layer=layer):
            total = jnp.zeros((rows, channels), jnp.float32)
            for a in range(3):
                for b in range(3):
                    piece = slopes[i + 2 - a, 2 - b : 2 - b + extent].reshape(rows, channels)
                    total = total + lax.dot_general(
                        piece,
                        weight_ref[layer, 3 * a + b],
                        (((1,), (1,)), ((), ())),
                        preferred_element_type=jnp.float32,
                    )
            if layer == 1:
                flow[i] = total.astype(jnp.bfloat16).reshape(extent, boxes, channels)
            else:
                place = pl.ds(pl.multiple_of(i * rows, 8), rows)
                crops_ref[0, place, :] = total[:, : channels // 2]
                crops_ref[1, place, :] = total[:, channels // 2 :]
            return carry

        lax.fori_loop(0, extent, backward, 0)


def conv_chain(grad_t, saved_t, weight, bias):
    extent, boxes, channels = grad_t.shape[0], grad_t.shape[2], grad_t.shape[3]
    layers = saved_t.shape[0]
    padded = (extent + 2, extent + 2, boxes, channels)
    return pl.pallas_call(
        chain_kernel,
        name="conv_chain",
        out_shape=(
            jax.ShapeDtypeStruct((layers, extent, extent, boxes, channels), jnp.bfloat16),
            jax.ShapeDtypeStruct((2, extent * extent * boxes, channels // 2), jnp.float32),
            jax.ShapeDtypeStruct((layers, channels), jnp.float32),
        ),
        in_specs=[pl.BlockSpec(memory_space=VMEM)] * 4,
        out_specs=(pl.BlockSpec(memory_space=VMEM),) * 3,
        scratch_shapes=[
            pltpu.VMEM(padded, jnp.bfloat16),
            pltpu.VMEM(padded, jnp.bfloat16),
            pltpu.VMEM((extent, extent, boxes, channels), jnp.bfloat16),
        ],
        compiler_params=params(40),
        cost_estimate=pl.CostEstimate(flops=15000000000, bytes_accessed=5000000, transcendentals=0),
    )(grad_t, saved_t, weight, bias)


def pack_kernel(box_ref, crops_ref, tail_ref, out_ref, held, staged):
    slots = out_ref.shape[0]
    boxes = held.shape[0]
    bins = crops_ref.shape[1] // boxes
    step = pl.program_id(0)

    @pl.when(step == 0)
    def _():
        for box in range(boxes):
            for half in range(2):
                staged[box, half * bins : (half + 1) * bins, :] = crops_ref[
                    half, pl.ds(box, bins, stride=boxes), :
                ]
            staged[box, 2 * bins :, :] = tail_ref[...]
            held[box] = staged[box].astype(jnp.bfloat16)

    def place(index, carry):
        slot = step * slots + index
        owners = box_ref.shape[0] // 2
        out_ref[index] = held[box_ref[lax.rem(slot, 2) * owners + lax.div(slot, 2)]]
        return carry

    lax.fori_loop(0, slots, place, 0, unroll=4)


def pack(box_of_slot, crops, tail, boxes):
    slots = box_of_slot.shape[0]
    steps = 8
    half = crops.shape[2]
    return pl.pallas_call(
        pack_kernel,
        name="pack",
        out_shape=jax.ShapeDtypeStruct((slots, SLOT_ROWS, half), jnp.bfloat16),
        grid_spec=pltpu.PrefetchScalarGridSpec(
            num_scalar_prefetch=1,
            grid=(steps,),
            in_specs=[
                pl.BlockSpec(crops.shape, lambda g, ids: (0, 0, 0)),
                pl.BlockSpec(tail.shape, lambda g, ids: (0, 0)),
            ],
            out_specs=pl.BlockSpec((slots // steps, SLOT_ROWS, half), lambda g, ids: (g, 0, 0)),
            scratch_shapes=[
                pltpu.VMEM((boxes, SLOT_ROWS, half), jnp.bfloat16),
                pltpu.VMEM((boxes, SLOT_ROWS, half), jnp.float32),
            ],
        ),
        compiler_params=params(24),
        cost_estimate=pl.CostEstimate(flops=1000000, bytes_accessed=9000000, transcendentals=0),
    )(box_of_slot, crops, tail)


def weight_kernel(slope_ref, saved_ref, out_ref, padded):
    extent, boxes, channels = saved_ref.shape[1], saved_ref.shape[3], saved_ref.shape[4]
    bins = extent * extent * boxes
    offset = pl.program_id(1)

    @pl.when(offset == 0)
    def _():
        padded[...] = jnp.zeros_like(padded)
        padded[1 : extent + 1, 1 : extent + 1] = saved_ref[0]

    a, b = offset // 3, offset % 3
    piece = padded[pl.ds(a, extent), pl.ds(b, extent)].reshape(bins, channels)
    term = lax.dot_general(
        piece,
        slope_ref[0].reshape(bins, channels),
        (((0,), (0,)), ((), ())),
        preferred_element_type=jnp.float32,
    )
    out_ref[0, 0, 0] = term[:, : channels // 2].astype(jnp.bfloat16)
    out_ref[0, 1, 0] = term[:, channels // 2 :].astype(jnp.bfloat16)


def weight_terms(slope, saved_t):
    layers, extent, boxes, channels = slope.shape[0], slope.shape[1], slope.shape[3], slope.shape[4]
    block = (1, extent, extent, boxes, channels)
    return pl.pallas_call(
        weight_kernel,
        name="weight_terms",
        out_shape=jax.ShapeDtypeStruct((layers, 2, 9, channels, channels // 2), jnp.bfloat16),
        grid=(layers, 9),
        in_specs=[pl.BlockSpec(block, lambda l, o: (l, 0, 0, 0, 0))] * 2,
        out_specs=pl.BlockSpec((1, 2, 1, channels, channels // 2), lambda l, o: (l, 0, o, 0, 0)),
        scratch_shapes=[pltpu.VMEM((extent + 2, extent + 2, boxes, channels), jnp.bfloat16)],
        compiler_params=params(24),
        cost_estimate=pl.CostEstimate(flops=7400000000, bytes_accessed=5000000, transcendentals=0),
    )(slope, saved_t)


def hop_core():
    return [(r, r ^ 1) for r in range(8)]


def hop_x(k):
    return [(r, (r // 2 + k) % 4 * 2 + r % 2) for r in range(8)]


def pick(array, index):
    return lax.dynamic_index_in_dim(array, index, 0, keepdims=False)


def sum_lines(terms):
    row = lax.axis_index("row")
    core, x = row % 2, row // 2
    other = lax.ppermute(pick(terms, 1 - core), "row", hop_core())
    total = pick(terms, core).astype(jnp.float32) + other.astype(jnp.float32)
    held = total.astype(jnp.bfloat16)
    sent = [pick(held, (x + k) % 4) for k in range(1, 4)]
    return held, sent


def finish_lines(held, arrived):
    total = pick(held, lax.axis_index("row") // 2).astype(jnp.float32)
    for piece in arrived:
        total = total + piece.astype(jnp.float32)
    return total


def gather_lines(part):
    ring = jnp.stack([part] + [lax.ppermute(part, "row", hop_x(k)) for k in (3, 2, 1)])
    return ring, lax.ppermute(ring, "row", hop_core())


def widen_kernel(place_ref, own_ref, other_ref, out_ref, *, scale):
    mine = pl.program_id(0) == place_ref[1]
    chunk = jnp.where(mine, own_ref[0].astype(jnp.float32), other_ref[0].astype(jnp.float32))
    out_ref[0] = chunk * scale


def widen(own, other, layers, scale):
    row = lax.axis_index("row")
    place = jnp.stack([row // 2, row % 2]).astype(jnp.int32)
    chunks, rows, half = own.shape

    def source(layer, chunk, place):
        return (lax.rem(chunk + chunks - place[0], chunks), 0, 0)

    return pl.pallas_call(
        functools.partial(widen_kernel, scale=scale),
        name="widen",
        out_shape=jax.ShapeDtypeStruct((layers, chunks // 2 * rows, 2 * half), jnp.float32),
        grid_spec=pltpu.PrefetchScalarGridSpec(
            num_scalar_prefetch=1,
            grid=(layers, chunks),
            in_specs=[pl.BlockSpec((1, rows, half), source)] * 2,
            out_specs=pl.BlockSpec(
                (1, rows, half), lambda l, m, place: (l, lax.rem(m, chunks // 2), lax.div(m, chunks // 2))
            ),
        ),
        compiler_params=params(16),
        cost_estimate=pl.CostEstimate(flops=3_000_000, bytes_accessed=10_000_000, transcendentals=0),
    )(place, own, other)


def order_kernel(rows_ref, start_ref, end_ref, entry_ref, count):
    places = start_ref.shape[0]
    extent = 7
    slots = rows_ref.shape[0] // extent

    def begin(p, carry):
        count[p] = start_ref[p]
        return carry

    lax.fori_loop(0, places, begin, 0)

    def enter(slot, carry):
        @pl.when(rows_ref[slot * extent] >= 0)
        def _():
            for i in range(extent):
                first = rows_ref[slot * extent + i]
                for a in range(2):
                    n = count[first + a]
                    count[first + a] = n + 1
                    entry_ref[n] = slot * 16 + 2 * i + a

        return carry

    lax.fori_loop(0, slots, enter, 0)

    def fill(p, carry):
        def blank(n, inner):
            entry_ref[n] = 14
            return inner

        return lax.fori_loop(count[p], end_ref[p], blank, carry)

    lax.fori_loop(0, places, fill, 0)


def order_entries(rows, start, end, entries):
    return pl.pallas_call(
        order_kernel,
        name="order_entries",
        out_shape=jax.ShapeDtypeStruct((entries,), jnp.int32),
        in_specs=[pl.BlockSpec(memory_space=SMEM)] * 3,
        out_specs=pl.BlockSpec(memory_space=SMEM),
        scratch_shapes=[pltpu.SMEM((TILE,), jnp.int32)],
        cost_estimate=pl.CostEstimate(flops=10_000_000, bytes_accessed=30_000_000, transcendentals=0),
    )(rows, start, end)


def tile_kernel(
    base_ref, place_ref, groups_ref, got_ref, columns_ref, out_ref, biases_ref, crops
):
    step = pl.program_id(0)
    slots, half = got_ref.shape[0], got_ref.shape[2]
    bins = 49
    block = slots * SLOT_ROWS
    wide = got_ref[...].astype(jnp.float32)
    crops[pl.ds(pl.multiple_of(step * block, 8), block), :] = wide.reshape(block, half)
    spare = jnp.sum(wide[:, SLOT_ROWS - 8 :, :], axis=0)

    @pl.when(step == 0)
    def _():
        biases_ref[...] = spare

    @pl.when(step > 0)
    def _():
        biases_ref[...] += spare

    @pl.when(step == pl.num_programs(0) - 1)
    def _():
        out_ref[...] = jnp.zeros_like(out_ref)

        def group(t):
            left, right = [], []
            for n in range(GROUP):
                base = base_ref[t * GROUP + n]
                left.append(crops[pl.ds(base, 8), :])
                right.append(crops[pl.ds(base + bins, 8), :])
            values = jnp.concatenate(
                [jnp.concatenate(left, axis=0), jnp.concatenate(right, axis=0)], axis=1
            ).astype(jnp.bfloat16)
            return jnp.dot(columns_ref[t], values, preferred_element_type=jnp.float32)

        def several(t, carry):
            terms = [group(t * UNROLL + u) for u in range(UNROLL)]
            for u in range(UNROLL):
                out_ref[place_ref[t * UNROLL + u]] += terms[u]
            return carry

        lax.fori_loop(0, (groups_ref[0] + UNROLL - 1) // UNROLL, several, 0)


def tile_sum(base, place, groups, got, columns, channels):
    steps = 8
    slots, half = got.shape[0], got.shape[2]
    return pl.pallas_call(
        tile_kernel,
        name="tile_sum",
        out_shape=(
            jax.ShapeDtypeStruct((TILE, TILE, channels), jnp.float32),
            jax.ShapeDtypeStruct((8, half), jnp.float32),
        ),
        grid_spec=pltpu.PrefetchScalarGridSpec(
            num_scalar_prefetch=3,
            grid=(steps,),
            in_specs=[
                pl.BlockSpec((slots // steps, SLOT_ROWS, half), lambda g, *refs: (g, 0, 0)),
                pl.BlockSpec(columns.shape, lambda g, *refs: (0, 0, 0)),
            ],
            out_specs=(
                pl.BlockSpec((TILE, TILE, channels), lambda g, *refs: (0, 0, 0)),
                pl.BlockSpec((8, half), lambda g, *refs: (0, 0)),
            ),
            scratch_shapes=[pltpu.VMEM((slots * SLOT_ROWS, half), jnp.float32)],
        ),
        compiler_params=params(48),
        cost_estimate=pl.CostEstimate(
            flops=2 * columns.size * channels, bytes_accessed=17_000_000, transcendentals=0
        ),
    )(base, place, groups, got, columns)


def fields_kernel(tiles_ref, rows_ref, cols_ref, row_weight_ref, col_weight_ref, send_ref, boxes_ref):
    per_box, boxes = tiles_ref.shape
    extent = rows_ref.shape[0]
    pieces = per_box * boxes

    def wide(parts):
        return jnp.concatenate(parts, axis=1)

    targets = wide([tiles_ref[t : t + 1, :].astype(jnp.float32) for t in range(per_box)])
    rows = wide([rows_ref[:, t, :].astype(jnp.float32) for t in range(per_box)])
    cols = wide([cols_ref[:, t, :].astype(jnp.float32) for t in range(per_box)])
    row_weight = [
        wide([row_weight_ref[t, :, a, :].astype(jnp.float32) for t in range(per_box)])
        for a in range(2)
    ]
    col_weight = [
        wide([col_weight_ref[t, :, a, :].astype(jnp.float32) for t in range(per_box)])
        for a in range(2)
    ]
    blank = jnp.zeros((1, pieces), jnp.float32)
    parts = [targets, jnp.zeros((6, pieces), jnp.float32), jnp.ones((1, pieces), jnp.float32)]
    for array in [rows, cols] + row_weight + col_weight:
        parts = parts + [array, blank]
    parts.append(jnp.zeros((8, pieces), jnp.float32))
    fields = jnp.concatenate(parts, axis=0).astype(jnp.bfloat16)
    tile = lax.broadcasted_iota(jnp.int32, (pieces, pieces), 0)
    piece = lax.broadcasted_iota(jnp.int32, (pieces, pieces), 1)
    match = targets.astype(jnp.int32) == tile
    upper = jnp.where(tile < piece, 1.0, 0.0).astype(jnp.bfloat16)
    chosen = jnp.where(match, 1.0, 0.0)
    earlier = jnp.dot(chosen.astype(jnp.bfloat16), upper, preferred_element_type=jnp.float32)
    box = (lax.broadcasted_iota(jnp.int32, (8, pieces), 1) % boxes).astype(jnp.float32)
    slots = []
    for rank in range(2):
        ranked = jnp.where(earlier == float(rank), chosen, 0.0).astype(jnp.bfloat16)
        found = lax.dot_general(
            box.astype(jnp.bfloat16),
            ranked,
            (((1,), (1,)), ((), ())),
            preferred_element_type=jnp.float32,
        )
        boxes_ref[rank : rank + 1, :] = found[:1].astype(jnp.int32)
        slots.append(
            lax.dot_general(
                ranked, fields, (((1,), (1,)), ((), ())), preferred_element_type=jnp.float32
            )
        )
    send_ref[...] = jnp.concatenate(slots, axis=1).astype(jnp.bfloat16)


def describe(tile_ids, corner_rows, corner_cols, row_weight, col_weight):
    pieces = tile_ids.size
    extent = corner_rows.shape[2]
    return pl.pallas_call(
        fields_kernel,
        name="describe",
        out_shape=(
            jax.ShapeDtypeStruct((pieces, 128), jnp.bfloat16),
            jax.ShapeDtypeStruct((2, pieces), jnp.int32),
        ),
        in_specs=[pl.BlockSpec(memory_space=VMEM)] * 5,
        out_specs=(pl.BlockSpec(memory_space=VMEM),) * 2,
        compiler_params=params(8),
        cost_estimate=pl.CostEstimate(flops=10_000_000, bytes_accessed=200_000, transcendentals=0),
    )(
        jnp.transpose(tile_ids),
        jnp.transpose(corner_rows, (2, 1, 0)),
        jnp.transpose(corner_cols, (2, 1, 0)),
        jnp.transpose(row_weight, (1, 2, 3, 0)),
        jnp.transpose(col_weight, (1, 2, 3, 0)),
    )


def arrange(slots, extent):
    count = slots.shape[0]
    groups = count * extent * 2 // GROUP + TILE
    entries = groups * GROUP
    wide = extent + 1
    rows = jnp.where(slots[:, 7:8] > 0.5, slots[:, 8 : 8 + extent], -4.0).astype(jnp.int32)
    pixel = jnp.arange(TILE, dtype=jnp.int32)
    flat = rows.reshape(-1)
    hits = (flat == pixel[:, None]).astype(jnp.int32) + (flat + 1 == pixel[:, None]).astype(jnp.int32)
    tally = jnp.sum(hits, axis=1)
    needed = (tally + GROUP - 1) // GROUP
    ends = jnp.sum(jnp.where(pixel[None, :] <= pixel[:, None], needed[None, :], 0), axis=1)
    start = (ends - needed) * GROUP
    place = jnp.sum((jnp.arange(groups)[:, None] >= ends[None, :-1]).astype(jnp.int32), axis=1)
    entry = order_entries(flat, start, ends * GROUP, entries)
    inside = jnp.arange(entries, dtype=jnp.int32) < ends[-1] * GROUP
    entry = jnp.where(inside, entry, 14)
    owner, code = entry // 16, entry % 16
    line = jnp.minimum(code // 2, extent - 1)
    base = owner * SLOT_ROWS + extent * line
    chosen = (owner[:, None] == jnp.arange(count)).astype(jnp.bfloat16)
    values = jnp.dot(chosen, slots[:, 8:].astype(jnp.bfloat16), preferred_element_type=jnp.float32)
    which = jnp.arange(2 * wide, dtype=jnp.int32)
    wanted = (which[None, :] % wide == line[:, None]) & (which[None, :] // wide == code[:, None] % 2)
    wanted = wanted & (code[:, None] < 2 * extent)
    scale = jnp.sum(jnp.where(wanted, values[:, 2 * wide : 4 * wide], 0.0), axis=1)
    corner = values[:, wide : 2 * wide]
    low = values[:, 4 * wide : 5 * wide] * scale[:, None]
    high = values[:, 5 * wide : 6 * wide] * scale[:, None]

    def lanes(array):
        return array.reshape(groups, 1, GROUP * wide)

    corner, low, high = lanes(corner), lanes(low), lanes(high)
    position = jnp.arange(TILE, dtype=jnp.float32)[None, :, None]
    columns = jnp.where(position == corner, low, 0.0) + jnp.where(position == corner + 1.0, high, 0.0)
    return base, place, ends[-1:], columns.astype(jnp.bfloat16)


def shards(
    out_grad,
    saved,
    conv_weight,
    conv_bias,
    tile_ids,
    corner_rows,
    corner_cols,
    row_weight,
    col_weight,
):
    boxes, extent, channels = out_grad.shape[0], out_grad.shape[1], out_grad.shape[3]
    layers = saved.shape[0]
    devices = lax.axis_size("row") * lax.axis_size("col")
    grad_scale = 1.0 / math.sqrt(boxes * devices * extent * extent)
    slots, box_of_slot = describe(tile_ids, corner_rows, corner_cols, row_weight, col_weight)
    slots = lax.all_to_all(
        slots.reshape(devices, 1, -1), AXES, split_axis=0, concat_axis=0, tiled=True
    )

    grad_t = jnp.transpose(out_grad, (1, 2, 0, 3))
    saved_t = jnp.transpose(saved, (0, 2, 3, 1, 4))
    slope, crops, biases = conv_chain(grad_t, saved_t, conv_weight, conv_bias)
    terms = weight_terms(slope, saved_t)
    terms, slots = lax.optimization_barrier((terms, slots))
    lines = terms.size // layers // (channels // 2)
    terms = terms.reshape(layers, 4, lines // 4, channels // 2)
    held, sent = sum_lines(terms)
    tail = jnp.pad(biases.reshape(layers * 2, channels // 2), ((0, 2), (0, 0)))
    send = pack(box_of_slot.reshape(-1), crops, tail, boxes)
    arrived = [lax.ppermute(sent[k - 1], "row", hop_x(k)) for k in range(1, 4)]
    send, arrived, slots = lax.optimization_barrier((send, arrived, slots))
    got = lax.all_to_all(send, AXES, split_axis=0, concat_axis=0, tiled=True)
    part = lax.psum(finish_lines(held, arrived).astype(jnp.bfloat16), "col")

    base, place, groups, columns = arrange(slots.reshape(2 * devices, -1).astype(jnp.float32), extent)
    got, part, columns = lax.optimization_barrier((got, part, columns))
    feature_grad, spare = tile_sum(base, place, groups, got, columns, channels)
    own, other = gather_lines(part)
    weight_grad = widen(own, other, layers, grad_scale)
    bias_grad = (spare[2 : 2 + 2 * layers] * (0.5 * grad_scale)).reshape(layers, channels)
    return (weight_grad, bias_grad, feature_grad)


def solution(mesh):
    in_specs = (
        P(AXES, None, None, None),
        P(None, AXES, None, None, None),
        P(),
        P(),
        P(AXES, None),
        P(AXES, None, None),
        P(AXES, None, None),
        P(AXES, None, None, None),
        P(AXES, None, None, None),
    )
    out_specs = (P(), P(), P("row", "col", None))
    return jax.shard_map(shards, mesh=mesh, in_specs=in_specs, out_specs=out_specs, check_vma=False)
```

profile of v0, /device:TPU:1, one launch (start us, length us, event | category | flops | bytes accessed | tf_op | source)
XLA Modules:
  0.0 275.9 jit_solution(1214079354137539405)
XLA Ops:
  11.8 11.5 %all-to-all-start = ((bf16[128,1,128]{2,1,0:T(2,128)(2,1)}), bf16[128,1,128]{2,1,0:T(2,128)(2,1)S(1)}, u32[]{:S(2)}, u32[]{:S(2)}) async-start(bf16[128,1,128]{2,1,0:T(2,128)(2,1)} %copy.19), calls=%async_computation | async-start | bytes 131072 | tf_op jit(solution)/shard_map/all_to_all | solution.py:511
  28.2 15.3 %conv_chain.1 = (bf16[2,7,7,32,256]{4,3,2,1,0:T(8,128)(2,1)S(1)}, f32[2,1568,128]{2,1,0:T(8,128)S(1)}, f32[2,256]{1,0:T(2,128)S(1)}) custom-call(bf16[7,7,32,256]{3,2,1,0:T(8,128)(2,1)S(1)} %bitcast.43, bf16[2,7,7,32,256]{4,3,2,1,0:T(8,128)(2,1)S(1)} %bitcast.41, bf16[2,9,256,256]{3,2,1,0:T(8,128)(2,1)S(1)} %copy-done.9, f32[2,256]{1,0:T(2,128)S(1)} %copy-done.12), custom_call_target="tpu_custom_call" | custom-call | flops 15000000512 | bytes 5000000 | tf_op jit(solution)/shard_map/conv_chain/pallas_call | solution.py:89
  43.6 8.9 %weight_terms.1 = bf16[2,2,9,256,128]{4,3,2,1,0:T(8,128)(2,1)S(1)} custom-call(bf16[2,7,7,32,256]{4,3,2,1,0:T(8,128)(2,1)S(1)} %get-tuple-element.23.slope_ref, bf16[2,7,7,32,256]{4,3,2,1,0:T(8,128)(2,1)S(1)} %bitcast.42), custom_call_target="tpu_custom_call" | custom-call | flops 7400000000 | bytes 5000000 | tf_op jit(solution)/shard_map/weight_terms/pallas_call | solution.py:185
  54.4 2.6 collective-permute-done
  59.4 1.9 collective-permute-start.3
  62.5 3.7 %pack.1 = bf16[256,104,128]{2,1,0:T(8,128)(2,1)S(1)} custom-call(s32[256]{0:T(256)S(1)} %bitcast.40, f32[2,1568,128]{2,1,0:T(8,128)S(1)} %copy-done.3, f32[6,128]{1,0:T(8,128)S(1)} %pad.4.tail_ref), custom_call_target="tpu_custom_call" | custom-call | flops 1000000 | bytes 9000000 | tf_op jit(solution)/shard_map/pack/pallas_call | solution.py:138
  66.2 2.9 %copy-done = bf16[256,104,128]{2,1,0:T(8,128)(2,1)} copy-done((bf16[256,104,128]{2,1,0:T(8,128)(2,1)}, bf16[256,104,128]{2,1,0:T(8,128)(2,1)S(1)}, u32[]{:S(2)}) %copy-start) | copy-done | bytes 6815768
  69.1 1.8 collective-permute-done.2
  70.9 7.3 %collective-permute-done.1 = bf16[1152,128]{1,0:T(8,128)(2,1)} collective-permute-done((bf16[1152,128]{1,0:T(8,128)(2,1)S(1)}, bf16[1152,128]{1,0:T(8,128)(2,1)}, u32[]{:S(2)}, u32[]{:S(2)}) %collective-permute-start.1) | collective-permute-done | bytes 294944 | tf_op jit(solution)/shard_map/ppermute | solution.py:525
  78.2 8.0 %all-to-all-start.1 = ((bf16[256,104,128]{2,1,0:T(8,128)(2,1)}), bf16[256,104,128]{2,1,0:T(8,128)(2,1)}, u32[]{:S(2)}, u32[]{:S(2)}) async-start(bf16[256,104,128]{2,1,0:T(8,128)(2,1)} %copy-done), calls=%async_computation.1 | async-start | bytes 13631488 | tf_op jit(solution)/shard_map/all_to_all | solution.py:527
  86.2 2.0 fusion.5
  91.2 27.3 %order_entries.1 = s32[5632]{0:T(1024)} custom-call(s32[1792]{0:T(1024)} %copy-done.15, s32[64]{0:T(128)} %get-tuple-element.48.start_ref, s32[64]{0:T(128)} %get-tuple-element.47.end_ref), custom_call_target="tpu_custom_call" | custom-call | flops 10000000 | bytes 30000000 | tf_op jit(solution)/shard_map/order_entries/pallas_call | solution.py:299
  122.2 1.8 broadcast_in_dim.81
  124.9 1.8 broadcast_in_dim.84
  127.5 1.8 eq.118
  129.3 5.8 %add_convert_fusion.columns_ref = bf16[176,64,256]{2,1,0:T(8,128)(2,1)} fusion(f32[176,256]{1,0:T(8,128)S(1)} %broadcast_in_dim.84, f32[176,256]{1,0:T(8,128)S(1)} %broadcast_add_fusion, f32[176,256]{1,0:T(8,128)S(1)} %broadcast_in_dim.81, f32[176,256]{1,0:T(8,128)S(1)} %eq.118), kind=kLoop, calls=%fused_computation | loop fusion | flops 17301504 | bytes 6488064 | tf_op jit(solution)/shard_map/convert_element_type | solution.py:492
  135.1 93.3 %all-reduce.3.cloned.1.call-done = bf16[1152,128]{1,0:T(8,128)(2,1)} async-done(((bf16[1152,128]{1,0:T(8,128)(2,1)}), bf16[1152,128]{1,0:T(8,128)(2,1)}) %all-reduce.3.cloned.1.call-update) | async-done | bytes 294928 | tf_op jit(solution)/shard_map/psum | solution.py:528
  229.6 2.4 collective-permute-start.5
  233.1 3.2 %collective-permute-done.6 = bf16[1152,128]{1,0:T(8,128)(2,1)S(1)} collective-permute-done((bf16[1152,128]{1,0:T(8,128)(2,1)}, bf16[1152,128]{1,0:T(8,128)(2,1)S(1)}, u32[]{:S(2)}, u32[]{:S(2)}) %collective-permute-start.6) | collective-permute-done | bytes 294944 | tf_op jit(solution)/shard_map/ppermute | solution.py:228
  236.3 7.2 %collective-permute-done.5 = bf16[1152,128]{1,0:T(8,128)(2,1)S(1)} collective-permute-done((bf16[1152,128]{1,0:T(8,128)(2,1)}, bf16[1152,128]{1,0:T(8,128)(2,1)S(1)}, u32[]{:S(2)}, u32[]{:S(2)}) %collective-permute-start.5) | collective-permute-done | bytes 294944 | tf_op jit(solution)/shard_map/ppermute | solution.py:228
  245.2 2.4 collective-permute-start.7
  247.8 2.6 copy-done.1
  250.5 13.6 %tile_sum.1 = (f32[64,64,256]{2,1,0:T(8,128)}, f32[8,128]{1,0:T(8,128)S(1)}) custom-call(s32[5632]{0:T(1024)S(1)} %get-tuple-element.37.base_ref, s32[176]{0:T(256)S(1)} %convert_reduce_fusion.place_ref, s32[1]{0:T(128)} %slice.34.groups_ref, bf16[256,104,128]{2,1,0:T(8,128)(2,1)} %all-to-all-done.1.got_ref, bf16[176,64,256]{2,1,0:T(8,128)(2,1)S(1)} %copy-done.1), custom_call_target="tpu_custom_call" | custom-call | flops 1476395008 | bytes 17000000 | tf_op jit(solution)/shard_map/tile_sum/pallas_call | solution.py:356
  264.7 4.3 %widen.1 = f32[2,2304,256]{2,1,0:T(8,128)} custom-call(s32[2]{0:T(128)S(1)} %pad_add_fusion.place_ref, bf16[4,1152,128]{2,1,0:T(8,128)(2,1)S(1)} %pad_maximum_fusion.own_ref, bf16[4,1152,128]{2,1,0:T(8,128)(2,1)S(1)} %collective-permute-done.7.other_ref), custom_call_target="tpu_custom_call" | custom-call | flops 3000000 | bytes 10000000 | tf_op jit(solution)/shard_map/widen/pallas_call | solution.py:246
  (76 shorter events, 27.4 us)
Async XLA Ops:
  7.2 0.7 copy-start.4
  7.9 0.7 copy-start.5
  8.6 0.7 copy-start.6
  9.3 0.7 copy-start.7
  11.8 40.7 %all-to-all-start = ((bf16[128,1,128]{2,1,0:T(2,128)(2,1)}), bf16[128,1,128]{2,1,0:T(2,128)(2,1)S(1)}, u32[]{:S(2)}, u32[]{:S(2)}) async-start(bf16[128,1,128]{2,1,0:T(2,128)(2,1)} %copy.19), calls=%async_computation | async-start | bytes 131072 | tf_op jit(solution)/shard_map/all_to_all | solution.py:511
  23.3 1.7 copy-start.9
  25.0 1.4 copy-start.10
  26.4 1.1 copy-start.11
  43.6 8.9 %copy-start.2 = (f32[2,1568,128]{2,1,0:T(8,128)}, f32[2,1568,128]{2,1,0:T(8,128)S(1)}, u32[]{:S(2)}) copy-start(f32[2,1568,128]{2,1,0:T(8,128)S(1)} %get-tuple-element.21.crops_ref) | copy-start | bytes 4816900
  53.3 3.8 %collective-permute-start = (bf16[4,1152,128]{2,1,0:T(8,128)(2,1)S(1)}, bf16[4,1152,128]{2,1,0:T(8,128)(2,1)}, u32[]{:S(2)}, u32[]{:S(2)}) collective-permute-start(bf16[4,1152,128]{2,1,0:T(8,128)(2,1)S(1)} %dynamic-slice_bitcast_fusion), channel_id=1, source_target_pairs={{0,16},{16,0},{32,48},{48,32},{64,80},{80,64},{96,112},{112,96},{1... | collective-permute-start | bytes 3538952 | tf_op jit(solution)/shard_map/ppermute | solution.py:213
  58.6 3.9 %copy-start.3 = (f32[2,1568,128]{2,1,0:T(8,128)S(1)}, f32[2,1568,128]{2,1,0:T(8,128)}, u32[]{:S(2)}) copy-start(f32[2,1568,128]{2,1,0:T(8,128)} %copy-done.2) | copy-start | bytes 4816900
  59.4 9.7 %collective-permute-start.3 = (bf16[1152,128]{1,0:T(8,128)(2,1)}, bf16[1152,128]{1,0:T(8,128)(2,1)}, u32[]{:S(2)}, u32[]{:S(2)}) collective-permute-start(bf16[1152,128]{1,0:T(8,128)(2,1)} %get-tuple-element.43), channel_id=1, source_target_pairs={{0,96},{16,112},{32,0},{48,16},{64,32},{80,48},{96,64},{112,80},{1... | collective-permute-start | bytes 884744 | tf_op jit(solution)/shard_map/ppermute | solution.py:525
  61.3 9.6 %collective-permute-start.2 = (bf16[1152,128]{1,0:T(8,128)(2,1)S(1)}, bf16[1152,128]{1,0:T(8,128)(2,1)}, u32[]{:S(2)}, u32[]{:S(2)}) collective-permute-start(bf16[1152,128]{1,0:T(8,128)(2,1)S(1)} %get-tuple-element.44), channel_id=1, source_target_pairs={{0,64},{16,80},{32,96},{48,112},{64,0},{80,16},{96,32},{112,48},{1... | collective-permute-start | bytes 884744 | tf_op jit(solution)/shard_map/ppermute | solution.py:525
  61.9 16.3 %collective-permute-start.1 = (bf16[1152,128]{1,0:T(8,128)(2,1)S(1)}, bf16[1152,128]{1,0:T(8,128)(2,1)}, u32[]{:S(2)}, u32[]{:S(2)}) collective-permute-start(bf16[1152,128]{1,0:T(8,128)(2,1)S(1)} %get-tuple-element.45), channel_id=1, source_target_pairs={{0,32},{16,48},{32,64},{48,80},{64,96},{80,112},{96,0},{112,16},{1... | collective-permute-start | bytes 884744 | tf_op jit(solution)/shard_map/ppermute | solution.py:525
  66.2 2.9 %copy-start = (bf16[256,104,128]{2,1,0:T(8,128)(2,1)}, bf16[256,104,128]{2,1,0:T(8,128)(2,1)S(1)}, u32[]{:S(2)}) copy-start(bf16[256,104,128]{2,1,0:T(8,128)(2,1)S(1)} %pack.1) | copy-start | bytes 20447236
  69.1 19.1 %copy-start.14 = (bf16[128,1,128]{2,1,0:T(2,128)(2,1)S(1)}, bf16[128,1,128]{2,1,0:T(2,128)(2,1)}, u32[]{:S(2)}) copy-start(bf16[128,1,128]{2,1,0:T(2,128)(2,1)} %copy-done.13) | copy-start | bytes 98308
  78.2 150.2 %all-to-all-start.1 = ((bf16[256,104,128]{2,1,0:T(8,128)(2,1)}), bf16[256,104,128]{2,1,0:T(8,128)(2,1)}, u32[]{:S(2)}, u32[]{:S(2)}) async-start(bf16[256,104,128]{2,1,0:T(8,128)(2,1)} %copy-done), calls=%async_computation.1 | async-start | bytes 13631488 | tf_op jit(solution)/shard_map/all_to_all | solution.py:527
  86.1 142.2 %all-reduce.3.cloned.1.call-start = ((), (), s32[]{:S(2)}) async-start(), calls=%async_computation.2 | async-start | bytes 589824 | tf_op jit(solution)/shard_map/psum | solution.py:528
  89.1 2.1 copy-start.15
  228.4 7.9 %collective-permute-start.6 = (bf16[1152,128]{1,0:T(8,128)(2,1)}, bf16[1152,128]{1,0:T(8,128)(2,1)S(1)}, u32[]{:S(2)}, u32[]{:S(2)}) collective-permute-start(bf16[1152,128]{1,0:T(8,128)(2,1)} %all-reduce.3.cloned.1.call-done), channel_id=1, source_target_pairs={{0,32},{16,48},{32,64},{48,80},{64,96},{80,112},{96,0},{112,16},{1... | collective-permute-start | bytes 884744 | tf_op jit(solution)/shard_map/ppermute | solution.py:228
  229.6 14.0 %collective-permute-start.5 = (bf16[1152,128]{1,0:T(8,128)(2,1)}, bf16[1152,128]{1,0:T(8,128)(2,1)S(1)}, u32[]{:S(2)}, u32[]{:S(2)}) collective-permute-start(bf16[1152,128]{1,0:T(8,128)(2,1)} %all-reduce.3.cloned.1.call-done), channel_id=1, source_target_pairs={{0,64},{16,80},{32,96},{48,112},{64,0},{80,16},{96,32},{112,48},{1... | collective-permute-start | bytes 884744 | tf_op jit(solution)/shard_map/ppermute | solution.py:228
  232.0 12.1 %collective-permute-start.4 = (bf16[1152,128]{1,0:T(8,128)(2,1)}, bf16[1152,128]{1,0:T(8,128)(2,1)S(1)}, u32[]{:S(2)}, u32[]{:S(2)}) collective-permute-start(bf16[1152,128]{1,0:T(8,128)(2,1)} %all-reduce.3.cloned.1.call-done), channel_id=1, source_target_pairs={{0,96},{16,112},{32,0},{48,16},{64,32},{80,48},{96,64},{112,80},{1... | collective-permute-start | bytes 884744 | tf_op jit(solution)/shard_map/ppermute | solution.py:228
  245.2 19.5 %collective-permute-start.7 = (bf16[4,1152,128]{2,1,0:T(8,128)(2,1)S(1)}, bf16[4,1152,128]{2,1,0:T(8,128)(2,1)S(1)}, u32[]{:S(2)}, u32[]{:S(2)}) collective-permute-start(bf16[4,1152,128]{2,1,0:T(8,128)(2,1)S(1)} %pad_maximum_fusion.own_ref), channel_id=1, source_target_pairs={{0,16},{16,0},{32,48},{48,32},{64,80},{80,64},{96,112},{112,96},{1... | collective-permute-start | bytes 3538952 | tf_op jit(solution)/shard_map/ppermute | solution.py:229
  247.8 2.6 copy-start.1
  (3 other events, 2.0 us)
Sparse Core Ops, SparseCore 0:
  90.8 137.5 all-reduce.2
where the time goes:
time: 278 us; the launch traced here: 276 us
  waiting for transfers between devices  116 us (42%)
  Pallas kernels  73.7 us (27%)
  starting transfers between devices  30.9 us (11%)
  local copies, waits for them, and re-layouts  25.4 us (9%)
  between operations  14.9 us (5%)
  other arithmetic  13.9 us (5%)
    psum x1, waiting for transfers between devices, shards(): part = lax.psum(finish_lines(held, arrived).astype(jnp.bfloat16), 'col')  93.3 us
    pallas_call x1, Pallas kernels, order_entries(): pl.pallas_call(order_kernel, name='order_entries', out_shape=jax.ShapeDty...  27.3 us
    pallas_call x1, Pallas kernels, conv_chain(): pl.pallas_call(chain_kernel, name='conv_chain', out_shape=(jax.ShapeDtype...  15.3 us
    unnamed x32, local copies, waits for them, and re-layouts  14.6 us
    pallas_call x1, Pallas kernels, tile_sum(): pl.pallas_call(tile_kernel, name='tile_sum', out_shape=(jax.ShapeDtypeStr...  13.6 us
    all_to_all x1, starting transfers between devices, shards(): lax.all_to_all(slots.reshape(devices, 1, -1), AXES, split_axis=0, concat_...  11.5 us
    ppermute x3, waiting for transfers between devices, gather_lines(): lax.ppermute(part, 'row', hop_x(k))  10.9 us
    ppermute x3, waiting for transfers between devices, shards(): arrived = [lax.ppermute(sent[k - 1], 'row', hop_x(k)) for k in range(1, 4)]  9.05 us
  transfers between devices with their start and end apart: 11, of which 7 were waited for; matrix products, arithmetic and copies ran while one was open for 8% of the time, Pallas kernels for 25%

commit v1 on v0

--- a/solution.py
+++ b/solution.py
@@ -10,6 +10,7 @@
 
 TILE = 64
 SLOT_ROWS = 104
+SUM_ROWS = 40
 GROUP = 32
 UNROLL = 8
 VMEM = pltpu.MemorySpace.VMEM
@@ -106,10 +107,11 @@
     )(grad_t, saved_t, weight, bias)
 
 
-def pack_kernel(box_ref, crops_ref, tail_ref, out_ref, held, staged):
-    slots = out_ref.shape[0]
-    boxes = held.shape[0]
+def pack_kernel(box_ref, crops_ref, tail_ref, sums_ref, out_ref, staged):
+    count = out_ref.shape[0]
+    boxes = staged.shape[0]
     bins = crops_ref.shape[1] // boxes
+    owners = box_ref.shape[0] // 2
     step = pl.program_id(0)
 
     @pl.when(step == 0)
@@ -120,41 +122,40 @@
                     half, pl.ds(box, bins, stride=boxes), :
                 ]
             staged[box, 2 * bins :, :] = tail_ref[...]
-            held[box] = staged[box].astype(jnp.bfloat16)
 
     def place(index, carry):
-        slot = step * slots + index
-        owners = box_ref.shape[0] // 2
-        out_ref[index] = held[box_ref[lax.rem(slot, 2) * owners + lax.div(slot, 2)]]
+        owner = step * count + index
+        out_ref[index] = jnp.concatenate(
+            [staged[box_ref[owner]], staged[box_ref[owners + owner]], sums_ref[index]], axis=0
+        ).astype(jnp.bfloat16)
         return carry
 
-    lax.fori_loop(0, slots, place, 0, unroll=4)
-
-
-def pack(box_of_slot, crops, tail, boxes):
-    slots = box_of_slot.shape[0]
+    lax.fori_loop(0, count, place, 0, unroll=4)
+
+
+def pack(box_of_slot, crops, tail, sums, boxes):
+    owners = sums.shape[0]
     steps = 8
     half = crops.shape[2]
+    rows = 2 * SLOT_ROWS + SUM_ROWS
     return pl.pallas_call(
         pack_kernel,
         name="pack",
-        out_shape=jax.ShapeDtypeStruct((slots, SLOT_ROWS, half), jnp.bfloat16),
+        out_shape=jax.ShapeDtypeStruct((owners, rows, half), jnp.bfloat16),
         grid_spec=pltpu.PrefetchScalarGridSpec(
             num_scalar_prefetch=1,
             grid=(steps,),
             in_specs=[
                 pl.BlockSpec(crops.shape, lambda g, ids: (0, 0, 0)),
                 pl.BlockSpec(tail.shape, lambda g, ids: (0, 0)),
+                pl.BlockSpec((owners // steps, SUM_ROWS, half), lambda g, ids: (g, 0, 0)),
             ],
-            out_specs=pl.BlockSpec((slots // steps, SLOT_ROWS, half), lambda g, ids: (g, 0, 0)),
-            scratch_shapes=[
-                pltpu.VMEM((boxes, SLOT_ROWS, half), jnp.bfloat16),
-                pltpu.VMEM((boxes, SLOT_ROWS, half), jnp.float32),
-            ],
+            out_specs=pl.BlockSpec((owners // steps, rows, half), lambda g, ids: (g, 0, 0)),
+            scratch_shapes=[pltpu.VMEM((boxes, SLOT_ROWS, half), jnp.float32)],
         ),
-        compiler_params=params(24),
-        cost_estimate=pl.CostEstimate(flops=1000000, bytes_accessed=9000000, transcendentals=0),
-    )(box_of_slot, crops, tail)
+        compiler_params=params(56),
+        cost_estimate=pl.CostEstimate(flops=1_000_000, bytes_accessed=9_000_000, transcendentals=0),
+    )(box_of_slot, crops, tail, sums)
 
 
 def weight_kernel(slope_ref, saved_ref, out_ref, padded):
@@ -203,59 +204,74 @@
     return [(r, (r // 2 + k) % 4 * 2 + r % 2) for r in range(8)]
 
 
+def hop_y(k):
+    return [(c, c // 4 * 4 + (c % 4 + k) % 4) for c in range(16)]
+
+
+def hop_z(k):
+    return [(c, (c // 4 + k) % 4 * 4 + c % 4) for c in range(16)]
+
+
 def pick(array, index):
     return lax.dynamic_index_in_dim(array, index, 0, keepdims=False)
 
 
-def sum_lines(terms):
-    row = lax.axis_index("row")
-    core, x = row % 2, row // 2
+def sum_chip(terms, owners):
+    core = lax.axis_index("row") % 2
     other = lax.ppermute(pick(terms, 1 - core), "row", hop_core())
     total = pick(terms, core).astype(jnp.float32) + other.astype(jnp.float32)
-    held = total.astype(jnp.bfloat16)
-    sent = [pick(held, (x + k) % 4) for k in range(1, 4)]
-    return held, sent
-
-
-def finish_lines(held, arrived):
-    total = pick(held, lax.axis_index("row") // 2).astype(jnp.float32)
-    for piece in arrived:
-        total = total + piece.astype(jnp.float32)
-    return total
-
-
-def gather_lines(part):
-    ring = jnp.stack([part] + [lax.ppermute(part, "row", hop_x(k)) for k in (3, 2, 1)])
-    return ring, lax.ppermute(ring, "row", hop_core())
+    total = jnp.pad(total, ((0, owners * SUM_ROWS - total.shape[0]), (0, 0)))
+    return total.reshape(owners, SUM_ROWS, total.shape[1])
+
+
+def ring(part, name, hop):
+    return jnp.stack([part] + [lax.ppermute(part, name, hop(k)) for k in (3, 2, 1)])
 
 
 def widen_kernel(place_ref, own_ref, other_ref, out_ref, *, scale):
-    mine = pl.program_id(0) == place_ref[1]
-    chunk = jnp.where(mine, own_ref[0].astype(jnp.float32), other_ref[0].astype(jnp.float32))
-    out_ref[0] = chunk * scale
-
-
-def widen(own, other, layers, scale):
-    row = lax.axis_index("row")
-    place = jnp.stack([row // 2, row % 2]).astype(jnp.int32)
-    chunks, rows, half = own.shape
-
-    def source(layer, chunk, place):
-        return (lax.rem(chunk + chunks - place[0], chunks), 0, 0)
-
+    length, half = out_ref.shape[1], out_ref.shape[2] // 2
+    turns = [[lax.rem(q + 4 - place_ref[axis], 4) for q in range(4)] for axis in range(3)]
+
+    def copy(core, source_ref):
+        for x in range(4):
+            for z in range(4):
+                for y in range(4):
+                    start = (((x * 2 + core) * 4 + z) * 4 + y) * SUM_ROWS
+                    values = source_ref[turns[0][x], turns[1][y], turns[2][z]].astype(jnp.float32)
+                    values = values * scale
+                    for column in range(2):
+                        low = max(start, column * length)
+                        high = min(start + SUM_ROWS, (column + 1) * length)
+                        if low < high:
+                            out_ref[
+                                :,
+                                low - column * length : high - column * length,
+                                column * half : (column + 1) * half,
+                            ] = values[:, low - start : high - start, :]
+
+    for core in range(2):
+
+        @pl.when(place_ref[3] == core)
+        def _(core=core):
+            copy(core, own_ref)
+            copy(1 - core, other_ref)
+
+
+def widen(own, other, length, scale):
+    row, col = lax.axis_index("row"), lax.axis_index("col")
+    place = jnp.stack([row // 2, col % 4, col // 4, row % 2]).astype(jnp.int32)
+    layers, half = own.shape[3], own.shape[5]
     return pl.pallas_call(
         functools.partial(widen_kernel, scale=scale),
         name="widen",
-        out_shape=jax.ShapeDtypeStruct((layers, chunks // 2 * rows, 2 * half), jnp.float32),
-        grid_spec=pltpu.PrefetchScalarGridSpec(
-            num_scalar_prefetch=1,
-            grid=(layers, chunks),
-            in_specs=[pl.BlockSpec((1, rows, half), source)] * 2,
-            out_specs=pl.BlockSpec(
-                (1, rows, half), lambda l, m, place: (l, lax.rem(m, chunks // 2), lax.div(m, chunks // 2))
-            ),
-        ),
-        compiler_params=params(16),
+        out_shape=jax.ShapeDtypeStruct((layers, length, 2 * half), jnp.float32),
+        in_specs=[
+            pl.BlockSpec(memory_space=SMEM),
+            pl.BlockSpec(memory_space=VMEM),
+            pl.BlockSpec(memory_space=VMEM),
+        ],
+        out_specs=pl.BlockSpec(memory_space=VMEM),
+        compiler_params=params(24),
         cost_estimate=pl.CostEstimate(flops=3_000_000, bytes_accessed=10_000_000, transcendentals=0),
     )(place, own, other)
 
@@ -311,12 +327,12 @@
     base_ref, place_ref, groups_ref, got_ref, columns_ref, out_ref, biases_ref, crops
 ):
     step = pl.program_id(0)
-    slots, half = got_ref.shape[0], got_ref.shape[2]
+    owners, half = got_ref.shape[0], got_ref.shape[2]
     bins = 49
-    block = slots * SLOT_ROWS
-    wide = got_ref[...].astype(jnp.float32)
+    block = 2 * owners * SLOT_ROWS
+    wide = got_ref[...].astype(jnp.float32)[:, : 2 * SLOT_ROWS, :]
     crops[pl.ds(pl.multiple_of(step * block, 8), block), :] = wide.reshape(block, half)
-    spare = jnp.sum(wide[:, SLOT_ROWS - 8 :, :], axis=0)
+    spare = jnp.sum(wide[:, SLOT_ROWS - 8 : SLOT_ROWS, :], axis=0)
 
     @pl.when(step == 0)
     def _():
@@ -352,7 +368,7 @@
 
 def tile_sum(base, place, groups, got, columns, channels):
     steps = 8
-    slots, half = got.shape[0], got.shape[2]
+    owners, rows, half = got.shape
     return pl.pallas_call(
         tile_kernel,
         name="tile_sum",
@@ -364,14 +380,14 @@
             num_scalar_prefetch=3,
             grid=(steps,),
             in_specs=[
-                pl.BlockSpec((slots // steps, SLOT_ROWS, half), lambda g, *refs: (g, 0, 0)),
+                pl.BlockSpec((owners // steps, rows, half), lambda g, *refs: (g, 0, 0)),
                 pl.BlockSpec(columns.shape, lambda g, *refs: (0, 0, 0)),
             ],
             out_specs=(
                 pl.BlockSpec((TILE, TILE, channels), lambda g, *refs: (0, 0, 0)),
                 pl.BlockSpec((8, half), lambda g, *refs: (0, 0)),
             ),
-            scratch_shapes=[pltpu.VMEM((slots * SLOT_ROWS, half), jnp.float32)],
+            scratch_shapes=[pltpu.VMEM((2 * owners * SLOT_ROWS, half), jnp.float32)],
         ),
         compiler_params=params(48),
         cost_estimate=pl.CostEstimate(
@@ -517,22 +533,25 @@
     slope, crops, biases = conv_chain(grad_t, saved_t, conv_weight, conv_bias)
     terms = weight_terms(slope, saved_t)
     terms, slots = lax.optimization_barrier((terms, slots))
-    lines = terms.size // layers // (channels // 2)
-    terms = terms.reshape(layers, 4, lines // 4, channels // 2)
-    held, sent = sum_lines(terms)
+    sums = sum_chip(terms.reshape(layers, -1, channels // 2), devices)
     tail = jnp.pad(biases.reshape(layers * 2, channels // 2), ((0, 2), (0, 0)))
-    send = pack(box_of_slot.reshape(-1), crops, tail, boxes)
-    arrived = [lax.ppermute(sent[k - 1], "row", hop_x(k)) for k in range(1, 4)]
-    send, arrived, slots = lax.optimization_barrier((send, arrived, slots))
+    send = pack(box_of_slot.reshape(-1), crops, tail, sums, boxes)
+    send, slots = lax.optimization_barrier((send, slots))
     got = lax.all_to_all(send, AXES, split_axis=0, concat_axis=0, tiled=True)
-    part = lax.psum(finish_lines(held, arrived).astype(jnp.bfloat16), "col")
 
     base, place, groups, columns = arrange(slots.reshape(2 * devices, -1).astype(jnp.float32), extent)
-    got, part, columns = lax.optimization_barrier((got, part, columns))
+    got, columns = lax.optimization_barrier((got, columns))
+    cols = lax.axis_size("col")
+    arrived = got[:, 2 * SLOT_ROWS :, :].reshape(-1, layers, cols, SUM_ROWS, channels // 2)
+    part = jnp.sum(arrived.astype(jnp.float32), axis=(0, 2)).astype(jnp.bfloat16)
+    part = ring(ring(part, "col", hop_z), "col", hop_y)
+    part, got = lax.optimization_barrier((part, got))
+    own = ring(part, "row", hop_x)
     feature_grad, spare = tile_sum(base, place, groups, got, columns, channels)
-    own, other = gather_lines(part)
-    weight_grad = widen(own, other, layers, grad_scale)
-    bias_grad = (spare[2 : 2 + 2 * layers] * (0.5 * grad_scale)).reshape(layers, channels)
+    own, feature_grad = lax.optimization_barrier((own, feature_grad))
+    other = lax.ppermute(own, "row", hop_core())
+    weight_grad = widen(own, other, 9 * channels, grad_scale)
+    bias_grad = (spare[2 : 2 + 2 * layers] * grad_scale).reshape(layers, channels)
     return (weight_grad, bias_grad, feature_grad)
 
 

time: 278 us -> 223 us (0.80)
  waiting for transfers between devices: 116 us -> 61.7 us
  between operations: 14.9 us -> 1.56 us
  starting transfers between devices: 30.9 us -> 42.8 us
  other arithmetic: 13.9 us -> 9.96 us
  Pallas kernels: 73.7 us -> 77.3 us
    psum x1 -> x0, waiting for transfers between devices: 93.3 us -> none  [shards(): part = lax.psum(finish_lines(held, arrived).astype(jnp.bfloat16), 'col')]
    all_to_all x1, waiting for transfers between devices: 0.01 us -> 53.1 us  [shards(): got = lax.all_to_all(send, AXES, split_axis=0, concat_axis=0, tiled=True)]
    ppermute x8 -> x11, waiting for transfers between devices: 22.6 us -> 8.53 us  [the longest x9 4.48 us: ring(): lax.ppermute(part, name, hop(k))]
    ppermute x8 -> x11, starting transfers between devices: 11.4 us -> 21.8 us  [the longest x9 14.6 us: ring(): lax.ppermute(part, name, hop(k))]
    pallas_call x1, Pallas kernels: 3.75 us -> 9.59 us  [pack(): pl.pallas_call(pack_kernel, name='pack', out_shape=jax.ShapeDtypeStruct((...]
    convert_element_type x2 -> x0, other arithmetic: 3.59 us -> none  [the longest x1 2.02 us: shards(): part = lax.psum(finish_lines(held, arrived).astype(jnp.bfloat16), 'col')]
    unnamed x32 -> x30, local copies, waits for them, and re-layouts: 14.6 us -> 12.2 us
  transfers between devices with their start and end apart: 11 -> 13, of which waited for: 7 -> 7; matrix products, arithmetic and copies ran while one was open for 8% -> 9% of each run, Pallas kernels for 25% -> 29%
where the time goes in v1:
time: 223 us; the launch traced here: 221 us
  Pallas kernels  77.3 us (35%)
  waiting for transfers between devices  61.7 us (28%)
  starting transfers between devices  42.8 us (19%)
  local copies, waits for them, and re-layouts  27 us (12%)
  other arithmetic  9.96 us (4%)
    all_to_all x1, waiting for transfers between devices, shards(): got = lax.all_to_all(send, AXES, split_axis=0, concat_axis=0, tiled=True)  53.1 us
    pallas_call x1, Pallas kernels, order_entries(): pl.pallas_call(order_kernel, name='order_entries', out_shape=jax.ShapeDty...  26.2 us
    pallas_call x1, Pallas kernels, conv_chain(): pl.pallas_call(chain_kernel, name='conv_chain', out_shape=(jax.ShapeDtype...  15.4 us
    ppermute x9, starting transfers between devices, ring(): lax.ppermute(part, name, hop(k))  14.6 us
    pallas_call x1, Pallas kernels, tile_sum(): pl.pallas_call(tile_kernel, name='tile_sum', out_shape=(jax.ShapeDtypeStr...  13.6 us
    unnamed x30, local copies, waits for them, and re-layouts  12.2 us
    all_to_all x1, starting transfers between devices, shards(): lax.all_to_all(slots.reshape(devices, 1, -1), AXES, split_axis=0, concat_...  11.5 us
    pallas_call x1, Pallas kernels, pack(): pl.pallas_call(pack_kernel, name='pack', out_shape=jax.ShapeDtypeStruct((...  9.59 us
  transfers between devices with their start and end apart: 13, of which 7 were waited for; matrix products, arithmetic and copies ran while one was open for 9% of the time, Pallas kernels for 29%

profile of v1, /device:TPU:1, one launch (start us, length us, event | category | flops | bytes accessed | tf_op | source)
XLA Modules:
  0.0 221.4 jit_solution(9600333043743431886)
XLA Ops:
  5.9 11.5 %all-to-all-start = ((bf16[128,1,128]{2,1,0:T(2,128)(2,1)}), bf16[128,1,128]{2,1,0:T(2,128)(2,1)S(1)}, u32[]{:S(2)}, u32[]{:S(2)}) async-start(bf16[128,1,128]{2,1,0:T(2,128)(2,1)} %copy.19), calls=%async_computation | async-start | bytes 131072 | tf_op jit(solution)/shard_map/all_to_all | solution.py:527
  17.4 1.7 copy-done.8
  22.3 15.4 %conv_chain.1 = (bf16[2,7,7,32,256]{4,3,2,1,0:T(8,128)(2,1)S(1)}, f32[2,1568,128]{2,1,0:T(8,128)S(1)}, f32[2,256]{1,0:T(2,128)S(1)}) custom-call(bf16[7,7,32,256]{3,2,1,0:T(8,128)(2,1)S(1)} %bitcast.47, bf16[2,7,7,32,256]{4,3,2,1,0:T(8,128)(2,1)S(1)} %bitcast.45, bf16[2,9,256,256]{3,2,1,0:T(8,128)(2,1)S(1)} %copy-done.8, f32[2,256]{1,0:T(2,128)S(1)} %copy-done.11), custom_call_target="tpu_custom_call" | custom-call | flops 15000000512 | bytes 5000000 | tf_op jit(solution)/shard_map/conv_chain/pallas_call | solution.py:90
  37.7 9.0 %weight_terms.1 = bf16[2,2,9,256,128]{4,3,2,1,0:T(8,128)(2,1)S(1)} custom-call(bf16[2,7,7,32,256]{4,3,2,1,0:T(8,128)(2,1)S(1)} %get-tuple-element.23.slope_ref, bf16[2,7,7,32,256]{4,3,2,1,0:T(8,128)(2,1)S(1)} %bitcast.46), custom_call_target="tpu_custom_call" | custom-call | flops 7400000000 | bytes 5000000 | tf_op jit(solution)/shard_map/weight_terms/pallas_call | solution.py:186
  50.1 2.1 collective-permute-done
  52.5 1.7 pad.9
  54.1 9.6 %pack.1 = bf16[128,248,128]{2,1,0:T(8,128)(2,1)} custom-call(s32[256]{0:T(256)} %bitcast.44, f32[2,1568,128]{2,1,0:T(8,128)} %copy-done.1, f32[6,128]{1,0:T(8,128)} %pad.8.tail_ref, f32[128,40,128]{2,1,0:T(8,128)} %bitcast.48), custom_call_target="tpu_custom_call" | custom-call | flops 1000000 | bytes 9000000 | tf_op jit(solution)/shard_map/pack/pallas_call | solution.py:141
  63.7 9.5 %all-to-all-start.1 = ((bf16[128,248,128]{2,1,0:T(8,128)(2,1)}), bf16[128,248,128]{2,1,0:T(8,128)(2,1)}, u32[]{:S(2)}, u32[]{:S(2)}) async-start(bf16[128,248,128]{2,1,0:T(8,128)(2,1)} %pack.1), calls=%async_computation.1 | async-start | bytes 16252928 | tf_op jit(solution)/shard_map/all_to_all | solution.py:540
  76.2 26.2 %order_entries.1 = s32[5632]{0:T(1024)} custom-call(s32[1792]{0:T(1024)} %copy-done.14, s32[64]{0:T(128)} %get-tuple-element.47.start_ref, s32[64]{0:T(128)} %get-tuple-element.46.end_ref), custom_call_target="tpu_custom_call" | custom-call | flops 10000000 | bytes 30000000 | tf_op jit(solution)/shard_map/order_entries/pallas_call | solution.py:315
  106.2 1.8 broadcast_in_dim.81
  108.8 1.8 broadcast_in_dim.84
  111.4 1.8 eq.116
  113.3 5.8 %add_convert_fusion.columns_ref = bf16[176,64,256]{2,1,0:T(8,128)(2,1)} fusion(f32[176,256]{1,0:T(8,128)S(1)} %broadcast_in_dim.84, f32[176,256]{1,0:T(8,128)S(1)} %broadcast_add_fusion, f32[176,256]{1,0:T(8,128)S(1)} %broadcast_in_dim.81, f32[176,256]{1,0:T(8,128)S(1)} %eq.116), kind=kLoop, calls=%fused_computation | loop fusion | flops 17301504 | bytes 6488064 | tf_op jit(solution)/shard_map/convert_element_type | solution.py:508
  119.1 53.1 %all-to-all-done.1.got_ref = bf16[128,248,128]{2,1,0:T(8,128)(2,1)} async-done(((bf16[128,248,128]{2,1,0:T(8,128)(2,1)}), bf16[128,248,128]{2,1,0:T(8,128)(2,1)}, u32[]{:S(2)}, u32[]{:S(2)}) %all-to-all-start.1) | async-done | bytes 8126496 | tf_op jit(solution)/shard_map/all_to_all | solution.py:540
  173.8 3.5 %collective-permute-start.3 = (bf16[2,40,128]{2,1,0:T(8,128)(2,1)S(1)}, bf16[2,40,128]{2,1,0:T(8,128)(2,1)S(1)}, u32[]{:S(2)}, u32[]{:S(2)}) collective-permute-start(bf16[2,40,128]{2,1,0:T(8,128)(2,1)S(1)} %reduce_sum.51), channel_id=1, source_target_pairs={{0,4},{1,5},{2,6},{3,7},{4,8},{5,9},{6,10},{7,11},{8,12},{9,13},{1... | collective-permute-start | bytes 61448 | tf_op jit(solution)/shard_map/ppermute | solution.py:228
  177.9 2.2 collective-permute-start.1
  181.5 2.7 %collective-permute-start.5 = (bf16[4,2,40,128]{3,2,1,0:T(8,128)(2,1)S(1)}, bf16[4,2,40,128]{3,2,1,0:T(8,128)(2,1)S(1)}, u32[]{:S(2)}, u32[]{:S(2)}) collective-permute-start(bf16[4,2,40,128]{3,2,1,0:T(8,128)(2,1)S(1)} %get-tuple-element.44), channel_id=1, source_target_pairs={{0,2},{1,3},{2,0},{3,1},{4,6},{5,7},{6,4},{7,5},{8,10},{9,11},{10,... | collective-permute-start | bytes 245768 | tf_op jit(solution)/shard_map/ppermute | solution.py:228
  186.4 1.7 collective-permute-done.4
  188.8 4.2 %collective-permute-start.8 = (bf16[4,4,2,40,128]{4,3,2,1,0:T(8,128)(2,1)S(1)}, bf16[4,4,2,40,128]{4,3,2,1,0:T(8,128)(2,1)S(1)}, u32[]{:S(2)}, u32[]{:S(2)}) collective-permute-start(bf16[4,4,2,40,128]{4,3,2,1,0:T(8,128)(2,1)S(1)} %pad_maximum_fusion.1), channel_id=1, source_target_pairs={{0,64},{16,80},{32,96},{48,112},{64,0},{80,16},{96,32},{112,48},{1... | collective-permute-start | bytes 983048 | tf_op jit(solution)/shard_map/ppermute | solution.py:228
  193.1 2.6 %copy-done = bf16[176,64,256]{2,1,0:T(8,128)(2,1)S(1)} copy-done((bf16[176,64,256]{2,1,0:T(8,128)(2,1)S(1)}, bf16[176,64,256]{2,1,0:T(8,128)(2,1)}, u32[]{:S(2)}) %copy-start) | copy-done | bytes 5767192
  195.8 13.6 %tile_sum.1 = (f32[64,64,256]{2,1,0:T(8,128)}, f32[8,128]{1,0:T(8,128)S(1)}) custom-call(s32[5632]{0:T(1024)S(1)} %get-tuple-element.37.base_ref, s32[176]{0:T(256)S(1)} %convert_reduce_fusion.place_ref, s32[1]{0:T(128)} %slice.37.groups_ref, bf16[128,248,128]{2,1,0:T(8,128)(2,1)} %all-to-all-done.1.got_ref, bf16[176,64,256]{2,1,0:T(8,128)(2,1)S(1)} %copy-done), custom_call_target="tpu_custom_call" | custom-call | flops 1476395008 | bytes 17000000 | tf_op jit(solution)/shard_map/tile_sum/pallas_call | solution.py:372
  209.5 6.1 %collective-permute-start.10 = (bf16[4,4,4,2,40,128]{5,4,3,2,1,0:T(8,128)(2,1)S(1)}, bf16[4,4,4,2,40,128]{5,4,3,2,1,0:T(8,128)(2,1)S(1)}, u32[]{:S(2)}, u32[]{:S(2)}) collective-permute-start(bf16[4,4,4,2,40,128]{5,4,3,2,1,0:T(8,128)(2,1)S(1)} %pad_maximum_fusion.own_ref), channel_id=1, source_target_pairs={{0,16},{16,0},{32,48},{48,32},{64,80},{80,64},{96,112},{112,96},{1... | collective-permute-start | bytes 3932168 | tf_op jit(solution)/shard_map/ppermute | solution.py:552
  216.3 2.0 collective-permute-done.10.other_ref
  218.3 3.1 %widen.1 = f32[2,2304,256]{2,1,0:T(8,128)} custom-call(s32[4]{0:T(128)S(1)} %pad_add_fusion.place_ref, bf16[4,4,4,2,40,128]{5,4,3,2,1,0:T(8,128)(2,1)S(1)} %pad_maximum_fusion.own_ref, bf16[4,4,4,2,40,128]{5,4,3,2,1,0:T(8,128)(2,1)S(1)} %collective-permute-done.10.other_ref), custom_call_target="tpu_custom_call" | custom-call | flops 3000000 | bytes 10000000 | tf_op jit(solution)/shard_map/widen/pallas_call | solution.py:264
  (80 shorter events, 27.3 us)
Async XLA Ops:
  0.6 0.7 copy-start.2
  1.3 0.7 copy-start.3
  2.1 0.7 copy-start.4
  2.8 0.7 copy-start.5
  5.9 40.8 %all-to-all-start = ((bf16[128,1,128]{2,1,0:T(2,128)(2,1)}), bf16[128,1,128]{2,1,0:T(2,128)(2,1)S(1)}, u32[]{:S(2)}, u32[]{:S(2)}) async-start(bf16[128,1,128]{2,1,0:T(2,128)(2,1)} %copy.19), calls=%async_computation | async-start | bytes 131072 | tf_op jit(solution)/shard_map/all_to_all | solution.py:527
  17.4 1.7 copy-start.8
  19.0 1.4 copy-start.9
  20.5 1.1 copy-start.10
  37.6 9.0 %copy-start.1 = (f32[2,1568,128]{2,1,0:T(8,128)}, f32[2,1568,128]{2,1,0:T(8,128)S(1)}, u32[]{:S(2)}) copy-start(f32[2,1568,128]{2,1,0:T(8,128)S(1)} %get-tuple-element.21.crops_ref) | copy-start | bytes 4816900
  48.4 3.8 %collective-permute-start = (bf16[4608,128]{1,0:T(8,128)(2,1)}, bf16[4608,128]{1,0:T(8,128)(2,1)S(1)}, u32[]{:S(2)}, u32[]{:S(2)}) collective-permute-start(bf16[4608,128]{1,0:T(8,128)(2,1)} %dynamic-slice_bitcast_fusion), channel_id=1, source_target_pairs={{0,16},{16,0},{32,48},{48,32},{64,80},{80,64},{96,112},{112,96},{1... | collective-permute-start | bytes 3538952 | tf_op jit(solution)/shard_map/ppermute | solution.py:221
  63.7 9.5 %copy-start.13 = (bf16[128,1,128]{2,1,0:T(2,128)(2,1)S(1)}, bf16[128,1,128]{2,1,0:T(2,128)(2,1)}, u32[]{:S(2)}) copy-start(bf16[128,1,128]{2,1,0:T(2,128)(2,1)} %copy-done.12) | copy-start | bytes 98308
  63.7 108.5 %all-to-all-start.1 = ((bf16[128,248,128]{2,1,0:T(8,128)(2,1)}), bf16[128,248,128]{2,1,0:T(8,128)(2,1)}, u32[]{:S(2)}, u32[]{:S(2)}) async-start(bf16[128,248,128]{2,1,0:T(8,128)(2,1)} %pack.1), calls=%async_computation.1 | async-start | bytes 16252928 | tf_op jit(solution)/shard_map/all_to_all | solution.py:540
  74.0 2.2 copy-start.14
  173.8 6.2 %collective-permute-start.3 = (bf16[2,40,128]{2,1,0:T(8,128)(2,1)S(1)}, bf16[2,40,128]{2,1,0:T(8,128)(2,1)S(1)}, u32[]{:S(2)}, u32[]{:S(2)}) collective-permute-start(bf16[2,40,128]{2,1,0:T(8,128)(2,1)S(1)} %reduce_sum.51), channel_id=1, source_target_pairs={{0,4},{1,5},{2,6},{3,7},{4,8},{5,9},{6,10},{7,11},{8,12},{9,13},{1... | collective-permute-start | bytes 61448 | tf_op jit(solution)/shard_map/ppermute | solution.py:228
  177.3 4.1 %collective-permute-start.2 = (bf16[2,40,128]{2,1,0:T(8,128)(2,1)S(1)}, bf16[2,40,128]{2,1,0:T(8,128)(2,1)S(1)}, u32[]{:S(2)}, u32[]{:S(2)}) collective-permute-start(bf16[2,40,128]{2,1,0:T(8,128)(2,1)S(1)} %reduce_sum.51), channel_id=1, source_target_pairs={{0,8},{1,9},{2,10},{3,11},{4,12},{5,13},{6,14},{7,15},{8,0},{9,1},... | collective-permute-start | bytes 61448 | tf_op jit(solution)/shard_map/ppermute | solution.py:228
  177.9 3.6 %collective-permute-start.1 = (bf16[2,40,128]{2,1,0:T(8,128)(2,1)S(1)}, bf16[2,40,128]{2,1,0:T(8,128)(2,1)S(1)}, u32[]{:S(2)}, u32[]{:S(2)}) collective-permute-start(bf16[2,40,128]{2,1,0:T(8,128)(2,1)S(1)} %reduce_sum.51), channel_id=1, source_target_pairs={{0,12},{1,13},{2,14},{3,15},{4,0},{5,1},{6,2},{7,3},{8,4},{9,5},{1... | collective-permute-start | bytes 61448 | tf_op jit(solution)/shard_map/ppermute | solution.py:228
  181.5 4.9 %collective-permute-start.5 = (bf16[4,2,40,128]{3,2,1,0:T(8,128)(2,1)S(1)}, bf16[4,2,40,128]{3,2,1,0:T(8,128)(2,1)S(1)}, u32[]{:S(2)}, u32[]{:S(2)}) collective-permute-start(bf16[4,2,40,128]{3,2,1,0:T(8,128)(2,1)S(1)} %get-tuple-element.44), channel_id=1, source_target_pairs={{0,2},{1,3},{2,0},{3,1},{4,6},{5,7},{6,4},{7,5},{8,10},{9,11},{10,... | collective-permute-start | bytes 245768 | tf_op jit(solution)/shard_map/ppermute | solution.py:228
  184.2 3.9 %collective-permute-start.4 = (bf16[4,2,40,128]{3,2,1,0:T(8,128)(2,1)S(1)}, bf16[4,2,40,128]{3,2,1,0:T(8,128)(2,1)S(1)}, u32[]{:S(2)}, u32[]{:S(2)}) collective-permute-start(bf16[4,2,40,128]{3,2,1,0:T(8,128)(2,1)S(1)} %get-tuple-element.44), channel_id=1, source_target_pairs={{0,3},{1,0},{2,1},{3,2},{4,7},{5,4},{6,5},{7,6},{8,11},{9,8},{10,9... | collective-permute-start | bytes 245768 | tf_op jit(solution)/shard_map/ppermute | solution.py:228
  184.2 4.5 %collective-permute-start.6 = (bf16[4,2,40,128]{3,2,1,0:T(8,128)(2,1)S(1)}, bf16[4,2,40,128]{3,2,1,0:T(8,128)(2,1)S(1)}, u32[]{:S(2)}, u32[]{:S(2)}) collective-permute-start(bf16[4,2,40,128]{3,2,1,0:T(8,128)(2,1)S(1)} %get-tuple-element.44), channel_id=1, source_target_pairs={{0,1},{1,2},{2,3},{3,0},{4,5},{5,6},{6,7},{7,4},{8,9},{9,10},{10,1... | collective-permute-start | bytes 245768 | tf_op jit(solution)/shard_map/ppermute | solution.py:228
  188.7 20.6 %collective-permute-start.9 = (bf16[4,4,2,40,128]{4,3,2,1,0:T(8,128)(2,1)S(1)}, bf16[4,4,2,40,128]{4,3,2,1,0:T(8,128)(2,1)S(1)}, u32[]{:S(2)}, u32[]{:S(2)}) collective-permute-start(bf16[4,4,2,40,128]{4,3,2,1,0:T(8,128)(2,1)S(1)} %pad_maximum_fusion.1), channel_id=1, source_target_pairs={{0,32},{16,48},{32,64},{48,80},{64,96},{80,112},{96,0},{112,16},{1... | collective-permute-start | bytes 983048 | tf_op jit(solution)/shard_map/ppermute | solution.py:228
  188.8 20.5 %collective-permute-start.8 = (bf16[4,4,2,40,128]{4,3,2,1,0:T(8,128)(2,1)S(1)}, bf16[4,4,2,40,128]{4,3,2,1,0:T(8,128)(2,1)S(1)}, u32[]{:S(2)}, u32[]{:S(2)}) collective-permute-start(bf16[4,4,2,40,128]{4,3,2,1,0:T(8,128)(2,1)S(1)} %pad_maximum_fusion.1), channel_id=1, source_target_pairs={{0,64},{16,80},{32,96},{48,112},{64,0},{80,16},{96,32},{112,48},{1... | collective-permute-start | bytes 983048 | tf_op jit(solution)/shard_map/ppermute | solution.py:228
  193.0 16.3 %collective-permute-start.7 = (bf16[4,4,2,40,128]{4,3,2,1,0:T(8,128)(2,1)S(1)}, bf16[4,4,2,40,128]{4,3,2,1,0:T(8,128)(2,1)S(1)}, u32[]{:S(2)}, u32[]{:S(2)}) collective-permute-start(bf16[4,4,2,40,128]{4,3,2,1,0:T(8,128)(2,1)S(1)} %pad_maximum_fusion.1), channel_id=1, source_target_pairs={{0,96},{16,112},{32,0},{48,16},{64,32},{80,48},{96,64},{112,80},{1... | collective-permute-start | bytes 983048 | tf_op jit(solution)/shard_map/ppermute | solution.py:228
  193.1 2.6 %copy-start = (bf16[176,64,256]{2,1,0:T(8,128)(2,1)S(1)}, bf16[176,64,256]{2,1,0:T(8,128)(2,1)}, u32[]{:S(2)}) copy-start(bf16[176,64,256]{2,1,0:T(8,128)(2,1)} %add_convert_fusion.columns_ref) | copy-start | bytes 17301508
  209.5 8.8 %collective-permute-start.10 = (bf16[4,4,4,2,40,128]{5,4,3,2,1,0:T(8,128)(2,1)S(1)}, bf16[4,4,4,2,40,128]{5,4,3,2,1,0:T(8,128)(2,1)S(1)}, u32[]{:S(2)}, u32[]{:S(2)}) collective-permute-start(bf16[4,4,4,2,40,128]{5,4,3,2,1,0:T(8,128)(2,1)S(1)} %pad_maximum_fusion.own_ref), channel_id=1, source_target_pairs={{0,16},{16,0},{32,48},{48,32},{64,80},{80,64},{96,112},{112,96},{1... | collective-permute-start | bytes 3932168 | tf_op jit(solution)/shard_map/ppermute | solution.py:552
  (4 other events, 2.5 us)

commit v2 on v1

--- a/solution.py
+++ b/solution.py
@@ -9,7 +9,6 @@
 from jax.sharding import PartitionSpec as P
 
 TILE = 64
-SLOT_ROWS = 104
 SUM_ROWS = 40
 GROUP = 32
 UNROLL = 8
@@ -28,16 +27,49 @@
 
 
 def chain_kernel(
-    grad_ref, saved_ref, weight_ref, bias_ref, slope_ref, crops_ref, biases_ref, padded, slopes, flow
+    grad_hbm,
+    saved_hbm,
+    weight_hbm,
+    bias_ref,
+    slope_ref,
+    crops_ref,
+    biases_ref,
+    both,
+    slopes,
+    flow,
+    grad_ref,
+    weight_ref,
+    sems,
 ):
     extent, boxes, channels = grad_ref.shape[0], grad_ref.shape[2], grad_ref.shape[3]
     rows = extent * boxes
-    padded[...] = jnp.zeros_like(padded)
+    inner = pl.ds(1, extent)
+    fetches = {}
+    for layer in (1, 0):
+        fetches[layer] = [
+            pltpu.make_async_copy(
+                saved_hbm.at[layer], both.at[layer, inner, inner], sems.at[2 * layer]
+            ),
+            pltpu.make_async_copy(
+                weight_hbm.at[layer], weight_ref.at[layer], sems.at[2 * layer + 1]
+            ),
+        ]
+    fetches[1].append(pltpu.make_async_copy(grad_hbm, grad_ref, sems.at[4]))
+    for layer in (1, 0):
+        for fetch in fetches[layer]:
+            fetch.start()
     slopes[...] = jnp.zeros_like(slopes)
+    edge = jnp.zeros((extent + 2, boxes, channels), jnp.bfloat16)
     for layer in (1, 0):
-        padded[1 : extent + 1, 1 : extent + 1] = saved_ref[layer]
-
-        def forward(i, sums, layer=layer):
+        for end in (0, extent + 1):
+            both[layer, end] = edge
+            both[layer, 1 : extent + 1, end] = edge[:extent]
+    for layer in (1, 0):
+        padded = both.at[layer]
+        for fetch in fetches[layer]:
+            fetch.wait()
+
+        def forward(i, sums, layer=layer, padded=padded):
             pieces = [
                 padded[i + a, b : b + extent].reshape(rows, channels)
                 for a in range(3)
@@ -58,7 +90,9 @@
                 slope.astype(jnp.float32).reshape(rows // 8, 8, channels), axis=0
             )
 
-        sums = lax.fori_loop(0, extent, forward, jnp.zeros((8, channels), jnp.float32))
+        sums = jnp.zeros((8, channels), jnp.float32)
+        for i in range(extent):
+            sums = forward(i, sums)
         biases_ref[layer : layer + 1, :] = jnp.sum(sums, axis=0, keepdims=True)
 
         def backward(i, carry, layer=layer):
@@ -75,12 +109,13 @@
             if layer == 1:
                 flow[i] = total.astype(jnp.bfloat16).reshape(extent, boxes, channels)
             else:
-                place = pl.ds(pl.multiple_of(i * rows, 8), rows)
+                place = pl.ds(i * rows, rows)
                 crops_ref[0, place, :] = total[:, : channels // 2]
                 crops_ref[1, place, :] = total[:, channels // 2 :]
             return carry
 
-        lax.fori_loop(0, extent, backward, 0)
+        for i in range(extent):
+            backward(i, 0)
 
 
 def conv_chain(grad_t, saved_t, weight, bias):
@@ -95,39 +130,57 @@
             jax.ShapeDtypeStruct((2, extent * extent * boxes, channels // 2), jnp.float32),
             jax.ShapeDtypeStruct((layers, channels), jnp.float32),
         ),
-        in_specs=[pl.BlockSpec(memory_space=VMEM)] * 4,
+        in_specs=[pl.BlockSpec(memory_space=pl.ANY)] * 3 + [pl.BlockSpec(memory_space=VMEM)],
         out_specs=(pl.BlockSpec(memory_space=VMEM),) * 3,
         scratch_shapes=[
-            pltpu.VMEM(padded, jnp.bfloat16),
+            pltpu.VMEM((layers,) + padded, jnp.bfloat16),
             pltpu.VMEM(padded, jnp.bfloat16),
             pltpu.VMEM((extent, extent, boxes, channels), jnp.bfloat16),
+            pltpu.VMEM(grad_t.shape, jnp.bfloat16),
+            pltpu.VMEM(weight.shape, jnp.bfloat16),
+            pltpu.SemaphoreType.DMA((5,)),
         ],
-        compiler_params=params(40),
+        compiler_params=params(56),
         cost_estimate=pl.CostEstimate(flops=15000000000, bytes_accessed=5000000, transcendentals=0),
     )(grad_t, saved_t, weight, bias)
 
 
-def pack_kernel(box_ref, crops_ref, tail_ref, sums_ref, out_ref, staged):
+def pack_kernel(box_ref, crops_ref, tail_ref, sums_ref, out_ref, first, second, staged):
     count = out_ref.shape[0]
-    boxes = staged.shape[0]
+    boxes = first.shape[0]
     bins = crops_ref.shape[1] // boxes
     owners = box_ref.shape[0] // 2
     step = pl.program_id(0)
 
     @pl.when(step == 0)
     def _():
+        staged[...] = jnp.zeros_like(staged)
         for box in range(boxes):
             for half in range(2):
-                staged[box, half * bins : (half + 1) * bins, :] = crops_ref[
-                    half, pl.ds(box, bins, stride=boxes), :
-                ]
-            staged[box, 2 * bins :, :] = tail_ref[...]
+                rows = crops_ref[half, pl.ds(box, bins, stride=boxes), :]
+                staged[0, box, half * bins : (half + 1) * bins, :] = rows
+                staged[1, box, half * bins + 2 : (half + 1) * bins + 2, :] = rows
+            staged[1, box, 2 * bins + 2 : 2 * bins + 6, :] = tail_ref[...]
+            first[box] = staged[0, box].astype(jnp.bfloat16)
+            second[box] = staged[1, box].astype(jnp.bfloat16)
+
+    def both(left, right):
+        return (left.astype(jnp.float32) + right.astype(jnp.float32)).astype(jnp.bfloat16)
 
     def place(index, carry):
         owner = step * count + index
+        one, two = first[box_ref[owner]], second[box_ref[owners + owner]]
+        sums = sums_ref[index]
         out_ref[index] = jnp.concatenate(
-            [staged[box_ref[owner]], staged[box_ref[owners + owner]], sums_ref[index]], axis=0
-        ).astype(jnp.bfloat16)
+            [
+                one[:96],
+                both(one[96:112], two[:16]),
+                two[16:96],
+                both(two[96:112], sums[:16]),
+                sums[16:48],
+            ],
+            axis=0,
+        )
         return carry
 
     lax.fori_loop(0, count, place, 0, unroll=4)
@@ -137,7 +190,8 @@
     owners = sums.shape[0]
     steps = 8
     half = crops.shape[2]
-    rows = 2 * SLOT_ROWS + SUM_ROWS
+    rows = 200 + SUM_ROWS
+    sums = jnp.pad(sums.astype(jnp.bfloat16), ((0, 0), (8, 0), (0, 0)))
     return pl.pallas_call(
         pack_kernel,
         name="pack",
@@ -148,10 +202,14 @@
             in_specs=[
                 pl.BlockSpec(crops.shape, lambda g, ids: (0, 0, 0)),
                 pl.BlockSpec(tail.shape, lambda g, ids: (0, 0)),
-                pl.BlockSpec((owners // steps, SUM_ROWS, half), lambda g, ids: (g, 0, 0)),
+                pl.BlockSpec((owners // steps, 8 + SUM_ROWS, half), lambda g, ids: (g, 0, 0)),
             ],
             out_specs=pl.BlockSpec((owners // steps, rows, half), lambda g, ids: (g, 0, 0)),
-            scratch_shapes=[pltpu.VMEM((boxes, SLOT_ROWS, half), jnp.float32)],
+            scratch_shapes=[
+                pltpu.VMEM((boxes, 112, half), jnp.bfloat16),
+                pltpu.VMEM((boxes, 112, half), jnp.bfloat16),
+                pltpu.VMEM((2, boxes, 112, half), jnp.float32),
+            ],
         ),
         compiler_params=params(56),
         cost_estimate=pl.CostEstimate(flops=1_000_000, bytes_accessed=9_000_000, transcendentals=0),
@@ -161,23 +219,24 @@
 def weight_kernel(slope_ref, saved_ref, out_ref, padded):
     extent, boxes, channels = saved_ref.shape[1], saved_ref.shape[3], saved_ref.shape[4]
     bins = extent * extent * boxes
-    offset = pl.program_id(1)
-
-    @pl.when(offset == 0)
+    step = pl.program_id(1)
+
+    @pl.when(step == 0)
     def _():
         padded[...] = jnp.zeros_like(padded)
         padded[1 : extent + 1, 1 : extent + 1] = saved_ref[0]
 
-    a, b = offset // 3, offset % 3
-    piece = padded[pl.ds(a, extent), pl.ds(b, extent)].reshape(bins, channels)
-    term = lax.dot_general(
-        piece,
-        slope_ref[0].reshape(bins, channels),
-        (((0,), (0,)), ((), ())),
-        preferred_element_type=jnp.float32,
-    )
-    out_ref[0, 0, 0] = term[:, : channels // 2].astype(jnp.bfloat16)
-    out_ref[0, 1, 0] = term[:, channels // 2 :].astype(jnp.bfloat16)
+    for k in range(9):
+        a, b = k // 3, k % 3
+        piece = padded[pl.ds(a, extent), pl.ds(b, extent)].reshape(bins, channels)
+        term = lax.dot_general(
+            piece,
+            slope_ref[0].reshape(bins, channels),
+            (((0,), (0,)), ((), ())),
+            preferred_element_type=jnp.float32,
+        )
+        out_ref[0, 0, k] = term[:, : channels // 2].astype(jnp.bfloat16)
+        out_ref[0, 1, k] = term[:, channels // 2 :].astype(jnp.bfloat16)
 
 
 def weight_terms(slope, saved_t):
@@ -187,9 +246,9 @@
         weight_kernel,
         name="weight_terms",
         out_shape=jax.ShapeDtypeStruct((layers, 2, 9, channels, channels // 2), jnp.bfloat16),
-        grid=(layers, 9),
+        grid=(layers, 1),
         in_specs=[pl.BlockSpec(block, lambda l, o: (l, 0, 0, 0, 0))] * 2,
-        out_specs=pl.BlockSpec((1, 2, 1, channels, channels // 2), lambda l, o: (l, 0, o, 0, 0)),
+        out_specs=pl.BlockSpec((1, 2, 9, channels, channels // 2), lambda l, o: (l, 0, o, 0, 0)),
         scratch_shapes=[pltpu.VMEM((extent + 2, extent + 2, boxes, channels), jnp.bfloat16)],
         compiler_params=params(24),
         cost_estimate=pl.CostEstimate(flops=7400000000, bytes_accessed=5000000, transcendentals=0),
@@ -324,15 +383,21 @@
 
 
 def tile_kernel(
-    base_ref, place_ref, groups_ref, got_ref, columns_ref, out_ref, biases_ref, crops
+    base_ref, place_ref, groups_ref, got_ref, columns_hbm, out_ref, biases_ref, crops, columns_ref, sem
 ):
     step = pl.program_id(0)
     owners, half = got_ref.shape[0], got_ref.shape[2]
     bins = 49
-    block = 2 * owners * SLOT_ROWS
-    wide = got_ref[...].astype(jnp.float32)[:, : 2 * SLOT_ROWS, :]
+    block = owners * 200
+    fetch = pltpu.make_async_copy(columns_hbm, columns_ref, sem)
+
+    @pl.when(step == 0)
+    def _():
+        fetch.start()
+
+    wide = got_ref[...].astype(jnp.float32)[:, :200, :]
     crops[pl.ds(pl.multiple_of(step * block, 8), block), :] = wide.reshape(block, half)
-    spare = jnp.sum(wide[:, SLOT_ROWS - 8 : SLOT_ROWS, :], axis=0)
+    spare = jnp.sum(wide[:, 192:, :], axis=0)
 
     @pl.when(step == 0)
     def _():
@@ -345,6 +410,7 @@
     @pl.when(step == pl.num_programs(0) - 1)
     def _():
         out_ref[...] = jnp.zeros_like(out_ref)
+        fetch.wait()
 
         def group(t):
             left, right = [], []
@@ -381,13 +447,17 @@
             grid=(steps,),
             in_specs=[
                 pl.BlockSpec((owners // steps, rows, half), lambda g, *refs: (g, 0, 0)),
-                pl.BlockSpec(columns.shape, lambda g, *refs: (0, 0, 0)),
+                pl.BlockSpec(memory_space=pl.ANY),
             ],
             out_specs=(
                 pl.BlockSpec((TILE, TILE, channels), lambda g, *refs: (0, 0, 0)),
                 pl.BlockSpec((8, half), lambda g, *refs: (0, 0)),
             ),
-            scratch_shapes=[pltpu.VMEM((2 * owners * SLOT_ROWS, half), jnp.float32)],
+            scratch_shapes=[
+                pltpu.VMEM((owners * 200, half), jnp.float32),
+                pltpu.VMEM(columns.shape, jnp.bfloat16),
+                pltpu.SemaphoreType.DMA(()),
+            ],
         ),
         compiler_params=params(48),
         cost_estimate=pl.CostEstimate(
@@ -488,7 +558,7 @@
     entry = jnp.where(inside, entry, 14)
     owner, code = entry // 16, entry % 16
     line = jnp.minimum(code // 2, extent - 1)
-    base = owner * SLOT_ROWS + extent * line
+    base = owner // 2 * 200 + owner % 2 * 98 + extent * line
     chosen = (owner[:, None] == jnp.arange(count)).astype(jnp.bfloat16)
     values = jnp.dot(chosen, slots[:, 8:].astype(jnp.bfloat16), preferred_element_type=jnp.float32)
     which = jnp.arange(2 * wide, dtype=jnp.int32)
@@ -534,7 +604,7 @@
     terms = weight_terms(slope, saved_t)
     terms, slots = lax.optimization_barrier((terms, slots))
     sums = sum_chip(terms.reshape(layers, -1, channels // 2), devices)
-    tail = jnp.pad(biases.reshape(layers * 2, channels // 2), ((0, 2), (0, 0)))
+    tail = biases.reshape(layers * 2, channels // 2)
     send = pack(box_of_slot.reshape(-1), crops, tail, sums, boxes)
     send, slots = lax.optimization_barrier((send, slots))
     got = lax.all_to_all(send, AXES, split_axis=0, concat_axis=0, tiled=True)
@@ -542,7 +612,7 @@
     base, place, groups, columns = arrange(slots.reshape(2 * devices, -1).astype(jnp.float32), extent)
     got, columns = lax.optimization_barrier((got, columns))
     cols = lax.axis_size("col")
-    arrived = got[:, 2 * SLOT_ROWS :, :].reshape(-1, layers, cols, SUM_ROWS, channels // 2)
+    arrived = got[:, 200:, :].reshape(-1, layers, cols, SUM_ROWS, channels // 2)
     part = jnp.sum(arrived.astype(jnp.float32), axis=(0, 2)).astype(jnp.bfloat16)
     part = ring(ring(part, "col", hop_z), "col", hop_y)
     part, got = lax.optimization_barrier((part, got))
@@ -551,7 +621,7 @@
     own, feature_grad = lax.optimization_barrier((own, feature_grad))
     other = lax.ppermute(own, "row", hop_core())
     weight_grad = widen(own, other, 9 * channels, grad_scale)
-    bias_grad = (spare[2 : 2 + 2 * layers] * grad_scale).reshape(layers, channels)
+    bias_grad = (spare[4 : 4 + 2 * layers] * grad_scale).reshape(layers, channels)
     return (weight_grad, bias_grad, feature_grad)
 
 

time: 223 us -> 211 us (0.946)
  Pallas kernels: 77.3 us -> 70.8 us
  local copies, waits for them, and re-layouts: 27 us -> 22.2 us
    pallas_call x1, Pallas kernels: 8.99 us -> 4.75 us  [weight_terms(): pl.pallas_call(weight_kernel, name='weight_terms', out_shape=jax.ShapeDty...]
    unnamed x30 -> x26, local copies, waits for them, and re-layouts: 12.2 us -> 8.76 us
    all_to_all x1, waiting for transfers between devices: 53.1 us -> 50.4 us  [shards(): got = lax.all_to_all(send, AXES, split_axis=0, concat_axis=0, tiled=True)]
    pallas_call x1, Pallas kernels: 15.4 us -> 12.7 us  [conv_chain(): pl.pallas_call(chain_kernel, name='conv_chain', out_shape=(jax.ShapeDtype...]
  transfers between devices with their start and end apart: 13 -> 13, of which waited for: 7 -> 8; matrix products, arithmetic and copies ran while one was open for 9% -> 10% of each run, Pallas kernels for 29% -> 27%
where the time goes in v2:
time: 211 us; the launch traced here: 210 us
  Pallas kernels  70.8 us (34%)
  waiting for transfers between devices  59.9 us (28%)
  starting transfers between devices  43.5 us (21%)
  local copies, waits for them, and re-layouts  22.2 us (11%)
  other arithmetic  11.1 us (5%)
    all_to_all x1, waiting for transfers between devices, shards(): got = lax.all_to_all(send, AXES, split_axis=0, concat_axis=0, tiled=True)  50.4 us
    pallas_call x1, Pallas kernels, order_entries(): pl.pallas_call(order_kernel, name='order_entries', out_shape=jax.ShapeDty...  26.1 us
    pallas_call x1, Pallas kernels, tile_sum(): pl.pallas_call(tile_kernel, name='tile_sum', out_shape=(jax.ShapeDtypeStr...  13.5 us
    ppermute x9, starting transfers between devices, ring(): lax.ppermute(part, name, hop(k))  13.1 us
    pallas_call x1, Pallas kernels, conv_chain(): pl.pallas_call(chain_kernel, name='conv_chain', out_shape=(jax.ShapeDtype...  12.7 us
    all_to_all x1, starting transfers between devices, shards(): lax.all_to_all(slots.reshape(devices, 1, -1), AXES, split_axis=0, concat_...  11.5 us
    pallas_call x1, Pallas kernels, pack(): pl.pallas_call(pack_kernel, name='pack', out_shape=jax.ShapeDtypeStruct((...  10.2 us
    all_to_all x1, starting transfers between devices, shards(): got = lax.all_to_all(send, AXES, split_axis=0, concat_axis=0, tiled=True)  9.47 us
  transfers between devices with their start and end apart: 13, of which 8 were waited for; matrix products, arithmetic and copies ran while one was open for 10% of the time, Pallas kernels for 27%

profile of v2, /device:TPU:1, one launch (start us, length us, event | category | flops | bytes accessed | tf_op | source)
XLA Modules:
  0.0 210.3 jit_solution(6085978450516936103)
XLA Ops:
  5.9 11.5 %all-to-all-start = ((bf16[128,1,128]{2,1,0:T(2,128)(2,1)}), bf16[128,1,128]{2,1,0:T(2,128)(2,1)S(1)}, u32[]{:S(2)}, u32[]{:S(2)}) async-start(bf16[128,1,128]{2,1,0:T(2,128)(2,1)} %copy.19), calls=%async_computation | async-start | bytes 131072 | tf_op jit(solution)/shard_map/all_to_all | solution.py:597
  17.4 12.7 %conv_chain.1 = (bf16[2,7,7,32,256]{4,3,2,1,0:T(8,128)(2,1)}, f32[2,1568,128]{2,1,0:T(8,128)}, f32[2,256]{1,0:T(2,128)}) custom-call(bf16[7,7,32,256]{3,2,1,0:T(8,128)(2,1)} %bitcast.61, bf16[2,7,7,32,256]{4,3,2,1,0:T(8,128)(2,1)} %bitcast.45, bf16[2,9,256,256]{3,2,1,0:T(8,128)(2,1)} %weight_hbm.1, f32[2,256]{1,0:T(2,128)} %bias_ref.1), custom_call_target="tpu_custom_call" | custom-call | flops 15000000512 | bytes 5000000 | tf_op jit(solution)/shard_map/conv_chain/pallas_call | solution.py:125
  31.5 4.8 %weight_terms.1 = bf16[2,2,9,256,128]{4,3,2,1,0:T(8,128)(2,1)S(1)} custom-call(bf16[2,7,7,32,256]{4,3,2,1,0:T(8,128)(2,1)S(1)} %copy-done.8, bf16[2,7,7,32,256]{4,3,2,1,0:T(8,128)(2,1)S(1)} %bitcast.46), custom_call_target="tpu_custom_call" | custom-call | flops 7400000000 | bytes 5000000 | tf_op jit(solution)/shard_map/weight_terms/pallas_call | solution.py:245
  38.9 2.0 collective-permute-done
  43.8 10.2 %pack.1 = bf16[128,240,128]{2,1,0:T(8,128)(2,1)} custom-call(s32[256]{0:T(256)} %bitcast.44, f32[2,1568,128]{2,1,0:T(8,128)} %get-tuple-element.21.crops_ref, f32[4,128]{1,0:T(4,128)} %reshape.137.tail_ref, bf16[128,48,128]{2,1,0:T(8,128)(2,1)} %pad.10.sums_ref), custom_call_target="tpu_custom_call" | custom-call | flops 1000000 | bytes 9000000 | tf_op jit(solution)/shard_map/pack/pallas_call | solution.py:195
  54.1 9.5 %all-to-all-start.1 = ((bf16[128,240,128]{2,1,0:T(8,128)(2,1)}), bf16[128,240,128]{2,1,0:T(8,128)(2,1)}, u32[]{:S(2)}, u32[]{:S(2)}) async-start(bf16[128,240,128]{2,1,0:T(8,128)(2,1)} %pack.1), calls=%async_computation.1 | async-start | bytes 15728640 | tf_op jit(solution)/shard_map/all_to_all | solution.py:610
  66.5 26.1 %order_entries.1 = s32[5632]{0:T(1024)} custom-call(s32[1792]{0:T(1024)} %copy-done.11, s32[64]{0:T(128)} %get-tuple-element.47.start_ref, s32[64]{0:T(128)} %get-tuple-element.46.end_ref), custom_call_target="tpu_custom_call" | custom-call | flops 10000000 | bytes 30000000 | tf_op jit(solution)/shard_map/order_entries/pallas_call | solution.py:374
  96.4 1.8 broadcast_in_dim.81
  99.0 1.8 broadcast_in_dim.84
  101.6 1.8 eq.117
  103.4 5.8 %add_convert_fusion.columns_hbm = bf16[176,64,256]{2,1,0:T(8,128)(2,1)} fusion(f32[176,256]{1,0:T(8,128)S(1)} %broadcast_in_dim.84, f32[176,256]{1,0:T(8,128)S(1)} %broadcast_add_fusion, f32[176,256]{1,0:T(8,128)S(1)} %broadcast_in_dim.81, f32[176,256]{1,0:T(8,128)S(1)} %eq.117), kind=kLoop, calls=%fused_computation | loop fusion | flops 17301504 | bytes 6488064 | tf_op jit(solution)/shard_map/convert_element_type | solution.py:578
  109.2 50.4 %all-to-all-done.1.got_ref = bf16[128,240,128]{2,1,0:T(8,128)(2,1)} async-done(((bf16[128,240,128]{2,1,0:T(8,128)(2,1)}), bf16[128,240,128]{2,1,0:T(8,128)(2,1)}, u32[]{:S(2)}, u32[]{:S(2)}) %all-to-all-start.1) | async-done | bytes 7864352 | tf_op jit(solution)/shard_map/all_to_all | solution.py:610
  161.3 2.2 %collective-permute-start.3 = (bf16[2,40,128]{2,1,0:T(8,128)(2,1)S(1)}, bf16[2,40,128]{2,1,0:T(8,128)(2,1)S(1)}, u32[]{:S(2)}, u32[]{:S(2)}) collective-permute-start(bf16[2,40,128]{2,1,0:T(8,128)(2,1)S(1)} %reduce_sum.51), channel_id=1, source_target_pairs={{0,4},{1,5},{2,6},{3,7},{4,8},{5,9},{6,10},{7,11},{8,12},{9,13},{1... | collective-permute-start | bytes 61448 | tf_op jit(solution)/shard_map/ppermute | solution.py:287
  163.5 1.7 collective-permute-start.2
  167.8 1.7 collective-permute-start.5
  171.0 1.7 collective-permute-done.5
  173.2 1.7 collective-permute-done.6
  175.0 2.9 %collective-permute-start.8 = (bf16[4,4,2,40,128]{4,3,2,1,0:T(8,128)(2,1)S(1)}, bf16[4,4,2,40,128]{4,3,2,1,0:T(8,128)(2,1)S(1)}, u32[]{:S(2)}, u32[]{:S(2)}) collective-permute-start(bf16[4,4,2,40,128]{4,3,2,1,0:T(8,128)(2,1)S(1)} %pad_maximum_fusion.1), channel_id=1, source_target_pairs={{0,64},{16,80},{32,96},{48,112},{64,0},{80,16},{96,32},{112,48},{1... | collective-permute-start | bytes 983048 | tf_op jit(solution)/shard_map/ppermute | solution.py:287
  177.9 2.0 collective-permute-start.7
  180.0 2.6 %copy-done = bf16[176,64,256]{2,1,0:T(8,128)(2,1)S(1)} copy-done((bf16[176,64,256]{2,1,0:T(8,128)(2,1)S(1)}, bf16[176,64,256]{2,1,0:T(8,128)(2,1)}, u32[]{:S(2)}) %copy-start) | copy-done | bytes 5767192
  182.6 13.5 %tile_sum.1 = (f32[64,64,256]{2,1,0:T(8,128)}, f32[8,128]{1,0:T(8,128)S(1)}) custom-call(s32[5632]{0:T(1024)S(1)} %get-tuple-element.37.base_ref, s32[176]{0:T(256)S(1)} %convert_reduce_fusion.place_ref, s32[1]{0:T(128)} %slice.37.groups_ref, bf16[128,240,128]{2,1,0:T(8,128)(2,1)} %all-to-all-done.1.got_ref, bf16[176,64,256]{2,1,0:T(8,128)(2,1)S(1)} %copy-done), custom_call_target="tpu_custom_call" | custom-call | flops 1476395008 | bytes 17000000 | tf_op jit(solution)/shard_map/tile_sum/pallas_call | solution.py:438
  196.3 8.1 %collective-permute-start.10 = (bf16[4,4,4,2,40,128]{5,4,3,2,1,0:T(8,128)(2,1)S(1)}, bf16[4,4,4,2,40,128]{5,4,3,2,1,0:T(8,128)(2,1)S(1)}, u32[]{:S(2)}, u32[]{:S(2)}) collective-permute-start(bf16[4,4,4,2,40,128]{5,4,3,2,1,0:T(8,128)(2,1)S(1)} %pad_maximum_fusion.own_ref), channel_id=1, source_target_pairs={{0,16},{16,0},{32,48},{48,32},{64,80},{80,64},{96,112},{112,96},{1... | collective-permute-start | bytes 3932168 | tf_op jit(solution)/shard_map/ppermute | solution.py:622
  205.1 2.0 collective-permute-done.10.other_ref
  207.1 3.1 %widen.1 = f32[2,2304,256]{2,1,0:T(8,128)} custom-call(s32[4]{0:T(128)S(1)} %pad_add_fusion.place_ref, bf16[4,4,4,2,40,128]{5,4,3,2,1,0:T(8,128)(2,1)S(1)} %pad_maximum_fusion.own_ref, bf16[4,4,4,2,40,128]{5,4,3,2,1,0:T(8,128)(2,1)S(1)} %collective-permute-done.10.other_ref), custom_call_target="tpu_custom_call" | custom-call | flops 3000000 | bytes 10000000 | tf_op jit(solution)/shard_map/widen/pallas_call | solution.py:323
  (76 shorter events, 27.1 us)
Async XLA Ops:
  0.6 0.7 copy-start.1
  1.3 0.7 copy-start.2
  2.1 0.7 copy-start.3
  2.8 0.7 copy-start.4
  3.5 0.7 copy-start.5
  5.9 30.4 %all-to-all-start = ((bf16[128,1,128]{2,1,0:T(2,128)(2,1)}), bf16[128,1,128]{2,1,0:T(2,128)(2,1)S(1)}, u32[]{:S(2)}, u32[]{:S(2)}) async-start(bf16[128,1,128]{2,1,0:T(2,128)(2,1)} %copy.19), calls=%async_computation | async-start | bytes 131072 | tf_op jit(solution)/shard_map/all_to_all | solution.py:597
  17.4 12.7 %copy-start.7 = (bf16[2,32,7,7,256]{4,1,3,2,0:T(8,128)(2,1)S(1)}, bf16[2,32,7,7,256]{4,1,3,2,0:T(8,128)(2,1)}, u32[]{:S(2)}) copy-start(bf16[2,32,7,7,256]{4,1,3,2,0:T(8,128)(2,1)} %param.10) | copy-start | bytes 4816900
  30.1 1.4 copy-start.8
  36.2 2.0 copy-start.12
  37.0 3.9 %collective-permute-start = (bf16[4608,128]{1,0:T(8,128)(2,1)S(1)}, bf16[4608,128]{1,0:T(8,128)(2,1)}, u32[]{:S(2)}, u32[]{:S(2)}) collective-permute-start(bf16[4608,128]{1,0:T(8,128)(2,1)S(1)} %dynamic-slice_bitcast_fusion), channel_id=1, source_target_pairs={{0,16},{16,0},{32,48},{48,32},{64,80},{80,64},{96,112},{112,96},{1... | collective-permute-start | bytes 3538952 | tf_op jit(solution)/shard_map/ppermute | solution.py:280
  54.1 9.5 %copy-start.10 = (bf16[128,1,128]{2,1,0:T(2,128)(2,1)S(1)}, bf16[128,1,128]{2,1,0:T(2,128)(2,1)}, u32[]{:S(2)}) copy-start(bf16[128,1,128]{2,1,0:T(2,128)(2,1)} %copy-done.9) | copy-start | bytes 98308
  54.1 105.5 %all-to-all-start.1 = ((bf16[128,240,128]{2,1,0:T(8,128)(2,1)}), bf16[128,240,128]{2,1,0:T(8,128)(2,1)}, u32[]{:S(2)}, u32[]{:S(2)}) async-start(bf16[128,240,128]{2,1,0:T(8,128)(2,1)} %pack.1), calls=%async_computation.1 | async-start | bytes 15728640 | tf_op jit(solution)/shard_map/all_to_all | solution.py:610
  64.4 2.1 copy-start.11
  161.3 4.9 %collective-permute-start.3 = (bf16[2,40,128]{2,1,0:T(8,128)(2,1)S(1)}, bf16[2,40,128]{2,1,0:T(8,128)(2,1)S(1)}, u32[]{:S(2)}, u32[]{:S(2)}) collective-permute-start(bf16[2,40,128]{2,1,0:T(8,128)(2,1)S(1)} %reduce_sum.51), channel_id=1, source_target_pairs={{0,4},{1,5},{2,6},{3,7},{4,8},{5,9},{6,10},{7,11},{8,12},{9,13},{1... | collective-permute-start | bytes 61448 | tf_op jit(solution)/shard_map/ppermute | solution.py:287
  163.5 4.1 %collective-permute-start.2 = (bf16[2,40,128]{2,1,0:T(8,128)(2,1)S(1)}, bf16[2,40,128]{2,1,0:T(8,128)(2,1)S(1)}, u32[]{:S(2)}, u32[]{:S(2)}) collective-permute-start(bf16[2,40,128]{2,1,0:T(8,128)(2,1)S(1)} %reduce_sum.51), channel_id=1, source_target_pairs={{0,8},{1,9},{2,10},{3,11},{4,12},{5,13},{6,14},{7,15},{8,0},{9,1},... | collective-permute-start | bytes 61448 | tf_op jit(solution)/shard_map/ppermute | solution.py:287
  165.2 2.6 %collective-permute-start.1 = (bf16[2,40,128]{2,1,0:T(8,128)(2,1)S(1)}, bf16[2,40,128]{2,1,0:T(8,128)(2,1)S(1)}, u32[]{:S(2)}, u32[]{:S(2)}) collective-permute-start(bf16[2,40,128]{2,1,0:T(8,128)(2,1)S(1)} %reduce_sum.51), channel_id=1, source_target_pairs={{0,12},{1,13},{2,14},{3,15},{4,0},{5,1},{6,2},{7,3},{8,4},{9,5},{1... | collective-permute-start | bytes 61448 | tf_op jit(solution)/shard_map/ppermute | solution.py:287
  167.8 4.9 %collective-permute-start.5 = (bf16[4,2,40,128]{3,2,1,0:T(8,128)(2,1)S(1)}, bf16[4,2,40,128]{3,2,1,0:T(8,128)(2,1)S(1)}, u32[]{:S(2)}, u32[]{:S(2)}) collective-permute-start(bf16[4,2,40,128]{3,2,1,0:T(8,128)(2,1)S(1)} %get-tuple-element.44), channel_id=1, source_target_pairs={{0,2},{1,3},{2,0},{3,1},{4,6},{5,7},{6,4},{7,5},{8,10},{9,11},{10,... | collective-permute-start | bytes 245768 | tf_op jit(solution)/shard_map/ppermute | solution.py:287
  169.6 3.6 %collective-permute-start.4 = (bf16[4,2,40,128]{3,2,1,0:T(8,128)(2,1)S(1)}, bf16[4,2,40,128]{3,2,1,0:T(8,128)(2,1)S(1)}, u32[]{:S(2)}, u32[]{:S(2)}) collective-permute-start(bf16[4,2,40,128]{3,2,1,0:T(8,128)(2,1)S(1)} %get-tuple-element.44), channel_id=1, source_target_pairs={{0,3},{1,0},{2,1},{3,2},{4,7},{5,4},{6,5},{7,6},{8,11},{9,8},{10,9... | collective-permute-start | bytes 245768 | tf_op jit(solution)/shard_map/ppermute | solution.py:287
  170.4 4.5 %collective-permute-start.6 = (bf16[4,2,40,128]{3,2,1,0:T(8,128)(2,1)S(1)}, bf16[4,2,40,128]{3,2,1,0:T(8,128)(2,1)S(1)}, u32[]{:S(2)}, u32[]{:S(2)}) collective-permute-start(bf16[4,2,40,128]{3,2,1,0:T(8,128)(2,1)S(1)} %get-tuple-element.44), channel_id=1, source_target_pairs={{0,1},{1,2},{2,3},{3,0},{4,5},{5,6},{6,7},{7,4},{8,9},{9,10},{10,1... | collective-permute-start | bytes 245768 | tf_op jit(solution)/shard_map/ppermute | solution.py:287
  175.0 21.2 %collective-permute-start.9 = (bf16[4,4,2,40,128]{4,3,2,1,0:T(8,128)(2,1)S(1)}, bf16[4,4,2,40,128]{4,3,2,1,0:T(8,128)(2,1)S(1)}, u32[]{:S(2)}, u32[]{:S(2)}) collective-permute-start(bf16[4,4,2,40,128]{4,3,2,1,0:T(8,128)(2,1)S(1)} %pad_maximum_fusion.1), channel_id=1, source_target_pairs={{0,32},{16,48},{32,64},{48,80},{64,96},{80,112},{96,0},{112,16},{1... | collective-permute-start | bytes 983048 | tf_op jit(solution)/shard_map/ppermute | solution.py:287
  175.0 21.1 %collective-permute-start.8 = (bf16[4,4,2,40,128]{4,3,2,1,0:T(8,128)(2,1)S(1)}, bf16[4,4,2,40,128]{4,3,2,1,0:T(8,128)(2,1)S(1)}, u32[]{:S(2)}, u32[]{:S(2)}) collective-permute-start(bf16[4,4,2,40,128]{4,3,2,1,0:T(8,128)(2,1)S(1)} %pad_maximum_fusion.1), channel_id=1, source_target_pairs={{0,64},{16,80},{32,96},{48,112},{64,0},{80,16},{96,32},{112,48},{1... | collective-permute-start | bytes 983048 | tf_op jit(solution)/shard_map/ppermute | solution.py:287
  177.9 18.2 %collective-permute-start.7 = (bf16[4,4,2,40,128]{4,3,2,1,0:T(8,128)(2,1)S(1)}, bf16[4,4,2,40,128]{4,3,2,1,0:T(8,128)(2,1)S(1)}, u32[]{:S(2)}, u32[]{:S(2)}) collective-permute-start(bf16[4,4,2,40,128]{4,3,2,1,0:T(8,128)(2,1)S(1)} %pad_maximum_fusion.1), channel_id=1, source_target_pairs={{0,96},{16,112},{32,0},{48,16},{64,32},{80,48},{96,64},{112,80},{1... | collective-permute-start | bytes 983048 | tf_op jit(solution)/shard_map/ppermute | solution.py:287
  180.0 2.6 %copy-start = (bf16[176,64,256]{2,1,0:T(8,128)(2,1)S(1)}, bf16[176,64,256]{2,1,0:T(8,128)(2,1)}, u32[]{:S(2)}) copy-start(bf16[176,64,256]{2,1,0:T(8,128)(2,1)} %add_convert_fusion.columns_hbm) | copy-start | bytes 17301508
  196.3 10.8 %collective-permute-start.10 = (bf16[4,4,4,2,40,128]{5,4,3,2,1,0:T(8,128)(2,1)S(1)}, bf16[4,4,4,2,40,128]{5,4,3,2,1,0:T(8,128)(2,1)S(1)}, u32[]{:S(2)}, u32[]{:S(2)}) collective-permute-start(bf16[4,4,4,2,40,128]{5,4,3,2,1,0:T(8,128)(2,1)S(1)} %pad_maximum_fusion.own_ref), channel_id=1, source_target_pairs={{0,16},{16,0},{32,48},{48,32},{64,80},{80,64},{96,112},{112,96},{1... | collective-permute-start | bytes 3932168 | tf_op jit(solution)/shard_map/ppermute | solution.py:622
  (2 other events, 1.2 us)

commit v3 on v2

--- a/solution.py
+++ b/solution.py
@@ -31,7 +31,7 @@
     saved_hbm,
     weight_hbm,
     bias_ref,
-    slope_ref,
+    terms_ref,
     crops_ref,
     biases_ref,
     both,
@@ -85,7 +85,6 @@
             upper = upper.reshape(rows, channels).astype(jnp.float32)
             slope = (upper * gelu_slope(pre)).astype(jnp.bfloat16)
             slopes[i + 1, 1 : extent + 1] = slope.reshape(extent, boxes, channels)
-            slope_ref[layer, i] = slope.reshape(extent, boxes, channels)
             return sums + jnp.sum(
                 slope.astype(jnp.float32).reshape(rows // 8, 8, channels), axis=0
             )
@@ -94,6 +93,24 @@
         for i in range(extent):
             sums = forward(i, sums)
         biases_ref[layer : layer + 1, :] = jnp.sum(sums, axis=0, keepdims=True)
+
+        whole = slopes[1 : extent + 1, 1 : extent + 1].reshape(extent * rows, channels)
+        for k in range(9):
+            piece = padded[pl.ds(k // 3, extent), pl.ds(k % 3, extent)]
+            term = lax.dot_general(
+                piece.reshape(extent * rows, channels),
+                whole,
+                (((0,), (0,)), ((), ())),
+                preferred_element_type=jnp.float32,
+            ).astype(jnp.bfloat16)
+            for half in range(2):
+                terms_ref[layer, (9 * half + k) * channels : (9 * half + k + 1) * channels, :] = (
+                    term[:, half * channels // 2 : (half + 1) * channels // 2]
+                )
+        last = 18 * channels
+        terms_ref[layer, last:, :] = jnp.zeros(
+            (terms_ref.shape[1] - last, channels // 2), jnp.bfloat16
+        )
 
         def backward(i, carry, layer=layer):
             total = jnp.zeros((rows, channels), jnp.float32)
@@ -118,7 +135,7 @@
             backward(i, 0)
 
 
-def conv_chain(grad_t, saved_t, weight, bias):
+def conv_chain(grad_t, saved_t, weight, bias, lines):
     extent, boxes, channels = grad_t.shape[0], grad_t.shape[2], grad_t.shape[3]
     layers = saved_t.shape[0]
     padded = (extent + 2, extent + 2, boxes, channels)
@@ -126,7 +143,7 @@
         chain_kernel,
         name="conv_chain",
         out_shape=(
-            jax.ShapeDtypeStruct((layers, extent, extent, boxes, channels), jnp.bfloat16),
+            jax.ShapeDtypeStruct((layers, lines, channels // 2), jnp.bfloat16),
             jax.ShapeDtypeStruct((2, extent * extent * boxes, channels // 2), jnp.float32),
             jax.ShapeDtypeStruct((layers, channels), jnp.float32),
         ),
@@ -141,118 +158,108 @@
             pltpu.SemaphoreType.DMA((5,)),
         ],
         compiler_params=params(56),
-        cost_estimate=pl.CostEstimate(flops=15000000000, bytes_accessed=5000000, transcendentals=0),
+        cost_estimate=pl.CostEstimate(flops=22000000000, bytes_accessed=9000000, transcendentals=0),
     )(grad_t, saved_t, weight, bias)
 
 
-def pack_kernel(box_ref, crops_ref, tail_ref, sums_ref, out_ref, first, second, staged):
-    count = out_ref.shape[0]
+def pack_kernel(
+    box_ref,
+    core_ref,
+    crops_ref,
+    tail_ref,
+    own_ref,
+    other_ref,
+    out_hbm,
+    first,
+    second,
+    staged,
+    sums,
+    out_ref,
+    sems,
+):
+    del core_ref
+    steps = sems.shape[0]
+    owners = out_ref.shape[0]
+    count = owners // steps
+    lines = count * SUM_ROWS
     boxes = first.shape[0]
     bins = crops_ref.shape[1] // boxes
-    owners = box_ref.shape[0] // 2
-    step = pl.program_id(0)
-
-    @pl.when(step == 0)
-    def _():
-        staged[...] = jnp.zeros_like(staged)
-        for box in range(boxes):
-            for half in range(2):
-                rows = crops_ref[half, pl.ds(box, bins, stride=boxes), :]
-                staged[0, box, half * bins : (half + 1) * bins, :] = rows
-                staged[1, box, half * bins + 2 : (half + 1) * bins + 2, :] = rows
-            staged[1, box, 2 * bins + 2 : 2 * bins + 6, :] = tail_ref[...]
-            first[box] = staged[0, box].astype(jnp.bfloat16)
-            second[box] = staged[1, box].astype(jnp.bfloat16)
+    staged[...] = jnp.zeros_like(staged)
+    for box in range(boxes):
+        for half in range(2):
+            rows = crops_ref[half, pl.ds(box, bins, stride=boxes), :]
+            staged[0, box, half * bins : (half + 1) * bins, :] = rows
+            staged[1, box, half * bins + 2 : (half + 1) * bins + 2, :] = rows
+        staged[1, box, 2 * bins + 2 : 2 * bins + 6, :] = tail_ref[...]
+        first[box] = staged[0, box].astype(jnp.bfloat16)
+        second[box] = staged[1, box].astype(jnp.bfloat16)
+    blank = jnp.zeros((8, sums.shape[1]), jnp.float32)
 
     def both(left, right):
         return (left.astype(jnp.float32) + right.astype(jnp.float32)).astype(jnp.bfloat16)
 
-    def place(index, carry):
-        owner = step * count + index
-        one, two = first[box_ref[owner]], second[box_ref[owners + owner]]
-        sums = sums_ref[index]
-        out_ref[index] = jnp.concatenate(
-            [
-                one[:96],
-                both(one[96:112], two[:16]),
-                two[16:96],
-                both(two[96:112], sums[:16]),
-                sums[16:48],
-            ],
-            axis=0,
-        )
-        return carry
-
-    lax.fori_loop(0, count, place, 0, unroll=4)
-
-
-def pack(box_of_slot, crops, tail, sums, boxes):
-    owners = sums.shape[0]
-    steps = 8
+    sends = []
+    for step in range(steps):
+        block = slice(step * lines, (step + 1) * lines)
+        sums[...] = own_ref[0, block, :].astype(jnp.float32) + other_ref[block, :].astype(jnp.float32)
+
+        def place(index, carry, step=step):
+            owner = step * count + index
+            one, two = first[box_ref[owner]], second[box_ref[owners + owner]]
+            chunk = sums[pl.ds(pl.multiple_of(index * SUM_ROWS, 8), SUM_ROWS), :]
+            chunk = jnp.concatenate([blank, chunk], axis=0).astype(jnp.bfloat16)
+            out_ref[owner] = jnp.concatenate(
+                [
+                    one[:96],
+                    both(one[96:112], two[:16]),
+                    two[16:96],
+                    both(two[96:112], chunk[:16]),
+                    chunk[16:],
+                ],
+                axis=0,
+            )
+            return carry
+
+        lax.fori_loop(0, count, place, 0, unroll=4)
+        part = pl.ds(step * count, count)
+        send = pltpu.make_async_copy(out_ref.at[part], out_hbm.at[part], sems.at[step])
+        send.start()
+        sends.append(send)
+    for send in sends:
+        send.wait()
+
+
+def pack(box_of_slot, core, crops, tail, own, other, boxes):
+    owners = box_of_slot.shape[0] // 2
+    steps = 16
     half = crops.shape[2]
     rows = 200 + SUM_ROWS
-    sums = jnp.pad(sums.astype(jnp.bfloat16), ((0, 0), (8, 0), (0, 0)))
     return pl.pallas_call(
         pack_kernel,
         name="pack",
         out_shape=jax.ShapeDtypeStruct((owners, rows, half), jnp.bfloat16),
         grid_spec=pltpu.PrefetchScalarGridSpec(
-            num_scalar_prefetch=1,
-            grid=(steps,),
+            num_scalar_prefetch=2,
+            grid=(1,),
             in_specs=[
-                pl.BlockSpec(crops.shape, lambda g, ids: (0, 0, 0)),
-                pl.BlockSpec(tail.shape, lambda g, ids: (0, 0)),
-                pl.BlockSpec((owners // steps, 8 + SUM_ROWS, half), lambda g, ids: (g, 0, 0)),
+                pl.BlockSpec(crops.shape, lambda g, ids, core: (0, 0, 0)),
+                pl.BlockSpec(tail.shape, lambda g, ids, core: (0, 0)),
+                pl.BlockSpec((1,) + other.shape, lambda g, ids, core: (core[0], 0, 0)),
+                pl.BlockSpec(other.shape, lambda g, ids, core: (0, 0)),
             ],
-            out_specs=pl.BlockSpec((owners // steps, rows, half), lambda g, ids: (g, 0, 0)),
+            out_specs=pl.BlockSpec(memory_space=pl.ANY),
             scratch_shapes=[
                 pltpu.VMEM((boxes, 112, half), jnp.bfloat16),
                 pltpu.VMEM((boxes, 112, half), jnp.bfloat16),
                 pltpu.VMEM((2, boxes, 112, half), jnp.float32),
+                pltpu.VMEM((owners // steps * SUM_ROWS, half), jnp.float32),
+                pltpu.VMEM((owners, rows, half), jnp.bfloat16),
+                pltpu.SemaphoreType.DMA((steps,)),
             ],
         ),
         compiler_params=params(56),
         cost_estimate=pl.CostEstimate(flops=1_000_000, bytes_accessed=9_000_000, transcendentals=0),
-    )(box_of_slot, crops, tail, sums)
-
-
-def weight_kernel(slope_ref, saved_ref, out_ref, padded):
-    extent, boxes, channels = saved_ref.shape[1], saved_ref.shape[3], saved_ref.shape[4]
-    bins = extent * extent * boxes
-    step = pl.program_id(1)
-
-    @pl.when(step == 0)
-    def _():
-        padded[...] = jnp.zeros_like(padded)
-        padded[1 : extent + 1, 1 : extent + 1] = saved_ref[0]
-
-    for k in range(9):
-        a, b = k // 3, k % 3
-        piece = padded[pl.ds(a, extent), pl.ds(b, extent)].reshape(bins, channels)
-        term = lax.dot_general(
-            piece,
-            slope_ref[0].reshape(bins, channels),
-            (((0,), (0,)), ((), ())),
-            preferred_element_type=jnp.float32,
-        )
-        out_ref[0, 0, k] = term[:, : channels // 2].astype(jnp.bfloat16)
-        out_ref[0, 1, k] = term[:, channels // 2 :].astype(jnp.bfloat16)
-
-
-def weight_terms(slope, saved_t):
-    layers, extent, boxes, channels = slope.shape[0], slope.shape[1], slope.shape[3], slope.shape[4]
-    block = (1, extent, extent, boxes, channels)
-    return pl.pallas_call(
-        weight_kernel,
-        name="weight_terms",
-        out_shape=jax.ShapeDtypeStruct((layers, 2, 9, channels, channels // 2), jnp.bfloat16),
-        grid=(layers, 1),
-        in_specs=[pl.BlockSpec(block, lambda l, o: (l, 0, 0, 0, 0))] * 2,
-        out_specs=pl.BlockSpec((1, 2, 9, channels, channels // 2), lambda l, o: (l, 0, o, 0, 0)),
-        scratch_shapes=[pltpu.VMEM((extent + 2, extent + 2, boxes, channels), jnp.bfloat16)],
-        compiler_params=params(24),
-        cost_estimate=pl.CostEstimate(flops=7400000000, bytes_accessed=5000000, transcendentals=0),
-    )(slope, saved_t)
+    )(box_of_slot, core.reshape(1), crops, tail, own, other)
 
 
 def hop_core():
@@ -273,14 +280,6 @@
 
 def pick(array, index):
     return lax.dynamic_index_in_dim(array, index, 0, keepdims=False)
-
-
-def sum_chip(terms, owners):
-    core = lax.axis_index("row") % 2
-    other = lax.ppermute(pick(terms, 1 - core), "row", hop_core())
-    total = pick(terms, core).astype(jnp.float32) + other.astype(jnp.float32)
-    total = jnp.pad(total, ((0, owners * SUM_ROWS - total.shape[0]), (0, 0)))
-    return total.reshape(owners, SUM_ROWS, total.shape[1])
 
 
 def ring(part, name, hop):
@@ -459,7 +458,7 @@
                 pltpu.SemaphoreType.DMA(()),
             ],
         ),
-        compiler_params=params(48),
+        compiler_params=params(58),
         cost_estimate=pl.CostEstimate(
             flops=2 * columns.size * channels, bytes_accessed=17_000_000, transcendentals=0
         ),
@@ -518,7 +517,13 @@
 
 def describe(tile_ids, corner_rows, corner_cols, row_weight, col_weight):
     pieces = tile_ids.size
-    extent = corner_rows.shape[2]
+    arrays = (
+        jnp.transpose(tile_ids),
+        jnp.transpose(corner_rows, (2, 1, 0)),
+        jnp.transpose(corner_cols, (2, 1, 0)),
+        jnp.transpose(row_weight, (1, 2, 3, 0)),
+        jnp.transpose(col_weight, (1, 2, 3, 0)),
+    )
     return pl.pallas_call(
         fields_kernel,
         name="describe",
@@ -526,17 +531,15 @@
             jax.ShapeDtypeStruct((pieces, 128), jnp.bfloat16),
             jax.ShapeDtypeStruct((2, pieces), jnp.int32),
         ),
-        in_specs=[pl.BlockSpec(memory_space=VMEM)] * 5,
-        out_specs=(pl.BlockSpec(memory_space=VMEM),) * 2,
-        compiler_params=params(8),
+        grid=(1,),
+        in_specs=[pl.BlockSpec(array.shape, lambda g, n=array.ndim: (0,) * n) for array in arrays],
+        out_specs=(
+            pl.BlockSpec((pieces, 128), lambda g: (0, 0)),
+            pl.BlockSpec((2, pieces), lambda g: (0, 0)),
+        ),
+        compiler_params=params(58),
         cost_estimate=pl.CostEstimate(flops=10_000_000, bytes_accessed=200_000, transcendentals=0),
-    )(
-        jnp.transpose(tile_ids),
-        jnp.transpose(corner_rows, (2, 1, 0)),
-        jnp.transpose(corner_cols, (2, 1, 0)),
-        jnp.transpose(row_weight, (1, 2, 3, 0)),
-        jnp.transpose(col_weight, (1, 2, 3, 0)),
-    )
+    )(*arrays)
 
 
 def arrange(slots, extent):
@@ -600,12 +603,13 @@
 
     grad_t = jnp.transpose(out_grad, (1, 2, 0, 3))
     saved_t = jnp.transpose(saved, (0, 2, 3, 1, 4))
-    slope, crops, biases = conv_chain(grad_t, saved_t, conv_weight, conv_bias)
-    terms = weight_terms(slope, saved_t)
+    lines = devices * SUM_ROWS
+    terms, crops, biases = conv_chain(grad_t, saved_t, conv_weight, conv_bias, lines)
     terms, slots = lax.optimization_barrier((terms, slots))
-    sums = sum_chip(terms.reshape(layers, -1, channels // 2), devices)
+    core = lax.axis_index("row") % 2
+    other = lax.ppermute(pick(terms, 1 - core), "row", hop_core())
     tail = biases.reshape(layers * 2, channels // 2)
-    send = pack(box_of_slot.reshape(-1), crops, tail, sums, boxes)
+    send = pack(box_of_slot.reshape(-1), core, crops, tail, terms, other, boxes)
     send, slots = lax.optimization_barrier((send, slots))
     got = lax.all_to_all(send, AXES, split_axis=0, concat_axis=0, tiled=True)
 

time: 211 us -> 204 us (0.967)
  local copies, waits for them, and re-layouts: 22.2 us -> 15.4 us
    unnamed x26 -> x8, local copies, waits for them, and re-layouts: 8.76 us -> 1.16 us
    pallas_call x1, Pallas kernels: 12.7 us -> 17.9 us  [conv_chain(): pl.pallas_call(chain_kernel, name='conv_chain', out_shape=(jax.ShapeDtype...]
    pallas_call x1 -> x0, Pallas kernels: 4.75 us -> none  [weight_terms(): pl.pallas_call(weight_kernel, name='weight_terms', out_shape=jax.ShapeDty...]
    pallas_call x1, Pallas kernels: 10.2 us -> 7.99 us  [pack(): pl.pallas_call(pack_kernel, name='pack', out_shape=jax.ShapeDtypeStruct((...]
  transfers between devices with their start and end apart: 13 -> 13, of which waited for: 8 -> 8; matrix products, arithmetic and copies ran while one was open for 10% -> 10% of each run, Pallas kernels for 27% -> 29%
where the time goes in v3:
time: 204 us; the launch traced here: 203 us
  Pallas kernels  71.9 us (35%)
  waiting for transfers between devices  59.6 us (29%)
  starting transfers between devices  43.5 us (21%)
  local copies, waits for them, and re-layouts  15.4 us (8%)
  other arithmetic  10.4 us (5%)
    all_to_all x1, waiting for transfers between devices, shards(): got = lax.all_to_all(send, AXES, split_axis=0, concat_axis=0, tiled=True)  50 us
    pallas_call x1, Pallas kernels, order_entries(): pl.pallas_call(order_kernel, name='order_entries', out_shape=jax.ShapeDty...  26.1 us
    pallas_call x1, Pallas kernels, conv_chain(): pl.pallas_call(chain_kernel, name='conv_chain', out_shape=(jax.ShapeDtype...  17.9 us
    pallas_call x1, Pallas kernels, tile_sum(): pl.pallas_call(tile_kernel, name='tile_sum', out_shape=(jax.ShapeDtypeStr...  14.8 us
    ppermute x9, starting transfers between devices, ring(): lax.ppermute(part, name, hop(k))  13.1 us
    all_to_all x1, starting transfers between devices, shards(): lax.all_to_all(slots.reshape(devices, 1, -1), AXES, split_axis=0, concat_...  11.5 us
    all_to_all x1, starting transfers between devices, shards(): got = lax.all_to_all(send, AXES, split_axis=0, concat_axis=0, tiled=True)  9.48 us
    ppermute x1, starting transfers between devices, shards(): other = lax.ppermute(own, 'row', hop_core())  8.13 us
  transfers between devices with their start and end apart: 13, of which 8 were waited for; matrix products, arithmetic and copies ran while one was open for 10% of the time, Pallas kernels for 29%

profile of v3, /device:TPU:1, one launch (start us, length us, event | category | flops | bytes accessed | tf_op | source)
XLA Modules:
  0.0 203.5 jit_solution(12223241138583593003)
XLA Ops:
  0.6 1.8 describe.1
  3.9 11.5 %all-to-all-start = ((bf16[128,1,128]{2,1,0:T(2,128)(2,1)}), bf16[128,1,128]{2,1,0:T(2,128)(2,1)S(1)}, u32[]{:S(2)}, u32[]{:S(2)}) async-start(bf16[128,1,128]{2,1,0:T(2,128)(2,1)} %copy.19), calls=%async_computation | async-start | bytes 131072 | tf_op jit(solution)/shard_map/all_to_all | solution.py:600
  15.4 17.9 %conv_chain.1 = (bf16[2,5120,128]{2,1,0:T(8,128)(2,1)}, f32[2,1568,128]{2,1,0:T(8,128)}, f32[2,256]{1,0:T(2,128)}) custom-call(bf16[7,7,32,256]{3,2,1,0:T(8,128)(2,1)} %bitcast.52, bf16[2,7,7,32,256]{4,3,2,1,0:T(8,128)(2,1)} %bitcast.51, bf16[2,9,256,256]{3,2,1,0:T(8,128)(2,1)} %weight_hbm.1, f32[2,256]{1,0:T(2,128)} %bias_ref.1), custom_call_target="tpu_custom_call" | custom-call | flops 22000001024 | bytes 9000000 | tf_op jit(solution)/shard_map/conv_chain/pallas_call | solution.py:142
  36.7 2.1 %collective-permute-done.other_ref = bf16[5120,128]{1,0:T(8,128)(2,1)S(1)} collective-permute-done((bf16[5120,128]{1,0:T(8,128)(2,1)S(1)}, bf16[5120,128]{1,0:T(8,128)(2,1)S(1)}, u32[]{:S(2)}, u32[]{:S(2)}) %collective-permute-start) | collective-permute-done | bytes 1310752 | tf_op jit(solution)/shard_map/ppermute | solution.py:610
  40.0 8.0 %pack.1 = bf16[128,240,128]{2,1,0:T(8,128)(2,1)} custom-call(s32[256]{0:T(256)} %bitcast.49, s32[1]{0:T(128)} %bitcast.3.core_ref, f32[2,1568,128]{2,1,0:T(8,128)} %get-tuple-element.21.crops_ref, f32[4,128]{1,0:T(4,128)} %reshape.131.tail_ref, bf16[2,5120,128]{2,1,0:T(8,128)(2,1)} %get-tuple-element.25.own_ref, bf16[5120,128]{1,0:T(8,128)(2,1)} %copy-done), custom_call_target="tpu_custom_call" | custom-call | flops 1000000 | bytes 9000000 | tf_op jit(solution)/shard_map/pack/pallas_call | solution.py:237
  48.0 9.5 %all-to-all-start.1 = ((bf16[128,240,128]{2,1,0:T(8,128)(2,1)}), bf16[128,240,128]{2,1,0:T(8,128)(2,1)}, u32[]{:S(2)}, u32[]{:S(2)}) async-start(bf16[128,240,128]{2,1,0:T(8,128)(2,1)} %pack.1), calls=%async_computation.1 | async-start | bytes 15728640 | tf_op jit(solution)/shard_map/all_to_all | solution.py:614
  60.5 26.1 %order_entries.1 = s32[5632]{0:T(1024)} custom-call(s32[1792]{0:T(1024)} %copy-done.1, s32[64]{0:T(128)} %get-tuple-element.47.start_ref, s32[64]{0:T(128)} %get-tuple-element.46.end_ref), custom_call_target="tpu_custom_call" | custom-call | flops 10000000 | bytes 30000000 | tf_op jit(solution)/shard_map/order_entries/pallas_call | solution.py:373
  91.0 1.8 broadcast_in_dim.81
  93.6 1.8 broadcast_in_dim.84
  96.3 1.8 eq.117
  98.1 5.4 %add_convert_fusion.columns_hbm = bf16[176,64,256]{2,1,0:T(8,128)(2,1)} fusion(f32[176,256]{1,0:T(8,128)S(1)} %broadcast_in_dim.84, f32[176,256]{1,0:T(8,128)S(1)} %broadcast_add_fusion, f32[176,256]{1,0:T(8,128)S(1)} %broadcast_in_dim.81, f32[176,256]{1,0:T(8,128)S(1)} %eq.117), kind=kLoop, calls=%fused_computation | loop fusion | flops 17301504 | bytes 6488064 | tf_op jit(solution)/shard_map/convert_element_type | solution.py:581
  103.5 50.0 %all-to-all-done.1.got_ref = bf16[128,240,128]{2,1,0:T(8,128)(2,1)} async-done(((bf16[128,240,128]{2,1,0:T(8,128)(2,1)}), bf16[128,240,128]{2,1,0:T(8,128)(2,1)}, u32[]{:S(2)}, u32[]{:S(2)}) %all-to-all-start.1) | async-done | bytes 7864352 | tf_op jit(solution)/shard_map/all_to_all | solution.py:614
  153.5 1.4 slice.43
  155.1 2.2 %collective-permute-start.3 = (bf16[2,40,128]{2,1,0:T(8,128)(2,1)S(1)}, bf16[2,40,128]{2,1,0:T(8,128)(2,1)S(1)}, u32[]{:S(2)}, u32[]{:S(2)}) collective-permute-start(bf16[2,40,128]{2,1,0:T(8,128)(2,1)S(1)} %reduce_sum.51), channel_id=1, source_target_pairs={{0,4},{1,5},{2,6},{3,7},{4,8},{5,9},{6,10},{7,11},{8,12},{9,13},{1... | collective-permute-start | bytes 61448 | tf_op jit(solution)/shard_map/ppermute | solution.py:286
  157.3 1.7 collective-permute-start.2
  161.7 1.7 collective-permute-start.5
  164.9 1.7 collective-permute-done.5
  167.1 1.7 collective-permute-done.6
  168.9 2.9 %collective-permute-start.8 = (bf16[4,4,2,40,128]{4,3,2,1,0:T(8,128)(2,1)S(1)}, bf16[4,4,2,40,128]{4,3,2,1,0:T(8,128)(2,1)S(1)}, u32[]{:S(2)}, u32[]{:S(2)}) collective-permute-start(bf16[4,4,2,40,128]{4,3,2,1,0:T(8,128)(2,1)S(1)} %pad_maximum_fusion.1), channel_id=1, source_target_pairs={{0,64},{16,80},{32,96},{48,112},{64,0},{80,16},{96,32},{112,48},{1... | collective-permute-start | bytes 983048 | tf_op jit(solution)/shard_map/ppermute | solution.py:286
  171.8 2.0 collective-permute-start.7
  174.4 14.8 %tile_sum.1 = (f32[64,64,256]{2,1,0:T(8,128)}, f32[8,128]{1,0:T(8,128)}) custom-call(s32[5632]{0:T(1024)} %get-tuple-element.37.base_ref, s32[176]{0:T(256)} %convert_reduce_fusion.place_ref, s32[1]{0:T(128)} %slice.37.groups_ref, bf16[128,240,128]{2,1,0:T(8,128)(2,1)} %all-to-all-done.1.got_ref, bf16[176,64,256]{2,1,0:T(8,128)(2,1)} %add_convert_fusion.columns_hbm), custom_call_target="tpu_custom_call" | custom-call | flops 1476395008 | bytes 17000000 | tf_op jit(solution)/shard_map/tile_sum/pallas_call | solution.py:437
  189.5 8.1 %collective-permute-start.10 = (bf16[4,4,4,2,40,128]{5,4,3,2,1,0:T(8,128)(2,1)S(1)}, bf16[4,4,4,2,40,128]{5,4,3,2,1,0:T(8,128)(2,1)S(1)}, u32[]{:S(2)}, u32[]{:S(2)}) collective-permute-start(bf16[4,4,4,2,40,128]{5,4,3,2,1,0:T(8,128)(2,1)S(1)} %pad_maximum_fusion.own_ref), channel_id=1, source_target_pairs={{0,16},{16,0},{32,48},{48,32},{64,80},{80,64},{96,112},{112,96},{1... | collective-permute-start | bytes 3932168 | tf_op jit(solution)/shard_map/ppermute | solution.py:626
  198.3 2.0 collective-permute-done.10.other_ref
  200.3 3.1 %widen.1 = f32[2,2304,256]{2,1,0:T(8,128)} custom-call(s32[4]{0:T(128)S(1)} %pad_add_fusion.place_ref, bf16[4,4,4,2,40,128]{5,4,3,2,1,0:T(8,128)(2,1)S(1)} %pad_maximum_fusion.own_ref, bf16[4,4,4,2,40,128]{5,4,3,2,1,0:T(8,128)(2,1)S(1)} %collective-permute-done.10.other_ref), custom_call_target="tpu_custom_call" | custom-call | flops 3000000 | bytes 10000000 | tf_op jit(solution)/shard_map/widen/pallas_call | solution.py:322
  (54 shorter events, 20.6 us)
Async XLA Ops:
  3.9 29.5 %all-to-all-start = ((bf16[128,1,128]{2,1,0:T(2,128)(2,1)}), bf16[128,1,128]{2,1,0:T(2,128)(2,1)S(1)}, u32[]{:S(2)}, u32[]{:S(2)}) async-start(bf16[128,1,128]{2,1,0:T(2,128)(2,1)} %copy.19), calls=%async_computation | async-start | bytes 131072 | tf_op jit(solution)/shard_map/all_to_all | solution.py:600
  33.4 2.8 %copy-start.2 = (f32[2,256]{1,0:T(2,128)S(1)}, f32[2,256]{1,0:T(2,128)}, u32[]{:S(2)}) copy-start(f32[2,256]{1,0:T(2,128)} %get-tuple-element.22) | copy-start | bytes 6148
  34.8 4.0 %collective-permute-start = (bf16[5120,128]{1,0:T(8,128)(2,1)S(1)}, bf16[5120,128]{1,0:T(8,128)(2,1)S(1)}, u32[]{:S(2)}, u32[]{:S(2)}) collective-permute-start(bf16[5120,128]{1,0:T(8,128)(2,1)S(1)} %dynamic-slice_bitcast_fusion), channel_id=1, source_target_pairs={{0,16},{16,0},{32,48},{48,32},{64,80},{80,64},{96,112},{112,96},{1... | collective-permute-start | bytes 3932168 | tf_op jit(solution)/shard_map/ppermute | solution.py:610
  38.8 1.1 copy-start
  48.0 105.5 %all-to-all-start.1 = ((bf16[128,240,128]{2,1,0:T(8,128)(2,1)}), bf16[128,240,128]{2,1,0:T(8,128)(2,1)}, u32[]{:S(2)}, u32[]{:S(2)}) async-start(bf16[128,240,128]{2,1,0:T(8,128)(2,1)} %pack.1), calls=%async_computation.1 | async-start | bytes 15728640 | tf_op jit(solution)/shard_map/all_to_all | solution.py:614
  58.3 2.3 %copy-start.1 = (s32[1792]{0:T(1024)}, s32[1792]{0:T(1024)S(1)}, u32[]{:S(2)}) copy-start(s32[1792]{0:T(1024)S(1)} %eq.107.rows_ref) | copy-start | bytes 21508
  155.1 4.9 %collective-permute-start.3 = (bf16[2,40,128]{2,1,0:T(8,128)(2,1)S(1)}, bf16[2,40,128]{2,1,0:T(8,128)(2,1)S(1)}, u32[]{:S(2)}, u32[]{:S(2)}) collective-permute-start(bf16[2,40,128]{2,1,0:T(8,128)(2,1)S(1)} %reduce_sum.51), channel_id=1, source_target_pairs={{0,4},{1,5},{2,6},{3,7},{4,8},{5,9},{6,10},{7,11},{8,12},{9,13},{1... | collective-permute-start | bytes 61448 | tf_op jit(solution)/shard_map/ppermute | solution.py:286
  157.3 4.1 %collective-permute-start.2 = (bf16[2,40,128]{2,1,0:T(8,128)(2,1)S(1)}, bf16[2,40,128]{2,1,0:T(8,128)(2,1)S(1)}, u32[]{:S(2)}, u32[]{:S(2)}) collective-permute-start(bf16[2,40,128]{2,1,0:T(8,128)(2,1)S(1)} %reduce_sum.51), channel_id=1, source_target_pairs={{0,8},{1,9},{2,10},{3,11},{4,12},{5,13},{6,14},{7,15},{8,0},{9,1},... | collective-permute-start | bytes 61448 | tf_op jit(solution)/shard_map/ppermute | solution.py:286
  159.1 2.6 %collective-permute-start.1 = (bf16[2,40,128]{2,1,0:T(8,128)(2,1)S(1)}, bf16[2,40,128]{2,1,0:T(8,128)(2,1)S(1)}, u32[]{:S(2)}, u32[]{:S(2)}) collective-permute-start(bf16[2,40,128]{2,1,0:T(8,128)(2,1)S(1)} %reduce_sum.51), channel_id=1, source_target_pairs={{0,12},{1,13},{2,14},{3,15},{4,0},{5,1},{6,2},{7,3},{8,4},{9,5},{1... | collective-permute-start | bytes 61448 | tf_op jit(solution)/shard_map/ppermute | solution.py:286
  161.7 4.9 %collective-permute-start.5 = (bf16[4,2,40,128]{3,2,1,0:T(8,128)(2,1)S(1)}, bf16[4,2,40,128]{3,2,1,0:T(8,128)(2,1)S(1)}, u32[]{:S(2)}, u32[]{:S(2)}) collective-permute-start(bf16[4,2,40,128]{3,2,1,0:T(8,128)(2,1)S(1)} %get-tuple-element.44), channel_id=1, source_target_pairs={{0,2},{1,3},{2,0},{3,1},{4,6},{5,7},{6,4},{7,5},{8,10},{9,11},{10,... | collective-permute-start | bytes 245768 | tf_op jit(solution)/shard_map/ppermute | solution.py:286
  163.5 3.6 %collective-permute-start.4 = (bf16[4,2,40,128]{3,2,1,0:T(8,128)(2,1)S(1)}, bf16[4,2,40,128]{3,2,1,0:T(8,128)(2,1)S(1)}, u32[]{:S(2)}, u32[]{:S(2)}) collective-permute-start(bf16[4,2,40,128]{3,2,1,0:T(8,128)(2,1)S(1)} %get-tuple-element.44), channel_id=1, source_target_pairs={{0,3},{1,0},{2,1},{3,2},{4,7},{5,4},{6,5},{7,6},{8,11},{9,8},{10,9... | collective-permute-start | bytes 245768 | tf_op jit(solution)/shard_map/ppermute | solution.py:286
  164.3 4.5 %collective-permute-start.6 = (bf16[4,2,40,128]{3,2,1,0:T(8,128)(2,1)S(1)}, bf16[4,2,40,128]{3,2,1,0:T(8,128)(2,1)S(1)}, u32[]{:S(2)}, u32[]{:S(2)}) collective-permute-start(bf16[4,2,40,128]{3,2,1,0:T(8,128)(2,1)S(1)} %get-tuple-element.44), channel_id=1, source_target_pairs={{0,1},{1,2},{2,3},{3,0},{4,5},{5,6},{6,7},{7,4},{8,9},{9,10},{10,1... | collective-permute-start | bytes 245768 | tf_op jit(solution)/shard_map/ppermute | solution.py:286
  168.8 20.5 %collective-permute-start.9 = (bf16[4,4,2,40,128]{4,3,2,1,0:T(8,128)(2,1)S(1)}, bf16[4,4,2,40,128]{4,3,2,1,0:T(8,128)(2,1)S(1)}, u32[]{:S(2)}, u32[]{:S(2)}) collective-permute-start(bf16[4,4,2,40,128]{4,3,2,1,0:T(8,128)(2,1)S(1)} %pad_maximum_fusion.1), channel_id=1, source_target_pairs={{0,32},{16,48},{32,64},{48,80},{64,96},{80,112},{96,0},{112,16},{1... | collective-permute-start | bytes 983048 | tf_op jit(solution)/shard_map/ppermute | solution.py:286
  168.9 20.4 %collective-permute-start.8 = (bf16[4,4,2,40,128]{4,3,2,1,0:T(8,128)(2,1)S(1)}, bf16[4,4,2,40,128]{4,3,2,1,0:T(8,128)(2,1)S(1)}, u32[]{:S(2)}, u32[]{:S(2)}) collective-permute-start(bf16[4,4,2,40,128]{4,3,2,1,0:T(8,128)(2,1)S(1)} %pad_maximum_fusion.1), channel_id=1, source_target_pairs={{0,64},{16,80},{32,96},{48,112},{64,0},{80,16},{96,32},{112,48},{1... | collective-permute-start | bytes 983048 | tf_op jit(solution)/shard_map/ppermute | solution.py:286
  171.8 17.5 %collective-permute-start.7 = (bf16[4,4,2,40,128]{4,3,2,1,0:T(8,128)(2,1)S(1)}, bf16[4,4,2,40,128]{4,3,2,1,0:T(8,128)(2,1)S(1)}, u32[]{:S(2)}, u32[]{:S(2)}) collective-permute-start(bf16[4,4,2,40,128]{4,3,2,1,0:T(8,128)(2,1)S(1)} %pad_maximum_fusion.1), channel_id=1, source_target_pairs={{0,96},{16,112},{32,0},{48,16},{64,32},{80,48},{96,64},{112,80},{1... | collective-permute-start | bytes 983048 | tf_op jit(solution)/shard_map/ppermute | solution.py:286
  189.3 8.4 %copy-start.3 = (f32[8,128]{1,0:T(8,128)S(1)}, f32[8,128]{1,0:T(8,128)}, u32[]{:S(2)}) copy-start(f32[8,128]{1,0:T(8,128)} %get-tuple-element.35) | copy-start | bytes 12292
  189.5 10.8 %collective-permute-start.10 = (bf16[4,4,4,2,40,128]{5,4,3,2,1,0:T(8,128)(2,1)S(1)}, bf16[4,4,4,2,40,128]{5,4,3,2,1,0:T(8,128)(2,1)S(1)}, u32[]{:S(2)}, u32[]{:S(2)}) collective-permute-start(bf16[4,4,4,2,40,128]{5,4,3,2,1,0:T(8,128)(2,1)S(1)} %pad_maximum_fusion.own_ref), channel_id=1, source_target_pairs={{0,16},{16,0},{32,48},{48,32},{64,80},{80,64},{96,112},{112,96},{1... | collective-permute-start | bytes 3932168 | tf_op jit(solution)/shard_map/ppermute | solution.py:626

commit v4 on v3

--- a/solution.py
+++ b/solution.py
@@ -11,7 +11,7 @@
 TILE = 64
 SUM_ROWS = 40
 GROUP = 32
-UNROLL = 8
+UNROLL = 16
 VMEM = pltpu.MemorySpace.VMEM
 SMEM = pltpu.MemorySpace.SMEM
 AXES = ("row", "col")
@@ -31,15 +31,21 @@
     saved_hbm,
     weight_hbm,
     bias_ref,
+    core_ref,
+    own_hbm,
+    give_hbm,
+    crops_hbm,
+    biases_ref,
     terms_ref,
     crops_ref,
-    biases_ref,
     both,
     slopes,
     flow,
     grad_ref,
     weight_ref,
     sems,
+    term_sems,
+    crop_sems,
 ):
     extent, boxes, channels = grad_ref.shape[0], grad_ref.shape[2], grad_ref.shape[3]
     rows = extent * boxes
@@ -58,6 +64,13 @@
     for layer in (1, 0):
         for fetch in fetches[layer]:
             fetch.start()
+
+    def crop_copy(i):
+        part = pl.ds(i * rows, rows)
+        return pltpu.make_async_copy(
+            crops_ref.at[:, part, :], crops_hbm.at[:, part, :], crop_sems.at[i]
+        )
+
     slopes[...] = jnp.zeros_like(slopes)
     edge = jnp.zeros((extent + 2, boxes, channels), jnp.bfloat16)
     for layer in (1, 0):
@@ -94,6 +107,9 @@
             sums = forward(i, sums)
         biases_ref[layer : layer + 1, :] = jnp.sum(sums, axis=0, keepdims=True)
 
+        def emit(target_hbm, layer=layer):
+            return pltpu.make_async_copy(terms_ref.at[layer], target_hbm, term_sems.at[layer])
+
         whole = slopes[1 : extent + 1, 1 : extent + 1].reshape(extent * rows, channels)
         for k in range(9):
             piece = padded[pl.ds(k // 3, extent), pl.ds(k % 3, extent)]
@@ -112,6 +128,14 @@
             (terms_ref.shape[1] - last, channels // 2), jnp.bfloat16
         )
 
+        @pl.when(core_ref[0] == layer)
+        def _(emit=emit):
+            emit(own_hbm).start()
+
+        @pl.when(core_ref[0] != layer)
+        def _(emit=emit):
+            emit(give_hbm).start()
+
         def backward(i, carry, layer=layer):
             total = jnp.zeros((rows, channels), jnp.float32)
             for a in range(3):
@@ -129,13 +153,18 @@
                 place = pl.ds(i * rows, rows)
                 crops_ref[0, place, :] = total[:, : channels // 2]
                 crops_ref[1, place, :] = total[:, channels // 2 :]
+                crop_copy(i).start()
             return carry
 
         for i in range(extent):
             backward(i, 0)
-
-
-def conv_chain(grad_t, saved_t, weight, bias, lines):
+    for layer in (1, 0):
+        pltpu.make_async_copy(terms_ref.at[layer], own_hbm, term_sems.at[layer]).wait()
+    for i in range(extent):
+        crop_copy(i).wait()
+
+
+def conv_chain(grad_t, saved_t, weight, bias, core, lines):
     extent, boxes, channels = grad_t.shape[0], grad_t.shape[2], grad_t.shape[3]
     layers = saved_t.shape[0]
     padded = (extent + 2, extent + 2, boxes, channels)
@@ -143,28 +172,33 @@
         chain_kernel,
         name="conv_chain",
         out_shape=(
-            jax.ShapeDtypeStruct((layers, lines, channels // 2), jnp.bfloat16),
+            jax.ShapeDtypeStruct((lines, channels // 2), jnp.bfloat16),
+            jax.ShapeDtypeStruct((lines, channels // 2), jnp.bfloat16),
             jax.ShapeDtypeStruct((2, extent * extent * boxes, channels // 2), jnp.float32),
             jax.ShapeDtypeStruct((layers, channels), jnp.float32),
         ),
-        in_specs=[pl.BlockSpec(memory_space=pl.ANY)] * 3 + [pl.BlockSpec(memory_space=VMEM)],
-        out_specs=(pl.BlockSpec(memory_space=VMEM),) * 3,
+        in_specs=[pl.BlockSpec(memory_space=pl.ANY)] * 3
+        + [pl.BlockSpec(memory_space=VMEM), pl.BlockSpec(memory_space=SMEM)],
+        out_specs=(pl.BlockSpec(memory_space=pl.ANY),) * 3 + (pl.BlockSpec(memory_space=VMEM),),
         scratch_shapes=[
+            pltpu.VMEM((layers, lines, channels // 2), jnp.bfloat16),
+            pltpu.VMEM((2, extent * extent * boxes, channels // 2), jnp.float32),
             pltpu.VMEM((layers,) + padded, jnp.bfloat16),
             pltpu.VMEM(padded, jnp.bfloat16),
             pltpu.VMEM((extent, extent, boxes, channels), jnp.bfloat16),
             pltpu.VMEM(grad_t.shape, jnp.bfloat16),
             pltpu.VMEM(weight.shape, jnp.bfloat16),
             pltpu.SemaphoreType.DMA((5,)),
+            pltpu.SemaphoreType.DMA((layers,)),
+            pltpu.SemaphoreType.DMA((extent,)),
         ],
         compiler_params=params(56),
         cost_estimate=pl.CostEstimate(flops=22000000000, bytes_accessed=9000000, transcendentals=0),
-    )(grad_t, saved_t, weight, bias)
+    )(grad_t, saved_t, weight, bias, core.reshape(1))
 
 
 def pack_kernel(
     box_ref,
-    core_ref,
     crops_ref,
     tail_ref,
     own_ref,
@@ -177,7 +211,6 @@
     out_ref,
     sems,
 ):
-    del core_ref
     steps = sems.shape[0]
     owners = out_ref.shape[0]
     count = owners // steps
@@ -201,7 +234,7 @@
     sends = []
     for step in range(steps):
         block = slice(step * lines, (step + 1) * lines)
-        sums[...] = own_ref[0, block, :].astype(jnp.float32) + other_ref[block, :].astype(jnp.float32)
+        sums[...] = own_ref[block, :].astype(jnp.float32) + other_ref[block, :].astype(jnp.float32)
 
         def place(index, carry, step=step):
             owner = step * count + index
@@ -229,7 +262,7 @@
         send.wait()
 
 
-def pack(box_of_slot, core, crops, tail, own, other, boxes):
+def pack(box_of_slot, crops, tail, own, other, boxes):
     owners = box_of_slot.shape[0] // 2
     steps = 16
     half = crops.shape[2]
@@ -239,13 +272,13 @@
         name="pack",
         out_shape=jax.ShapeDtypeStruct((owners, rows, half), jnp.bfloat16),
         grid_spec=pltpu.PrefetchScalarGridSpec(
-            num_scalar_prefetch=2,
+            num_scalar_prefetch=1,
             grid=(1,),
             in_specs=[
-                pl.BlockSpec(crops.shape, lambda g, ids, core: (0, 0, 0)),
-                pl.BlockSpec(tail.shape, lambda g, ids, core: (0, 0)),
-                pl.BlockSpec((1,) + other.shape, lambda g, ids, core: (core[0], 0, 0)),
-                pl.BlockSpec(other.shape, lambda g, ids, core: (0, 0)),
+                pl.BlockSpec(crops.shape, lambda g, ids: (0, 0, 0)),
+                pl.BlockSpec(tail.shape, lambda g, ids: (0, 0)),
+                pl.BlockSpec(own.shape, lambda g, ids: (0, 0)),
+                pl.BlockSpec(other.shape, lambda g, ids: (0, 0)),
             ],
             out_specs=pl.BlockSpec(memory_space=pl.ANY),
             scratch_shapes=[
@@ -259,7 +292,7 @@
         ),
         compiler_params=params(56),
         cost_estimate=pl.CostEstimate(flops=1_000_000, bytes_accessed=9_000_000, transcendentals=0),
-    )(box_of_slot, core.reshape(1), crops, tail, own, other)
+    )(box_of_slot, crops, tail, own, other)
 
 
 def hop_core():
@@ -278,15 +311,11 @@
     return [(c, (c // 4 + k) % 4 * 4 + c % 4) for c in range(16)]
 
 
-def pick(array, index):
-    return lax.dynamic_index_in_dim(array, index, 0, keepdims=False)
-
-
 def ring(part, name, hop):
     return jnp.stack([part] + [lax.ppermute(part, name, hop(k)) for k in (3, 2, 1)])
 
 
-def widen_kernel(place_ref, own_ref, other_ref, out_ref, *, scale):
+def widen_kernel(place_ref, own_ref, other_ref, out_hbm, out_ref, sems, *, scale):
     length, half = out_ref.shape[1], out_ref.shape[2] // 2
     turns = [[lax.rem(q + 4 - place_ref[axis], 4) for q in range(4)] for axis in range(3)]
 
@@ -314,6 +343,19 @@
             copy(core, own_ref)
             copy(1 - core, other_ref)
 
+    parts = sems.shape[0]
+    rows = length // parts
+    sends = []
+    for step in range(parts):
+        part = pl.ds(step * rows, rows)
+        sends.append(
+            pltpu.make_async_copy(out_ref.at[:, part, :], out_hbm.at[:, part, :], sems.at[step])
+        )
+    for send in sends:
+        send.start()
+    for send in sends:
+        send.wait()
+
 
 def widen(own, other, length, scale):
     row, col = lax.axis_index("row"), lax.axis_index("col")
@@ -328,7 +370,11 @@
             pl.BlockSpec(memory_space=VMEM),
             pl.BlockSpec(memory_space=VMEM),
         ],
-        out_specs=pl.BlockSpec(memory_space=VMEM),
+        out_specs=pl.BlockSpec(memory_space=pl.ANY),
+        scratch_shapes=[
+            pltpu.VMEM((layers, length, 2 * half), jnp.float32),
+            pltpu.SemaphoreType.DMA((8,)),
+        ],
         compiler_params=params(24),
         cost_estimate=pl.CostEstimate(flops=3_000_000, bytes_accessed=10_000_000, transcendentals=0),
     )(place, own, other)
@@ -382,87 +428,115 @@
 
 
 def tile_kernel(
-    base_ref, place_ref, groups_ref, got_ref, columns_hbm, out_ref, biases_ref, crops, columns_ref, sem
+    base_ref,
+    place_ref,
+    groups_ref,
+    got_hbm,
+    corner_ref,
+    low_ref,
+    high_ref,
+    out_hbm,
+    biases_ref,
+    landed,
+    crops,
+    out_ref,
+    sems,
+    out_sems,
 ):
-    step = pl.program_id(0)
-    owners, half = got_ref.shape[0], got_ref.shape[2]
+    steps = sems.shape[0]
+    owners, half = landed.shape[0] // steps, landed.shape[2]
     bins = 49
     block = owners * 200
-    fetch = pltpu.make_async_copy(columns_hbm, columns_ref, sem)
-
-    @pl.when(step == 0)
-    def _():
-        fetch.start()
-
-    wide = got_ref[...].astype(jnp.float32)[:, :200, :]
-    crops[pl.ds(pl.multiple_of(step * block, 8), block), :] = wide.reshape(block, half)
-    spare = jnp.sum(wide[:, 192:, :], axis=0)
-
-    @pl.when(step == 0)
-    def _():
-        biases_ref[...] = spare
-
-    @pl.when(step > 0)
-    def _():
-        biases_ref[...] += spare
-
-    @pl.when(step == pl.num_programs(0) - 1)
-    def _():
-        out_ref[...] = jnp.zeros_like(out_ref)
-        fetch.wait()
-
-        def group(t):
-            left, right = [], []
-            for n in range(GROUP):
-                base = base_ref[t * GROUP + n]
-                left.append(crops[pl.ds(base, 8), :])
-                right.append(crops[pl.ds(base + bins, 8), :])
-            values = jnp.concatenate(
-                [jnp.concatenate(left, axis=0), jnp.concatenate(right, axis=0)], axis=1
-            ).astype(jnp.bfloat16)
-            return jnp.dot(columns_ref[t], values, preferred_element_type=jnp.float32)
-
-        def several(t, carry):
-            terms = [group(t * UNROLL + u) for u in range(UNROLL)]
-            for u in range(UNROLL):
-                out_ref[place_ref[t * UNROLL + u]] += terms[u]
-            return carry
-
-        lax.fori_loop(0, (groups_ref[0] + UNROLL - 1) // UNROLL, several, 0)
-
-
-def tile_sum(base, place, groups, got, columns, channels):
-    steps = 8
+
+    def fetch(step):
+        part = pl.ds(step * owners, owners)
+        used = pl.ds(0, landed.shape[1])
+        return pltpu.make_async_copy(
+            got_hbm.at[part, used, :], landed.at[part], sems.at[step]
+        )
+
+    for step in range(steps):
+        fetch(step).start()
+    out_ref[...] = jnp.zeros_like(out_ref)
+
+    def convert(step, spare):
+        fetch(step).wait()
+        wide = landed[pl.ds(step * owners, owners)].astype(jnp.float32)[:, :200, :]
+        crops[pl.ds(pl.multiple_of(step * block, 8), block), :] = wide.reshape(block, half)
+        return spare + jnp.sum(wide[:, 192:, :], axis=0)
+
+    biases_ref[...] = lax.fori_loop(0, steps, convert, jnp.zeros(biases_ref.shape, jnp.float32))
+
+    position = lax.broadcasted_iota(jnp.int32, (TILE, corner_ref.shape[1]), 0).astype(jnp.float32)
+
+    def columns(t):
+        line = pl.ds(t, 1)
+        corner = corner_ref[line, :]
+        near = jnp.where(position == corner, low_ref[line, :], 0.0)
+        far = jnp.where(position == corner + 1.0, high_ref[line, :], 0.0)
+        return (near + far).astype(jnp.bfloat16)
+
+    def group(t):
+        left, right = [], []
+        for n in range(GROUP):
+            base = base_ref[t * GROUP + n]
+            left.append(crops[pl.ds(base, 8), :])
+            right.append(crops[pl.ds(base + bins, 8), :])
+        values = jnp.concatenate(
+            [jnp.concatenate(left, axis=0), jnp.concatenate(right, axis=0)], axis=1
+        ).astype(jnp.bfloat16)
+        return jnp.dot(columns(t), values, preferred_element_type=jnp.float32)
+
+    def several(t, carry):
+        terms = [group(t * UNROLL + u) for u in range(UNROLL)]
+        for u in range(UNROLL):
+            out_ref[place_ref[t * UNROLL + u]] += terms[u]
+        return carry
+
+    lax.fori_loop(0, (groups_ref[0] + UNROLL - 1) // UNROLL, several, 0)
+    rows = out_ref.shape[0] // out_sems.shape[0]
+    sends = []
+    for step in range(out_sems.shape[0]):
+        part = pl.ds(step * rows, rows)
+        sends.append(pltpu.make_async_copy(out_ref.at[part], out_hbm.at[part], out_sems.at[step]))
+    for send in sends:
+        send.start()
+    for send in sends:
+        send.wait()
+
+
+def tile_sum(base, place, groups, got, corner, low, high, channels):
     owners, rows, half = got.shape
+    tile = (TILE, TILE, channels)
     return pl.pallas_call(
         tile_kernel,
         name="tile_sum",
         out_shape=(
-            jax.ShapeDtypeStruct((TILE, TILE, channels), jnp.float32),
+            jax.ShapeDtypeStruct(tile, jnp.float32),
             jax.ShapeDtypeStruct((8, half), jnp.float32),
         ),
         grid_spec=pltpu.PrefetchScalarGridSpec(
             num_scalar_prefetch=3,
-            grid=(steps,),
-            in_specs=[
-                pl.BlockSpec((owners // steps, rows, half), lambda g, *refs: (g, 0, 0)),
+            grid=(1,),
+            in_specs=[pl.BlockSpec(memory_space=pl.ANY)]
+            + [pl.BlockSpec(corner.shape, lambda g, *refs: (0, 0))] * 3,
+            out_specs=(
                 pl.BlockSpec(memory_space=pl.ANY),
-            ],
-            out_specs=(
-                pl.BlockSpec((TILE, TILE, channels), lambda g, *refs: (0, 0, 0)),
                 pl.BlockSpec((8, half), lambda g, *refs: (0, 0)),
             ),
             scratch_shapes=[
+                pltpu.VMEM((owners, 208, half), jnp.bfloat16),
                 pltpu.VMEM((owners * 200, half), jnp.float32),
-                pltpu.VMEM(columns.shape, jnp.bfloat16),
-                pltpu.SemaphoreType.DMA(()),
+                pltpu.VMEM(tile, jnp.float32),
+                pltpu.SemaphoreType.DMA((16,)),
+                pltpu.SemaphoreType.DMA((8,)),
             ],
         ),
         compiler_params=params(58),
         cost_estimate=pl.CostEstimate(
-            flops=2 * columns.size * channels, bytes_accessed=17_000_000, transcendentals=0
+            flops=2 * TILE * corner.size * channels, bytes_accessed=17_000_000, transcendentals=0
         ),
-    )(base, place, groups, got, columns)
+    )(base, place, groups, got, corner, low, high)
 
 
 def fields_kernel(tiles_ref, rows_ref, cols_ref, row_weight_ref, col_weight_ref, send_ref, boxes_ref):
@@ -573,12 +647,9 @@
     high = values[:, 5 * wide : 6 * wide] * scale[:, None]
 
     def lanes(array):
-        return array.reshape(groups, 1, GROUP * wide)
-
-    corner, low, high = lanes(corner), lanes(low), lanes(high)
-    position = jnp.arange(TILE, dtype=jnp.float32)[None, :, None]
-    columns = jnp.where(position == corner, low, 0.0) + jnp.where(position == corner + 1.0, high, 0.0)
-    return base, place, ends[-1:], columns.astype(jnp.bfloat16)
+        return array.reshape(groups, GROUP * wide)
+
+    return base, place, ends[-1:], lanes(corner), lanes(low), lanes(high)
 
 
 def shards(
@@ -604,24 +675,24 @@
     grad_t = jnp.transpose(out_grad, (1, 2, 0, 3))
     saved_t = jnp.transpose(saved, (0, 2, 3, 1, 4))
     lines = devices * SUM_ROWS
-    terms, crops, biases = conv_chain(grad_t, saved_t, conv_weight, conv_bias, lines)
-    terms, slots = lax.optimization_barrier((terms, slots))
     core = lax.axis_index("row") % 2
-    other = lax.ppermute(pick(terms, 1 - core), "row", hop_core())
+    own, give, crops, biases = conv_chain(grad_t, saved_t, conv_weight, conv_bias, core, lines)
+    give, slots = lax.optimization_barrier((give, slots))
+    other = lax.ppermute(give, "row", hop_core())
     tail = biases.reshape(layers * 2, channels // 2)
-    send = pack(box_of_slot.reshape(-1), core, crops, tail, terms, other, boxes)
+    send = pack(box_of_slot.reshape(-1), crops, tail, own, other, boxes)
     send, slots = lax.optimization_barrier((send, slots))
     got = lax.all_to_all(send, AXES, split_axis=0, concat_axis=0, tiled=True)
 
-    base, place, groups, columns = arrange(slots.reshape(2 * devices, -1).astype(jnp.float32), extent)
-    got, columns = lax.optimization_barrier((got, columns))
+    base, place, groups, corner, low, high = arrange(slots.reshape(2 * devices, -1).astype(jnp.float32), extent)
+    got, corner, low, high = lax.optimization_barrier((got, corner, low, high))
     cols = lax.axis_size("col")
     arrived = got[:, 200:, :].reshape(-1, layers, cols, SUM_ROWS, channels // 2)
     part = jnp.sum(arrived.astype(jnp.float32), axis=(0, 2)).astype(jnp.bfloat16)
     part = ring(ring(part, "col", hop_z), "col", hop_y)
     part, got = lax.optimization_barrier((part, got))
     own = ring(part, "row", hop_x)
-    feature_grad, spare = tile_sum(base, place, groups, got, columns, channels)
+    feature_grad, spare = tile_sum(base, place, groups, got, corner, low, high, channels)
     own, feature_grad = lax.optimization_barrier((own, feature_grad))
     other = lax.ppermute(own, "row", hop_core())
     weight_grad = widen(own, other, 9 * channels, grad_scale)

time: 204 us -> 199 us (0.975)
  other arithmetic: 10.4 us -> 5.03 us
  Pallas kernels: 71.9 us -> 69.3 us
    reshape x0 -> x3, local copies, waits for them, and re-layouts: none -> 7.44 us  [lanes(): return array.reshape(groups, GROUP * wide)]
    convert_element_type x1 -> x0, other arithmetic: 5.42 us -> none  [arrange(): return (base, place, ends[-1:], columns.astype(jnp.bfloat16))]
    all_to_all x1, waiting for transfers between devices: 50 us -> 53.9 us  [shards(): got = lax.all_to_all(send, AXES, split_axis=0, concat_axis=0, tiled=True)]
    broadcast_in_dim x2 -> x0, local copies, waits for them, and re-layouts: 3.61 us -> none  [the longest x1 1.81 us: arrange(): jnp.where(position == corner, low, 0.0)]
    pallas_call x1, Pallas kernels: 14.8 us -> 12 us  [tile_sum(): pl.pallas_call(tile_kernel, name='tile_sum', out_shape=(jax.ShapeDtypeStr...]
    ppermute x1, starting transfers between devices: 8.13 us -> 5.48 us  [shards(): other = lax.ppermute(own, 'row', hop_core())]
  transfers between devices with their start and end apart: 13 -> 13, of which waited for: 8 -> 7; matrix products, arithmetic and copies ran while one was open for 10% -> 9% of each run, Pallas kernels for 29% -> 28%
where the time goes in v4:
time: 199 us; the launch traced here: 198 us
  Pallas kernels  69.3 us (35%)
  waiting for transfers between devices  61.6 us (31%)
  starting transfers between devices  42.3 us (21%)
  local copies, waits for them, and re-layouts  16.6 us (8%)
  other arithmetic  5.03 us (3%)
    all_to_all x1, waiting for transfers between devices, shards(): got = lax.all_to_all(send, AXES, split_axis=0, concat_axis=0, tiled=True)  53.9 us
    pallas_call x1, Pallas kernels, order_entries(): pl.pallas_call(order_kernel, name='order_entries', out_shape=jax.ShapeDty...  25.7 us
    pallas_call x1, Pallas kernels, conv_chain(): pl.pallas_call(chain_kernel, name='conv_chain', out_shape=(jax.ShapeDtype...  18.5 us
    ppermute x9, starting transfers between devices, ring(): lax.ppermute(part, name, hop(k))  14.8 us
    pallas_call x1, Pallas kernels, tile_sum(): pl.pallas_call(tile_kernel, name='tile_sum', out_shape=(jax.ShapeDtypeStr...  12 us
    all_to_all x1, starting transfers between devices, shards(): lax.all_to_all(slots.reshape(devices, 1, -1), AXES, split_axis=0, concat_...  11.5 us
    all_to_all x1, starting transfers between devices, shards(): got = lax.all_to_all(send, AXES, split_axis=0, concat_axis=0, tiled=True)  9.47 us
    pallas_call x1, Pallas kernels, pack(): pl.pallas_call(pack_kernel, name='pack', out_shape=jax.ShapeDtypeStruct((...  7.99 us
  transfers between devices with their start and end apart: 13, of which 7 were waited for; matrix products, arithmetic and copies ran while one was open for 9% of the time, Pallas kernels for 28%

profile of v4, /device:TPU:1, one launch (start us, length us, event | category | flops | bytes accessed | tf_op | source)
XLA Modules:
  0.0 197.6 jit_solution(8829028366033520225)
XLA Ops:
  0.6 1.8 describe.1
  3.9 11.5 %all-to-all-start = ((bf16[128,1,128]{2,1,0:T(2,128)(2,1)}), bf16[128,1,128]{2,1,0:T(2,128)(2,1)S(1)}, u32[]{:S(2)}, u32[]{:S(2)}) async-start(bf16[128,1,128]{2,1,0:T(2,128)(2,1)} %copy.22), calls=%async_computation | async-start | bytes 131072 | tf_op jit(solution)/shard_map/all_to_all | solution.py:671
  15.4 18.5 %conv_chain.1 = (bf16[5120,128]{1,0:T(8,128)(2,1)}, bf16[5120,128]{1,0:T(8,128)(2,1)}, f32[2,1568,128]{2,1,0:T(8,128)}, f32[2,256]{1,0:T(2,128)}) custom-call(bf16[7,7,32,256]{3,2,1,0:T(8,128)(2,1)} %bitcast.50, bf16[2,7,7,32,256]{4,3,2,1,0:T(8,128)(2,1)} %bitcast.49, bf16[2,9,256,256]{3,2,1,0:T(8,128)(2,1)} %weight_hbm.1, f32[2,256]{1,0:T(2,128)} %bias_ref.1, ...), custom_call_target="tpu_custom_call" | custom-call | flops 22000001024 | bytes 9000000 | tf_op jit(solution)/shard_map/conv_chain/pallas_call | solution.py:171
  36.3 1.6 collective-permute-done.other_ref
  39.1 8.0 %pack.1 = bf16[128,240,128]{2,1,0:T(8,128)(2,1)} custom-call(s32[256]{0:T(256)} %bitcast.47, f32[2,1568,128]{2,1,0:T(8,128)} %get-tuple-element.24.crops_ref, f32[4,128]{1,0:T(4,128)} %reshape.127.tail_ref, bf16[5120,128]{1,0:T(8,128)(2,1)} %get-tuple-element.26.own_ref, bf16[5120,128]{1,0:T(8,128)(2,1)} %copy-done), custom_call_target="tpu_custom_call" | custom-call | flops 1000000 | bytes 9000000 | tf_op jit(solution)/shard_map/pack/pallas_call | solution.py:270
  47.1 9.5 %all-to-all-start.1 = ((bf16[128,240,128]{2,1,0:T(8,128)(2,1)}), bf16[128,240,128]{2,1,0:T(8,128)(2,1)}, u32[]{:S(2)}, u32[]{:S(2)}) async-start(bf16[128,240,128]{2,1,0:T(8,128)(2,1)} %pack.1), calls=%async_computation.1 | async-start | bytes 15728640 | tf_op jit(solution)/shard_map/all_to_all | solution.py:685
  59.5 25.7 %order_entries.1 = s32[5632]{0:T(1024)} custom-call(s32[1792]{0:T(1024)} %copy-done.1, s32[64]{0:T(128)} %get-tuple-element.53.start_ref, s32[64]{0:T(128)} %get-tuple-element.52.end_ref), custom_call_target="tpu_custom_call" | custom-call | flops 10000000 | bytes 30000000 | tf_op jit(solution)/shard_map/order_entries/pallas_call | solution.py:419
  89.6 2.5 %reshape.129.corner_ref = f32[176,256]{1,0:T(8,128)} reshape(f32[5632,8]{1,0:T(8,128)S(1)} %copy.23) | data formatting | bytes 360448 | tf_op jit(solution)/shard_map/reshape | solution.py:650
  92.9 2.5 %reshape.130.low_ref = f32[176,256]{1,0:T(8,128)} reshape(f32[5632,8]{1,0:T(8,128)S(1)} %copy.24) | data formatting | bytes 360448 | tf_op jit(solution)/shard_map/reshape | solution.py:650
  96.2 2.5 %reshape.131.high_ref = f32[176,256]{1,0:T(8,128)} reshape(f32[5632,8]{1,0:T(8,128)S(1)} %copy.25) | data formatting | bytes 360448 | tf_op jit(solution)/shard_map/reshape | solution.py:650
  98.7 53.9 %all-to-all-done.1.got_hbm = bf16[128,240,128]{2,1,0:T(8,128)(2,1)} async-done(((bf16[128,240,128]{2,1,0:T(8,128)(2,1)}), bf16[128,240,128]{2,1,0:T(8,128)(2,1)}, u32[]{:S(2)}, u32[]{:S(2)}) %all-to-all-start.1) | async-done | bytes 7864352 | tf_op jit(solution)/shard_map/all_to_all | solution.py:685
  152.6 1.4 slice.43
  154.3 2.2 %collective-permute-start.3 = (bf16[2,40,128]{2,1,0:T(8,128)(2,1)S(1)}, bf16[2,40,128]{2,1,0:T(8,128)(2,1)S(1)}, u32[]{:S(2)}, u32[]{:S(2)}) collective-permute-start(bf16[2,40,128]{2,1,0:T(8,128)(2,1)S(1)} %reduce_sum.51), channel_id=1, source_target_pairs={{0,4},{1,5},{2,6},{3,7},{4,8},{5,9},{6,10},{7,11},{8,12},{9,13},{1... | collective-permute-start | bytes 61448 | tf_op jit(solution)/shard_map/ppermute | solution.py:315
  156.5 1.7 collective-permute-start.2
  159.0 1.6 collective-permute-done.2
  161.0 1.7 collective-permute-start.5
  162.7 2.0 %collective-permute-start.4 = (bf16[4,2,40,128]{3,2,1,0:T(8,128)(2,1)S(1)}, bf16[4,2,40,128]{3,2,1,0:T(8,128)(2,1)S(1)}, u32[]{:S(2)}, u32[]{:S(2)}) collective-permute-start(bf16[4,2,40,128]{3,2,1,0:T(8,128)(2,1)S(1)} %get-tuple-element.50), channel_id=1, source_target_pairs={{0,3},{1,0},{2,1},{3,2},{4,7},{5,4},{6,5},{7,6},{8,11},{9,8},{10,9... | collective-permute-start | bytes 245768 | tf_op jit(solution)/shard_map/ppermute | solution.py:315
  164.6 1.7 collective-permute-done.6
  167.0 4.4 %collective-permute-start.8 = (bf16[4,4,2,40,128]{4,3,2,1,0:T(8,128)(2,1)S(1)}, bf16[4,4,2,40,128]{4,3,2,1,0:T(8,128)(2,1)S(1)}, u32[]{:S(2)}, u32[]{:S(2)}) collective-permute-start(bf16[4,4,2,40,128]{4,3,2,1,0:T(8,128)(2,1)S(1)} %pad_maximum_fusion.1), channel_id=1, source_target_pairs={{0,64},{16,80},{32,96},{48,112},{64,0},{80,16},{96,32},{112,48},{1... | collective-permute-start | bytes 983048 | tf_op jit(solution)/shard_map/ppermute | solution.py:315
  171.4 1.8 collective-permute-start.7
  173.8 12.0 %tile_sum.1 = (f32[64,64,256]{2,1,0:T(8,128)}, f32[8,128]{1,0:T(8,128)}) custom-call(s32[5632]{0:T(1024)} %get-tuple-element.43.base_ref, s32[176]{0:T(256)} %convert_reduce_fusion.place_ref, s32[1]{0:T(128)} %slice.37.groups_ref, bf16[128,240,128]{2,1,0:T(8,128)(2,1)} %all-to-all-done.1.got_hbm, f32[176,256]{1,0:T(8,128)} %reshape.129.corner_ref, ...), custom_call_target="tpu_custom_call" | custom-call | flops 1476395008 | bytes 17000000 | tf_op jit(solution)/shard_map/tile_sum/pallas_call | solution.py:511
  186.1 5.5 %collective-permute-start.10 = (bf16[4,4,4,2,40,128]{5,4,3,2,1,0:T(8,128)(2,1)S(1)}, bf16[4,4,4,2,40,128]{5,4,3,2,1,0:T(8,128)(2,1)S(1)}, u32[]{:S(2)}, u32[]{:S(2)}) collective-permute-start(bf16[4,4,4,2,40,128]{5,4,3,2,1,0:T(8,128)(2,1)S(1)} %pad_maximum_fusion.own_ref), channel_id=1, source_target_pairs={{0,16},{16,0},{32,48},{48,32},{64,80},{80,64},{96,112},{112,96},{1... | collective-permute-start | bytes 3932168 | tf_op jit(solution)/shard_map/ppermute | solution.py:697
  192.3 2.0 %collective-permute-done.10.other_ref = bf16[4,4,4,2,40,128]{5,4,3,2,1,0:T(8,128)(2,1)S(1)} collective-permute-done((bf16[4,4,4,2,40,128]{5,4,3,2,1,0:T(8,128)(2,1)S(1)}, bf16[4,4,4,2,40,128]{5,4,3,2,1,0:T(8,128)(2,1)S(1)}, u32[]{:S(2)}, u32[]{:S(2)}) %collective-permute-start.10) | collective-permute-done | bytes 1310752 | tf_op jit(solution)/shard_map/ppermute | solution.py:697
  194.2 3.2 %widen.1 = f32[2,2304,256]{2,1,0:T(8,128)} custom-call(s32[4]{0:T(128)S(1)} %pad_add_fusion.place_ref, bf16[4,4,4,2,40,128]{5,4,3,2,1,0:T(8,128)(2,1)S(1)} %pad_maximum_fusion.own_ref, bf16[4,4,4,2,40,128]{5,4,3,2,1,0:T(8,128)(2,1)S(1)} %collective-permute-done.10.other_ref), custom_call_target="tpu_custom_call" | custom-call | flops 3000000 | bytes 10000000 | tf_op jit(solution)/shard_map/widen/pallas_call | solution.py:364
  (49 shorter events, 16.9 us)
Async XLA Ops:
  3.9 30.0 %all-to-all-start = ((bf16[128,1,128]{2,1,0:T(2,128)(2,1)}), bf16[128,1,128]{2,1,0:T(2,128)(2,1)S(1)}, u32[]{:S(2)}, u32[]{:S(2)}) async-start(bf16[128,1,128]{2,1,0:T(2,128)(2,1)} %copy.22), calls=%async_computation | async-start | bytes 131072 | tf_op jit(solution)/shard_map/all_to_all | solution.py:671
  33.9 4.0 %collective-permute-start = (bf16[5120,128]{1,0:T(8,128)(2,1)}, bf16[5120,128]{1,0:T(8,128)(2,1)S(1)}, u32[]{:S(2)}, u32[]{:S(2)}) collective-permute-start(bf16[5120,128]{1,0:T(8,128)(2,1)} %get-tuple-element.29), channel_id=1, source_target_pairs={{0,16},{16,0},{32,48},{48,32},{64,80},{80,64},{96,112},{112,96},{1... | collective-permute-start | bytes 3932168 | tf_op jit(solution)/shard_map/ppermute | solution.py:681
  37.9 1.2 copy-start
  47.1 105.5 %all-to-all-start.1 = ((bf16[128,240,128]{2,1,0:T(8,128)(2,1)}), bf16[128,240,128]{2,1,0:T(8,128)(2,1)}, u32[]{:S(2)}, u32[]{:S(2)}) async-start(bf16[128,240,128]{2,1,0:T(8,128)(2,1)} %pack.1), calls=%async_computation.1 | async-start | bytes 15728640 | tf_op jit(solution)/shard_map/all_to_all | solution.py:685
  57.4 2.1 %copy-start.1 = (s32[1792]{0:T(1024)}, s32[1792]{0:T(1024)S(1)}, u32[]{:S(2)}) copy-start(s32[1792]{0:T(1024)S(1)} %eq.78.rows_ref) | copy-start | bytes 21508
  154.3 4.7 %collective-permute-start.3 = (bf16[2,40,128]{2,1,0:T(8,128)(2,1)S(1)}, bf16[2,40,128]{2,1,0:T(8,128)(2,1)S(1)}, u32[]{:S(2)}, u32[]{:S(2)}) collective-permute-start(bf16[2,40,128]{2,1,0:T(8,128)(2,1)S(1)} %reduce_sum.51), channel_id=1, source_target_pairs={{0,4},{1,5},{2,6},{3,7},{4,8},{5,9},{6,10},{7,11},{8,12},{9,13},{1... | collective-permute-start | bytes 61448 | tf_op jit(solution)/shard_map/ppermute | solution.py:315
  156.5 4.1 %collective-permute-start.2 = (bf16[2,40,128]{2,1,0:T(8,128)(2,1)S(1)}, bf16[2,40,128]{2,1,0:T(8,128)(2,1)S(1)}, u32[]{:S(2)}, u32[]{:S(2)}) collective-permute-start(bf16[2,40,128]{2,1,0:T(8,128)(2,1)S(1)} %reduce_sum.51), channel_id=1, source_target_pairs={{0,8},{1,9},{2,10},{3,11},{4,12},{5,13},{6,14},{7,15},{8,0},{9,1},... | collective-permute-start | bytes 61448 | tf_op jit(solution)/shard_map/ppermute | solution.py:315
  158.2 2.6 %collective-permute-start.1 = (bf16[2,40,128]{2,1,0:T(8,128)(2,1)S(1)}, bf16[2,40,128]{2,1,0:T(8,128)(2,1)S(1)}, u32[]{:S(2)}, u32[]{:S(2)}) collective-permute-start(bf16[2,40,128]{2,1,0:T(8,128)(2,1)S(1)} %reduce_sum.51), channel_id=1, source_target_pairs={{0,12},{1,13},{2,14},{3,15},{4,0},{5,1},{6,2},{7,3},{8,4},{9,5},{1... | collective-permute-start | bytes 61448 | tf_op jit(solution)/shard_map/ppermute | solution.py:315
  160.8 5.4 %collective-permute-start.6 = (bf16[4,2,40,128]{3,2,1,0:T(8,128)(2,1)S(1)}, bf16[4,2,40,128]{3,2,1,0:T(8,128)(2,1)S(1)}, u32[]{:S(2)}, u32[]{:S(2)}) collective-permute-start(bf16[4,2,40,128]{3,2,1,0:T(8,128)(2,1)S(1)} %get-tuple-element.50), channel_id=1, source_target_pairs={{0,1},{1,2},{2,3},{3,0},{4,5},{5,6},{6,7},{7,4},{8,9},{9,10},{10,1... | collective-permute-start | bytes 245768 | tf_op jit(solution)/shard_map/ppermute | solution.py:315
  161.0 5.3 %collective-permute-start.5 = (bf16[4,2,40,128]{3,2,1,0:T(8,128)(2,1)S(1)}, bf16[4,2,40,128]{3,2,1,0:T(8,128)(2,1)S(1)}, u32[]{:S(2)}, u32[]{:S(2)}) collective-permute-start(bf16[4,2,40,128]{3,2,1,0:T(8,128)(2,1)S(1)} %get-tuple-element.50), channel_id=1, source_target_pairs={{0,2},{1,3},{2,0},{3,1},{4,6},{5,7},{6,4},{7,5},{8,10},{9,11},{10,... | collective-permute-start | bytes 245768 | tf_op jit(solution)/shard_map/ppermute | solution.py:315
  162.7 4.2 %collective-permute-start.4 = (bf16[4,2,40,128]{3,2,1,0:T(8,128)(2,1)S(1)}, bf16[4,2,40,128]{3,2,1,0:T(8,128)(2,1)S(1)}, u32[]{:S(2)}, u32[]{:S(2)}) collective-permute-start(bf16[4,2,40,128]{3,2,1,0:T(8,128)(2,1)S(1)} %get-tuple-element.50), channel_id=1, source_target_pairs={{0,3},{1,0},{2,1},{3,2},{4,7},{5,4},{6,5},{7,6},{8,11},{9,8},{10,9... | collective-permute-start | bytes 245768 | tf_op jit(solution)/shard_map/ppermute | solution.py:315
  166.9 19.0 %collective-permute-start.9 = (bf16[4,4,2,40,128]{4,3,2,1,0:T(8,128)(2,1)S(1)}, bf16[4,4,2,40,128]{4,3,2,1,0:T(8,128)(2,1)S(1)}, u32[]{:S(2)}, u32[]{:S(2)}) collective-permute-start(bf16[4,4,2,40,128]{4,3,2,1,0:T(8,128)(2,1)S(1)} %pad_maximum_fusion.1), channel_id=1, source_target_pairs={{0,32},{16,48},{32,64},{48,80},{64,96},{80,112},{96,0},{112,16},{1... | collective-permute-start | bytes 983048 | tf_op jit(solution)/shard_map/ppermute | solution.py:315
  167.0 18.9 %collective-permute-start.8 = (bf16[4,4,2,40,128]{4,3,2,1,0:T(8,128)(2,1)S(1)}, bf16[4,4,2,40,128]{4,3,2,1,0:T(8,128)(2,1)S(1)}, u32[]{:S(2)}, u32[]{:S(2)}) collective-permute-start(bf16[4,4,2,40,128]{4,3,2,1,0:T(8,128)(2,1)S(1)} %pad_maximum_fusion.1), channel_id=1, source_target_pairs={{0,64},{16,80},{32,96},{48,112},{64,0},{80,16},{96,32},{112,48},{1... | collective-permute-start | bytes 983048 | tf_op jit(solution)/shard_map/ppermute | solution.py:315
  171.4 14.5 %collective-permute-start.7 = (bf16[4,4,2,40,128]{4,3,2,1,0:T(8,128)(2,1)S(1)}, bf16[4,4,2,40,128]{4,3,2,1,0:T(8,128)(2,1)S(1)}, u32[]{:S(2)}, u32[]{:S(2)}) collective-permute-start(bf16[4,4,2,40,128]{4,3,2,1,0:T(8,128)(2,1)S(1)} %pad_maximum_fusion.1), channel_id=1, source_target_pairs={{0,96},{16,112},{32,0},{48,16},{64,32},{80,48},{96,64},{112,80},{1... | collective-permute-start | bytes 983048 | tf_op jit(solution)/shard_map/ppermute | solution.py:315
  185.9 5.7 %copy-start.2 = (f32[8,128]{1,0:T(8,128)S(1)}, f32[8,128]{1,0:T(8,128)}, u32[]{:S(2)}) copy-start(f32[8,128]{1,0:T(8,128)} %get-tuple-element.41) | copy-start | bytes 12292
  186.1 8.1 %collective-permute-start.10 = (bf16[4,4,4,2,40,128]{5,4,3,2,1,0:T(8,128)(2,1)S(1)}, bf16[4,4,4,2,40,128]{5,4,3,2,1,0:T(8,128)(2,1)S(1)}, u32[]{:S(2)}, u32[]{:S(2)}) collective-permute-start(bf16[4,4,4,2,40,128]{5,4,3,2,1,0:T(8,128)(2,1)S(1)} %pad_maximum_fusion.own_ref), channel_id=1, source_target_pairs={{0,16},{16,0},{32,48},{48,32},{64,80},{80,64},{96,112},{112,96},{1... | collective-permute-start | bytes 3932168 | tf_op jit(solution)/shard_map/ppermute | solution.py:697

commit v5 on v4

--- a/solution.py
+++ b/solution.py
@@ -105,7 +105,11 @@
         sums = jnp.zeros((8, channels), jnp.float32)
         for i in range(extent):
             sums = forward(i, sums)
-        biases_ref[layer : layer + 1, :] = jnp.sum(sums, axis=0, keepdims=True)
+        sums = jnp.sum(sums, axis=0, keepdims=True)
+        for half in range(2):
+            biases_ref[2 * layer + half : 2 * layer + half + 1, :] = (
+                sums[:, half * channels // 2 : (half + 1) * channels // 2]
+            )
 
         def emit(target_hbm, layer=layer):
             return pltpu.make_async_copy(terms_ref.at[layer], target_hbm, term_sems.at[layer])
@@ -175,7 +179,7 @@
             jax.ShapeDtypeStruct((lines, channels // 2), jnp.bfloat16),
             jax.ShapeDtypeStruct((lines, channels // 2), jnp.bfloat16),
             jax.ShapeDtypeStruct((2, extent * extent * boxes, channels // 2), jnp.float32),
-            jax.ShapeDtypeStruct((layers, channels), jnp.float32),
+            jax.ShapeDtypeStruct((2 * layers, channels // 2), jnp.float32),
         ),
         in_specs=[pl.BlockSpec(memory_space=pl.ANY)] * 3
         + [pl.BlockSpec(memory_space=VMEM), pl.BlockSpec(memory_space=SMEM)],
@@ -199,10 +203,10 @@
 
 def pack_kernel(
     box_ref,
-    crops_ref,
+    crops_hbm,
     tail_ref,
-    own_ref,
-    other_ref,
+    own_hbm,
+    other_hbm,
     out_hbm,
     first,
     second,
@@ -210,7 +214,17 @@
     sums,
     out_ref,
     sems,
+    crops_ref,
+    own_ref,
+    other_ref,
+    fetch_sems,
 ):
+    crops_fetch = pltpu.make_async_copy(crops_hbm, crops_ref, fetch_sems.at[0])
+    own_fetch = pltpu.make_async_copy(own_hbm, own_ref, fetch_sems.at[1])
+    other_fetch = pltpu.make_async_copy(other_hbm, other_ref, fetch_sems.at[2])
+    crops_fetch.start()
+    own_fetch.start()
+    other_fetch.start()
     steps = sems.shape[0]
     owners = out_ref.shape[0]
     count = owners // steps
@@ -218,6 +232,7 @@
     boxes = first.shape[0]
     bins = crops_ref.shape[1] // boxes
     staged[...] = jnp.zeros_like(staged)
+    crops_fetch.wait()
     for box in range(boxes):
         for half in range(2):
             rows = crops_ref[half, pl.ds(box, bins, stride=boxes), :]
@@ -231,6 +246,8 @@
     def both(left, right):
         return (left.astype(jnp.float32) + right.astype(jnp.float32)).astype(jnp.bfloat16)
 
+    own_fetch.wait()
+    other_fetch.wait()
     sends = []
     for step in range(steps):
         block = slice(step * lines, (step + 1) * lines)
@@ -275,10 +292,10 @@
             num_scalar_prefetch=1,
             grid=(1,),
             in_specs=[
-                pl.BlockSpec(crops.shape, lambda g, ids: (0, 0, 0)),
+                pl.BlockSpec(memory_space=pl.ANY),
                 pl.BlockSpec(tail.shape, lambda g, ids: (0, 0)),
-                pl.BlockSpec(own.shape, lambda g, ids: (0, 0)),
-                pl.BlockSpec(other.shape, lambda g, ids: (0, 0)),
+                pl.BlockSpec(memory_space=pl.ANY),
+                pl.BlockSpec(memory_space=pl.ANY),
             ],
             out_specs=pl.BlockSpec(memory_space=pl.ANY),
             scratch_shapes=[
@@ -288,6 +305,10 @@
                 pltpu.VMEM((owners // steps * SUM_ROWS, half), jnp.float32),
                 pltpu.VMEM((owners, rows, half), jnp.bfloat16),
                 pltpu.SemaphoreType.DMA((steps,)),
+                pltpu.VMEM(crops.shape, crops.dtype),
+                pltpu.VMEM(own.shape, own.dtype),
+                pltpu.VMEM(other.shape, other.dtype),
+                pltpu.SemaphoreType.DMA((3,)),
             ],
         ),
         compiler_params=params(56),
@@ -586,7 +607,7 @@
                 ranked, fields, (((1,), (1,)), ((), ())), preferred_element_type=jnp.float32
             )
         )
-    send_ref[...] = jnp.concatenate(slots, axis=1).astype(jnp.bfloat16)
+    send_ref[:, 0, :] = jnp.concatenate(slots, axis=1).astype(jnp.bfloat16)
 
 
 def describe(tile_ids, corner_rows, corner_cols, row_weight, col_weight):
@@ -602,13 +623,13 @@
         fields_kernel,
         name="describe",
         out_shape=(
-            jax.ShapeDtypeStruct((pieces, 128), jnp.bfloat16),
+            jax.ShapeDtypeStruct((pieces, 1, 128), jnp.bfloat16),
             jax.ShapeDtypeStruct((2, pieces), jnp.int32),
         ),
         grid=(1,),
         in_specs=[pl.BlockSpec(array.shape, lambda g, n=array.ndim: (0,) * n) for array in arrays],
         out_specs=(
-            pl.BlockSpec((pieces, 128), lambda g: (0, 0)),
+            pl.BlockSpec((pieces, 1, 128), lambda g: (0, 0, 0)),
             pl.BlockSpec((2, pieces), lambda g: (0, 0)),
         ),
         compiler_params=params(58),
@@ -668,9 +689,7 @@
     devices = lax.axis_size("row") * lax.axis_size("col")
     grad_scale = 1.0 / math.sqrt(boxes * devices * extent * extent)
     slots, box_of_slot = describe(tile_ids, corner_rows, corner_cols, row_weight, col_weight)
-    slots = lax.all_to_all(
-        slots.reshape(devices, 1, -1), AXES, split_axis=0, concat_axis=0, tiled=True
-    )
+    slots = lax.all_to_all(slots, AXES, split_axis=0, concat_axis=0, tiled=True)
 
     grad_t = jnp.transpose(out_grad, (1, 2, 0, 3))
     saved_t = jnp.transpose(saved, (0, 2, 3, 1, 4))
@@ -679,13 +698,12 @@
     own, give, crops, biases = conv_chain(grad_t, saved_t, conv_weight, conv_bias, core, lines)
     give, slots = lax.optimization_barrier((give, slots))
     other = lax.ppermute(give, "row", hop_core())
-    tail = biases.reshape(layers * 2, channels // 2)
-    send = pack(box_of_slot.reshape(-1), crops, tail, own, other, boxes)
+    send = pack(box_of_slot.reshape(-1), crops, biases, own, other, boxes)
     send, slots = lax.optimization_barrier((send, slots))
     got = lax.all_to_all(send, AXES, split_axis=0, concat_axis=0, tiled=True)
 
     base, place, groups, corner, low, high = arrange(slots.reshape(2 * devices, -1).astype(jnp.float32), extent)
-    got, corner, low, high = lax.optimization_barrier((got, corner, low, high))
+    got, place, corner, low, high = lax.optimization_barrier((got, place, corner, low, high))
     cols = lax.axis_size("col")
     arrived = got[:, 200:, :].reshape(-1, layers, cols, SUM_ROWS, channels // 2)
     part = jnp.sum(arrived.astype(jnp.float32), axis=(0, 2)).astype(jnp.bfloat16)

time: 199 us -> 196 us (0.985)
  local copies, waits for them, and re-layouts: 16.6 us -> 13.9 us
    reshape x2 -> x0, local copies, waits for them, and re-layouts: 2.71 us -> none  [the longest x1 1.43 us: shards(): slots.reshape(devices, 1, -1)]
  transfers between devices with their start and end apart: 13 -> 13, of which waited for: 7 -> 7; matrix products, arithmetic and copies ran while one was open for 9% -> 9% of each run, Pallas kernels for 28% -> 29%
where the time goes in v5:
time: 196 us; the launch traced here: 195 us
  Pallas kernels  69.3 us (35%)
  waiting for transfers between devices  61.9 us (32%)
  starting transfers between devices  42.5 us (22%)
  local copies, waits for them, and re-layouts  13.9 us (7%)
  other arithmetic  5.03 us (3%)
    all_to_all x1, waiting for transfers between devices, shards(): got = lax.all_to_all(send, AXES, split_axis=0, concat_axis=0, tiled=True)  52.9 us
    pallas_call x1, Pallas kernels, order_entries(): pl.pallas_call(order_kernel, name='order_entries', out_shape=jax.ShapeDty...  26.1 us
    pallas_call x1, Pallas kernels, conv_chain(): pl.pallas_call(chain_kernel, name='conv_chain', out_shape=(jax.ShapeDtype...  18.3 us
    ppermute x9, starting transfers between devices, ring(): lax.ppermute(part, name, hop(k))  14.8 us
    pallas_call x1, Pallas kernels, tile_sum(): pl.pallas_call(tile_kernel, name='tile_sum', out_shape=(jax.ShapeDtypeStr...  12 us
    all_to_all x1, starting transfers between devices, shards(): slots = lax.all_to_all(slots, AXES, split_axis=0, concat_axis=0, tiled=True)  11.5 us
    all_to_all x1, starting transfers between devices, shards(): got = lax.all_to_all(send, AXES, split_axis=0, concat_axis=0, tiled=True)  9.47 us
    pallas_call x1, Pallas kernels, pack(): pl.pallas_call(pack_kernel, name='pack', out_shape=jax.ShapeDtypeStruct((...  7.83 us
  transfers between devices with their start and end apart: 13, of which 7 were waited for; matrix products, arithmetic and copies ran while one was open for 9% of the time, Pallas kernels for 29%

profile of v5, /device:TPU:1, one launch (start us, length us, event | category | flops | bytes accessed | tf_op | source)
XLA Modules:
  0.0 195.4 jit_solution(440517738077957112)
XLA Ops:
  0.6 1.9 describe.1
  2.5 11.5 %all-to-all-start = ((bf16[128,1,128]{2,1,0:T(2,128)(2,1)}), bf16[128,1,128]{2,1,0:T(2,128)(2,1)S(1)}, u32[]{:S(2)}, u32[]{:S(2)}) async-start(bf16[128,1,128]{2,1,0:T(2,128)(2,1)} %get-tuple-element.29), calls=%async_computation | async-start | bytes 131072 | tf_op jit(solution)/shard_map/all_to_all | solution.py:692
  14.1 18.3 %conv_chain.1 = (bf16[5120,128]{1,0:T(8,128)(2,1)}, bf16[5120,128]{1,0:T(8,128)(2,1)}, f32[2,1568,128]{2,1,0:T(8,128)}, f32[4,128]{1,0:T(4,128)}) custom-call(bf16[7,7,32,256]{3,2,1,0:T(8,128)(2,1)} %bitcast.48, bf16[2,7,7,32,256]{4,3,2,1,0:T(8,128)(2,1)} %bitcast.47, bf16[2,9,256,256]{3,2,1,0:T(8,128)(2,1)} %weight_hbm.1, f32[2,256]{1,0:T(2,128)} %bias_ref.1, ...), custom_call_target="tpu_custom_call" | custom-call | flops 22000001024 | bytes 9000000 | tf_op jit(solution)/shard_map/conv_chain/pallas_call | solution.py:175
  33.6 2.9 %collective-permute-done.other_hbm = bf16[5120,128]{1,0:T(8,128)(2,1)S(1)} collective-permute-done((bf16[5120,128]{1,0:T(8,128)(2,1)}, bf16[5120,128]{1,0:T(8,128)(2,1)S(1)}, u32[]{:S(2)}, u32[]{:S(2)}) %collective-permute-start) | collective-permute-done | bytes 1310752 | tf_op jit(solution)/shard_map/ppermute | solution.py:700
  37.7 7.8 %pack.1 = bf16[128,240,128]{2,1,0:T(8,128)(2,1)} custom-call(s32[256]{0:T(256)} %bitcast.45, f32[2,1568,128]{2,1,0:T(8,128)} %get-tuple-element.25.crops_hbm, f32[4,128]{1,0:T(4,128)} %get-tuple-element.26.tail_ref, bf16[5120,128]{1,0:T(8,128)(2,1)} %get-tuple-element.27.own_hbm, bf16[5120,128]{1,0:T(8,128)(2,1)} %copy-done), custom_call_target="tpu_custom_call" | custom-call | flops 1000000 | bytes 9000000 | tf_op jit(solution)/shard_map/pack/pallas_call | solution.py:287
  45.5 9.5 %all-to-all-start.1 = ((bf16[128,240,128]{2,1,0:T(8,128)(2,1)}), bf16[128,240,128]{2,1,0:T(8,128)(2,1)}, u32[]{:S(2)}, u32[]{:S(2)}) async-start(bf16[128,240,128]{2,1,0:T(8,128)(2,1)} %pack.1), calls=%async_computation.1 | async-start | bytes 15728640 | tf_op jit(solution)/shard_map/all_to_all | solution.py:703
  58.0 26.1 %order_entries.1 = s32[5632]{0:T(1024)} custom-call(s32[1792]{0:T(1024)} %copy-done.1, s32[64]{0:T(128)} %get-tuple-element.55.start_ref, s32[64]{0:T(128)} %get-tuple-element.54.end_ref), custom_call_target="tpu_custom_call" | custom-call | flops 10000000 | bytes 30000000 | tf_op jit(solution)/shard_map/order_entries/pallas_call | solution.py:440
  88.4 2.5 %reshape.121.corner_ref = f32[176,256]{1,0:T(8,128)} reshape(f32[5632,8]{1,0:T(8,128)S(1)} %copy.18) | data formatting | bytes 360448 | tf_op jit(solution)/shard_map/reshape | solution.py:671
  91.7 2.5 %reshape.122.low_ref = f32[176,256]{1,0:T(8,128)} reshape(f32[5632,8]{1,0:T(8,128)S(1)} %copy.19) | data formatting | bytes 360448 | tf_op jit(solution)/shard_map/reshape | solution.py:671
  95.0 2.5 %reshape.123.high_ref = f32[176,256]{1,0:T(8,128)} reshape(f32[5632,8]{1,0:T(8,128)S(1)} %copy.20) | data formatting | bytes 360448 | tf_op jit(solution)/shard_map/reshape | solution.py:671
  98.1 52.9 %all-to-all-done.1.got_hbm = bf16[128,240,128]{2,1,0:T(8,128)(2,1)} async-done(((bf16[128,240,128]{2,1,0:T(8,128)(2,1)}), bf16[128,240,128]{2,1,0:T(8,128)(2,1)}, u32[]{:S(2)}, u32[]{:S(2)}) %all-to-all-start.1) | async-done | bytes 7864352 | tf_op jit(solution)/shard_map/all_to_all | solution.py:703
  151.0 1.4 slice.44
  152.7 2.2 %collective-permute-start.3 = (bf16[2,40,128]{2,1,0:T(8,128)(2,1)S(1)}, bf16[2,40,128]{2,1,0:T(8,128)(2,1)S(1)}, u32[]{:S(2)}, u32[]{:S(2)}) collective-permute-start(bf16[2,40,128]{2,1,0:T(8,128)(2,1)S(1)} %reduce_sum.52), channel_id=1, source_target_pairs={{0,4},{1,5},{2,6},{3,7},{4,8},{5,9},{6,10},{7,11},{8,12},{9,13},{1... | collective-permute-start | bytes 61448 | tf_op jit(solution)/shard_map/ppermute | solution.py:336
  154.9 1.7 collective-permute-start.2
  157.4 1.6 collective-permute-done.2
  159.4 1.7 collective-permute-start.5
  161.1 2.0 %collective-permute-start.4 = (bf16[4,2,40,128]{3,2,1,0:T(8,128)(2,1)S(1)}, bf16[4,2,40,128]{3,2,1,0:T(8,128)(2,1)S(1)}, u32[]{:S(2)}, u32[]{:S(2)}) collective-permute-start(bf16[4,2,40,128]{3,2,1,0:T(8,128)(2,1)S(1)} %get-tuple-element.52), channel_id=1, source_target_pairs={{0,3},{1,0},{2,1},{3,2},{4,7},{5,4},{6,5},{7,6},{8,11},{9,8},{10,9... | collective-permute-start | bytes 245768 | tf_op jit(solution)/shard_map/ppermute | solution.py:336
  163.1 1.7 collective-permute-done.6
  165.4 4.4 %collective-permute-start.8 = (bf16[4,4,2,40,128]{4,3,2,1,0:T(8,128)(2,1)S(1)}, bf16[4,4,2,40,128]{4,3,2,1,0:T(8,128)(2,1)S(1)}, u32[]{:S(2)}, u32[]{:S(2)}) collective-permute-start(bf16[4,4,2,40,128]{4,3,2,1,0:T(8,128)(2,1)S(1)} %pad_maximum_fusion.1), channel_id=1, source_target_pairs={{0,64},{16,80},{32,96},{48,112},{64,0},{80,16},{96,32},{112,48},{1... | collective-permute-start | bytes 983048 | tf_op jit(solution)/shard_map/ppermute | solution.py:336
  169.8 1.8 collective-permute-start.7
  171.6 12.0 %tile_sum.1 = (f32[64,64,256]{2,1,0:T(8,128)}, f32[8,128]{1,0:T(8,128)}) custom-call(s32[5632]{0:T(1024)} %get-tuple-element.45.base_ref, s32[176]{0:T(256)} %convert_reduce_fusion.place_ref, s32[1]{0:T(128)} %slice.38.groups_ref, bf16[128,240,128]{2,1,0:T(8,128)(2,1)} %all-to-all-done.1.got_hbm, f32[176,256]{1,0:T(8,128)} %reshape.121.corner_ref, ...), custom_call_target="tpu_custom_call" | custom-call | flops 1476395008 | bytes 17000000 | tf_op jit(solution)/shard_map/tile_sum/pallas_call | solution.py:532
  183.9 5.5 %collective-permute-start.10 = (bf16[4,4,4,2,40,128]{5,4,3,2,1,0:T(8,128)(2,1)S(1)}, bf16[4,4,4,2,40,128]{5,4,3,2,1,0:T(8,128)(2,1)S(1)}, u32[]{:S(2)}, u32[]{:S(2)}) collective-permute-start(bf16[4,4,4,2,40,128]{5,4,3,2,1,0:T(8,128)(2,1)S(1)} %pad_maximum_fusion.own_ref), channel_id=1, source_target_pairs={{0,16},{16,0},{32,48},{48,32},{64,80},{80,64},{96,112},{112,96},{1... | collective-permute-start | bytes 3932168 | tf_op jit(solution)/shard_map/ppermute | solution.py:715
  190.0 2.0 %collective-permute-done.10.other_ref = bf16[4,4,4,2,40,128]{5,4,3,2,1,0:T(8,128)(2,1)S(1)} collective-permute-done((bf16[4,4,4,2,40,128]{5,4,3,2,1,0:T(8,128)(2,1)S(1)}, bf16[4,4,4,2,40,128]{5,4,3,2,1,0:T(8,128)(2,1)S(1)}, u32[]{:S(2)}, u32[]{:S(2)}) %collective-permute-start.10) | collective-permute-done | bytes 1310752 | tf_op jit(solution)/shard_map/ppermute | solution.py:715
  192.0 3.2 %widen.1 = f32[2,2304,256]{2,1,0:T(8,128)} custom-call(s32[4]{0:T(128)S(1)} %pad_add_fusion.place_ref, bf16[4,4,4,2,40,128]{5,4,3,2,1,0:T(8,128)(2,1)S(1)} %pad_maximum_fusion.own_ref, bf16[4,4,4,2,40,128]{5,4,3,2,1,0:T(8,128)(2,1)S(1)} %collective-permute-done.10.other_ref), custom_call_target="tpu_custom_call" | custom-call | flops 3000000 | bytes 10000000 | tf_op jit(solution)/shard_map/widen/pallas_call | solution.py:385
  (47 shorter events, 14.3 us)
Async XLA Ops:
  2.5 29.8 %all-to-all-start = ((bf16[128,1,128]{2,1,0:T(2,128)(2,1)}), bf16[128,1,128]{2,1,0:T(2,128)(2,1)S(1)}, u32[]{:S(2)}, u32[]{:S(2)}) async-start(bf16[128,1,128]{2,1,0:T(2,128)(2,1)} %get-tuple-element.29), calls=%async_computation | async-start | bytes 131072 | tf_op jit(solution)/shard_map/all_to_all | solution.py:692
  32.3 4.2 %collective-permute-start = (bf16[5120,128]{1,0:T(8,128)(2,1)}, bf16[5120,128]{1,0:T(8,128)(2,1)S(1)}, u32[]{:S(2)}, u32[]{:S(2)}) collective-permute-start(bf16[5120,128]{1,0:T(8,128)(2,1)} %get-tuple-element.30), channel_id=1, source_target_pairs={{0,16},{16,0},{32,48},{48,32},{64,80},{80,64},{96,112},{112,96},{1... | collective-permute-start | bytes 3932168 | tf_op jit(solution)/shard_map/ppermute | solution.py:700
  36.5 1.2 copy-start
  45.5 105.5 %all-to-all-start.1 = ((bf16[128,240,128]{2,1,0:T(8,128)(2,1)}), bf16[128,240,128]{2,1,0:T(8,128)(2,1)}, u32[]{:S(2)}, u32[]{:S(2)}) async-start(bf16[128,240,128]{2,1,0:T(8,128)(2,1)} %pack.1), calls=%async_computation.1 | async-start | bytes 15728640 | tf_op jit(solution)/shard_map/all_to_all | solution.py:703
  55.8 2.1 %copy-start.1 = (s32[1792]{0:T(1024)}, s32[1792]{0:T(1024)S(1)}, u32[]{:S(2)}) copy-start(s32[1792]{0:T(1024)S(1)} %eq.78.rows_ref) | copy-start | bytes 21508
  152.7 4.7 %collective-permute-start.3 = (bf16[2,40,128]{2,1,0:T(8,128)(2,1)S(1)}, bf16[2,40,128]{2,1,0:T(8,128)(2,1)S(1)}, u32[]{:S(2)}, u32[]{:S(2)}) collective-permute-start(bf16[2,40,128]{2,1,0:T(8,128)(2,1)S(1)} %reduce_sum.52), channel_id=1, source_target_pairs={{0,4},{1,5},{2,6},{3,7},{4,8},{5,9},{6,10},{7,11},{8,12},{9,13},{1... | collective-permute-start | bytes 61448 | tf_op jit(solution)/shard_map/ppermute | solution.py:336
  154.9 4.1 %collective-permute-start.2 = (bf16[2,40,128]{2,1,0:T(8,128)(2,1)S(1)}, bf16[2,40,128]{2,1,0:T(8,128)(2,1)S(1)}, u32[]{:S(2)}, u32[]{:S(2)}) collective-permute-start(bf16[2,40,128]{2,1,0:T(8,128)(2,1)S(1)} %reduce_sum.52), channel_id=1, source_target_pairs={{0,8},{1,9},{2,10},{3,11},{4,12},{5,13},{6,14},{7,15},{8,0},{9,1},... | collective-permute-start | bytes 61448 | tf_op jit(solution)/shard_map/ppermute | solution.py:336
  156.6 2.6 %collective-permute-start.1 = (bf16[2,40,128]{2,1,0:T(8,128)(2,1)S(1)}, bf16[2,40,128]{2,1,0:T(8,128)(2,1)S(1)}, u32[]{:S(2)}, u32[]{:S(2)}) collective-permute-start(bf16[2,40,128]{2,1,0:T(8,128)(2,1)S(1)} %reduce_sum.52), channel_id=1, source_target_pairs={{0,12},{1,13},{2,14},{3,15},{4,0},{5,1},{6,2},{7,3},{8,4},{9,5},{1... | collective-permute-start | bytes 61448 | tf_op jit(solution)/shard_map/ppermute | solution.py:336
  159.3 5.4 %collective-permute-start.6 = (bf16[4,2,40,128]{3,2,1,0:T(8,128)(2,1)S(1)}, bf16[4,2,40,128]{3,2,1,0:T(8,128)(2,1)S(1)}, u32[]{:S(2)}, u32[]{:S(2)}) collective-permute-start(bf16[4,2,40,128]{3,2,1,0:T(8,128)(2,1)S(1)} %get-tuple-element.52), channel_id=1, source_target_pairs={{0,1},{1,2},{2,3},{3,0},{4,5},{5,6},{6,7},{7,4},{8,9},{9,10},{10,1... | collective-permute-start | bytes 245768 | tf_op jit(solution)/shard_map/ppermute | solution.py:336
  159.4 5.3 %collective-permute-start.5 = (bf16[4,2,40,128]{3,2,1,0:T(8,128)(2,1)S(1)}, bf16[4,2,40,128]{3,2,1,0:T(8,128)(2,1)S(1)}, u32[]{:S(2)}, u32[]{:S(2)}) collective-permute-start(bf16[4,2,40,128]{3,2,1,0:T(8,128)(2,1)S(1)} %get-tuple-element.52), channel_id=1, source_target_pairs={{0,2},{1,3},{2,0},{3,1},{4,6},{5,7},{6,4},{7,5},{8,10},{9,11},{10,... | collective-permute-start | bytes 245768 | tf_op jit(solution)/shard_map/ppermute | solution.py:336
  161.1 4.2 %collective-permute-start.4 = (bf16[4,2,40,128]{3,2,1,0:T(8,128)(2,1)S(1)}, bf16[4,2,40,128]{3,2,1,0:T(8,128)(2,1)S(1)}, u32[]{:S(2)}, u32[]{:S(2)}) collective-permute-start(bf16[4,2,40,128]{3,2,1,0:T(8,128)(2,1)S(1)} %get-tuple-element.52), channel_id=1, source_target_pairs={{0,3},{1,0},{2,1},{3,2},{4,7},{5,4},{6,5},{7,6},{8,11},{9,8},{10,9... | collective-permute-start | bytes 245768 | tf_op jit(solution)/shard_map/ppermute | solution.py:336
  165.3 18.3 %collective-permute-start.9 = (bf16[4,4,2,40,128]{4,3,2,1,0:T(8,128)(2,1)S(1)}, bf16[4,4,2,40,128]{4,3,2,1,0:T(8,128)(2,1)S(1)}, u32[]{:S(2)}, u32[]{:S(2)}) collective-permute-start(bf16[4,4,2,40,128]{4,3,2,1,0:T(8,128)(2,1)S(1)} %pad_maximum_fusion.1), channel_id=1, source_target_pairs={{0,32},{16,48},{32,64},{48,80},{64,96},{80,112},{96,0},{112,16},{1... | collective-permute-start | bytes 983048 | tf_op jit(solution)/shard_map/ppermute | solution.py:336
  165.4 18.2 %collective-permute-start.8 = (bf16[4,4,2,40,128]{4,3,2,1,0:T(8,128)(2,1)S(1)}, bf16[4,4,2,40,128]{4,3,2,1,0:T(8,128)(2,1)S(1)}, u32[]{:S(2)}, u32[]{:S(2)}) collective-permute-start(bf16[4,4,2,40,128]{4,3,2,1,0:T(8,128)(2,1)S(1)} %pad_maximum_fusion.1), channel_id=1, source_target_pairs={{0,64},{16,80},{32,96},{48,112},{64,0},{80,16},{96,32},{112,48},{1... | collective-permute-start | bytes 983048 | tf_op jit(solution)/shard_map/ppermute | solution.py:336
  169.8 13.8 %collective-permute-start.7 = (bf16[4,4,2,40,128]{4,3,2,1,0:T(8,128)(2,1)S(1)}, bf16[4,4,2,40,128]{4,3,2,1,0:T(8,128)(2,1)S(1)}, u32[]{:S(2)}, u32[]{:S(2)}) collective-permute-start(bf16[4,4,2,40,128]{4,3,2,1,0:T(8,128)(2,1)S(1)} %pad_maximum_fusion.1), channel_id=1, source_target_pairs={{0,96},{16,112},{32,0},{48,16},{64,32},{80,48},{96,64},{112,80},{1... | collective-permute-start | bytes 983048 | tf_op jit(solution)/shard_map/ppermute | solution.py:336
  183.7 5.7 %copy-start.2 = (f32[8,128]{1,0:T(8,128)S(1)}, f32[8,128]{1,0:T(8,128)}, u32[]{:S(2)}) copy-start(f32[8,128]{1,0:T(8,128)} %get-tuple-element.43) | copy-start | bytes 12292
  183.9 8.1 %collective-permute-start.10 = (bf16[4,4,4,2,40,128]{5,4,3,2,1,0:T(8,128)(2,1)S(1)}, bf16[4,4,4,2,40,128]{5,4,3,2,1,0:T(8,128)(2,1)S(1)}, u32[]{:S(2)}, u32[]{:S(2)}) collective-permute-start(bf16[4,4,4,2,40,128]{5,4,3,2,1,0:T(8,128)(2,1)S(1)} %pad_maximum_fusion.own_ref), channel_id=1, source_target_pairs={{0,16},{16,0},{32,48},{48,32},{64,80},{80,64},{96,112},{112,96},{1... | collective-permute-start | bytes 3932168 | tf_op jit(solution)/shard_map/ppermute | solution.py:715

commit v6 on v5

--- a/solution.py
+++ b/solution.py
@@ -688,15 +688,15 @@
     layers = saved.shape[0]
     devices = lax.axis_size("row") * lax.axis_size("col")
     grad_scale = 1.0 / math.sqrt(boxes * devices * extent * extent)
-    slots, box_of_slot = describe(tile_ids, corner_rows, corner_cols, row_weight, col_weight)
-    slots = lax.all_to_all(slots, AXES, split_axis=0, concat_axis=0, tiled=True)
 
     grad_t = jnp.transpose(out_grad, (1, 2, 0, 3))
     saved_t = jnp.transpose(saved, (0, 2, 3, 1, 4))
     lines = devices * SUM_ROWS
     core = lax.axis_index("row") % 2
     own, give, crops, biases = conv_chain(grad_t, saved_t, conv_weight, conv_bias, core, lines)
-    give, slots = lax.optimization_barrier((give, slots))
+    give, tile_ids = lax.optimization_barrier((give, tile_ids))
+    slots, box_of_slot = describe(tile_ids, corner_rows, corner_cols, row_weight, col_weight)
+    slots = lax.all_to_all(slots, AXES, split_axis=0, concat_axis=0, tiled=True)
     other = lax.ppermute(give, "row", hop_core())
     send = pack(box_of_slot.reshape(-1), crops, biases, own, other, boxes)
     send, slots = lax.optimization_barrier((send, slots))

time: 196 us -> 193 us (0.985)
  waiting for transfers between devices: 61.9 us -> 59.7 us
    ppermute x1, waiting for transfers between devices: 2.87 us -> 0.01 us  [shards(): other = lax.ppermute(give, 'row', hop_core())]
  transfers between devices with their start and end apart: 13 -> 13, of which waited for: 7 -> 8; matrix products, arithmetic and copies ran while one was open for 9% -> 9% of each run, Pallas kernels for 29% -> 25%
where the time goes in v6:
time: 193 us; the launch traced here: 192 us
  Pallas kernels  69.1 us (36%)
  waiting for transfers between devices  59.7 us (31%)
  starting transfers between devices  41.3 us (21%)
  local copies, waits for them, and re-layouts  13.9 us (7%)
  other arithmetic  5.03 us (3%)
    all_to_all x1, waiting for transfers between devices, shards(): got = lax.all_to_all(send, AXES, split_axis=0, concat_axis=0, tiled=True)  53 us
    pallas_call x1, Pallas kernels, order_entries(): pl.pallas_call(order_kernel, name='order_entries', out_shape=jax.ShapeDty...  25.9 us
    pallas_call x1, Pallas kernels, conv_chain(): pl.pallas_call(chain_kernel, name='conv_chain', out_shape=(jax.ShapeDtype...  18.3 us
    ppermute x9, starting transfers between devices, ring(): lax.ppermute(part, name, hop(k))  14.9 us
    pallas_call x1, Pallas kernels, tile_sum(): pl.pallas_call(tile_kernel, name='tile_sum', out_shape=(jax.ShapeDtypeStr...  12 us
    all_to_all x1, starting transfers between devices, shards(): slots = lax.all_to_all(slots, AXES, split_axis=0, concat_axis=0, tiled=True)  10.2 us
    all_to_all x1, starting transfers between devices, shards(): got = lax.all_to_all(send, AXES, split_axis=0, concat_axis=0, tiled=True)  9.41 us
    pallas_call x1, Pallas kernels, pack(): pl.pallas_call(pack_kernel, name='pack', out_shape=jax.ShapeDtypeStruct((...  7.83 us
  transfers between devices with their start and end apart: 13, of which 8 were waited for; matrix products, arithmetic and copies ran while one was open for 9% of the time, Pallas kernels for 25%

profile of v6, /device:TPU:1, one launch (start us, length us, event | category | flops | bytes accessed | tf_op | source)
XLA Modules:
  0.0 191.9 jit_solution(5869600344631561412)
XLA Ops:
  0.6 18.3 %conv_chain.1 = (bf16[5120,128]{1,0:T(8,128)(2,1)}, bf16[5120,128]{1,0:T(8,128)(2,1)}, f32[2,1568,128]{2,1,0:T(8,128)}, f32[4,128]{1,0:T(4,128)}) custom-call(bf16[7,7,32,256]{3,2,1,0:T(8,128)(2,1)} %bitcast.48, bf16[2,7,7,32,256]{4,3,2,1,0:T(8,128)(2,1)} %bitcast.47, bf16[2,9,256,256]{3,2,1,0:T(8,128)(2,1)} %weight_hbm.1, f32[2,256]{1,0:T(2,128)} %bias_ref.1, ...), custom_call_target="tpu_custom_call" | custom-call | flops 22000001024 | bytes 9000000 | tf_op jit(solution)/shard_map/conv_chain/pallas_call | solution.py:175
  18.9 1.7 collective-permute-start
  20.6 1.9 describe.1
  22.5 10.2 %all-to-all-start = ((bf16[128,1,128]{2,1,0:T(2,128)(2,1)}), bf16[128,1,128]{2,1,0:T(2,128)(2,1)S(1)}, u32[]{:S(2)}, u32[]{:S(2)}) async-start(bf16[128,1,128]{2,1,0:T(2,128)(2,1)} %get-tuple-element.31), calls=%async_computation | async-start | bytes 131072 | tf_op jit(solution)/shard_map/all_to_all | solution.py:699
  32.7 1.1 copy-done
  33.9 7.8 %pack.1 = bf16[128,240,128]{2,1,0:T(8,128)(2,1)} custom-call(s32[256]{0:T(256)} %bitcast.45, f32[2,1568,128]{2,1,0:T(8,128)} %get-tuple-element.27.crops_hbm, f32[4,128]{1,0:T(4,128)} %get-tuple-element.28.tail_ref, bf16[5120,128]{1,0:T(8,128)(2,1)} %get-tuple-element.29.own_hbm, bf16[5120,128]{1,0:T(8,128)(2,1)} %copy-done), custom_call_target="tpu_custom_call" | custom-call | flops 1000000 | bytes 9000000 | tf_op jit(solution)/shard_map/pack/pallas_call | solution.py:287
  42.5 9.4 %all-to-all-start.1 = ((bf16[128,240,128]{2,1,0:T(8,128)(2,1)}), bf16[128,240,128]{2,1,0:T(8,128)(2,1)}, u32[]{:S(2)}, u32[]{:S(2)}) async-start(bf16[128,240,128]{2,1,0:T(8,128)(2,1)} %pack.1), calls=%async_computation.1 | async-start | bytes 15728640 | tf_op jit(solution)/shard_map/all_to_all | solution.py:703
  54.9 25.9 %order_entries.1 = s32[5632]{0:T(1024)} custom-call(s32[1792]{0:T(1024)} %copy-done.1, s32[64]{0:T(128)} %get-tuple-element.55.start_ref, s32[64]{0:T(128)} %get-tuple-element.54.end_ref), custom_call_target="tpu_custom_call" | custom-call | flops 10000000 | bytes 30000000 | tf_op jit(solution)/shard_map/order_entries/pallas_call | solution.py:440
  81.5 1.4 fusion.9
  85.2 2.5 %reshape.121.corner_ref = f32[176,256]{1,0:T(8,128)} reshape(f32[5632,8]{1,0:T(8,128)S(1)} %copy.18) | data formatting | bytes 360448 | tf_op jit(solution)/shard_map/reshape | solution.py:671
  88.4 2.5 %reshape.122.low_ref = f32[176,256]{1,0:T(8,128)} reshape(f32[5632,8]{1,0:T(8,128)S(1)} %copy.19) | data formatting | bytes 360448 | tf_op jit(solution)/shard_map/reshape | solution.py:671
  91.7 2.5 %reshape.123.high_ref = f32[176,256]{1,0:T(8,128)} reshape(f32[5632,8]{1,0:T(8,128)S(1)} %copy.20) | data formatting | bytes 360448 | tf_op jit(solution)/shard_map/reshape | solution.py:671
  94.9 53.0 %all-to-all-done.1.got_hbm = bf16[128,240,128]{2,1,0:T(8,128)(2,1)} async-done(((bf16[128,240,128]{2,1,0:T(8,128)(2,1)}), bf16[128,240,128]{2,1,0:T(8,128)(2,1)}, u32[]{:S(2)}, u32[]{:S(2)}) %all-to-all-start.1) | async-done | bytes 7864352 | tf_op jit(solution)/shard_map/all_to_all | solution.py:703
  147.9 1.4 slice.44
  150.1 2.8 %collective-permute-start.2 = (bf16[2,40,128]{2,1,0:T(8,128)(2,1)S(1)}, bf16[2,40,128]{2,1,0:T(8,128)(2,1)S(1)}, u32[]{:S(2)}, u32[]{:S(2)}) collective-permute-start(bf16[2,40,128]{2,1,0:T(8,128)(2,1)S(1)} %reduce_sum.52), channel_id=1, source_target_pairs={{0,8},{1,9},{2,10},{3,11},{4,12},{5,13},{6,14},{7,15},{8,0},{9,1},... | collective-permute-start | bytes 61448 | tf_op jit(solution)/shard_map/ppermute | solution.py:336
  154.3 1.2 collective-permute-done.1
  156.6 3.0 %collective-permute-start.5 = (bf16[4,2,40,128]{3,2,1,0:T(8,128)(2,1)S(1)}, bf16[4,2,40,128]{3,2,1,0:T(8,128)(2,1)S(1)}, u32[]{:S(2)}, u32[]{:S(2)}) collective-permute-start(bf16[4,2,40,128]{3,2,1,0:T(8,128)(2,1)S(1)} %get-tuple-element.52), channel_id=1, source_target_pairs={{0,2},{1,3},{2,0},{3,1},{4,6},{5,7},{6,4},{7,5},{8,10},{9,11},{10,... | collective-permute-start | bytes 245768 | tf_op jit(solution)/shard_map/ppermute | solution.py:336
  159.6 1.7 collective-permute-start.4
  161.3 1.3 collective-permute-done.5
  163.0 5.4 %collective-permute-start.8 = (bf16[4,4,2,40,128]{4,3,2,1,0:T(8,128)(2,1)S(1)}, bf16[4,4,2,40,128]{4,3,2,1,0:T(8,128)(2,1)S(1)}, u32[]{:S(2)}, u32[]{:S(2)}) collective-permute-start(bf16[4,4,2,40,128]{4,3,2,1,0:T(8,128)(2,1)S(1)} %pad_maximum_fusion.1), channel_id=1, source_target_pairs={{0,64},{16,80},{32,96},{48,112},{64,0},{80,16},{96,32},{112,48},{1... | collective-permute-start | bytes 983048 | tf_op jit(solution)/shard_map/ppermute | solution.py:336
  168.3 12.0 %tile_sum.1 = (f32[64,64,256]{2,1,0:T(8,128)}, f32[8,128]{1,0:T(8,128)}) custom-call(s32[5632]{0:T(1024)} %get-tuple-element.45.base_ref, s32[176]{0:T(256)} %convert_reduce_fusion.place_ref, s32[1]{0:T(128)} %slice.38.groups_ref, bf16[128,240,128]{2,1,0:T(8,128)(2,1)} %all-to-all-done.1.got_hbm, f32[176,256]{1,0:T(8,128)} %reshape.121.corner_ref, ...), custom_call_target="tpu_custom_call" | custom-call | flops 1476395008 | bytes 17000000 | tf_op jit(solution)/shard_map/tile_sum/pallas_call | solution.py:532
  180.6 5.2 %collective-permute-start.10 = (bf16[4,4,4,2,40,128]{5,4,3,2,1,0:T(8,128)(2,1)S(1)}, bf16[4,4,4,2,40,128]{5,4,3,2,1,0:T(8,128)(2,1)S(1)}, u32[]{:S(2)}, u32[]{:S(2)}) collective-permute-start(bf16[4,4,4,2,40,128]{5,4,3,2,1,0:T(8,128)(2,1)S(1)} %pad_maximum_fusion.own_ref), channel_id=1, source_target_pairs={{0,16},{16,0},{32,48},{48,32},{64,80},{80,64},{96,112},{112,96},{1... | collective-permute-start | bytes 3932168 | tf_op jit(solution)/shard_map/ppermute | solution.py:715
  186.5 2.0 %collective-permute-done.10.other_ref = bf16[4,4,4,2,40,128]{5,4,3,2,1,0:T(8,128)(2,1)S(1)} collective-permute-done((bf16[4,4,4,2,40,128]{5,4,3,2,1,0:T(8,128)(2,1)S(1)}, bf16[4,4,4,2,40,128]{5,4,3,2,1,0:T(8,128)(2,1)S(1)}, u32[]{:S(2)}, u32[]{:S(2)}) %collective-permute-start.10) | collective-permute-done | bytes 1310752 | tf_op jit(solution)/shard_map/ppermute | solution.py:715
  188.5 3.2 %widen.1 = f32[2,2304,256]{2,1,0:T(8,128)} custom-call(s32[4]{0:T(128)S(1)} %pad_add_fusion.place_ref, bf16[4,4,4,2,40,128]{5,4,3,2,1,0:T(8,128)(2,1)S(1)} %pad_maximum_fusion.own_ref, bf16[4,4,4,2,40,128]{5,4,3,2,1,0:T(8,128)(2,1)S(1)} %collective-permute-done.10.other_ref), custom_call_target="tpu_custom_call" | custom-call | flops 3000000 | bytes 10000000 | tf_op jit(solution)/shard_map/widen/pallas_call | solution.py:385
  (47 shorter events, 12.8 us)
Async XLA Ops:
  18.9 13.8 %collective-permute-start = (bf16[5120,128]{1,0:T(8,128)(2,1)}, bf16[5120,128]{1,0:T(8,128)(2,1)S(1)}, u32[]{:S(2)}, u32[]{:S(2)}) collective-permute-start(bf16[5120,128]{1,0:T(8,128)(2,1)} %get-tuple-element.30), channel_id=1, source_target_pairs={{0,16},{16,0},{32,48},{48,32},{64,80},{80,64},{96,112},{112,96},{1... | collective-permute-start | bytes 3932168 | tf_op jit(solution)/shard_map/ppermute | solution.py:700
  22.5 20.0 %all-to-all-start = ((bf16[128,1,128]{2,1,0:T(2,128)(2,1)}), bf16[128,1,128]{2,1,0:T(2,128)(2,1)S(1)}, u32[]{:S(2)}, u32[]{:S(2)}) async-start(bf16[128,1,128]{2,1,0:T(2,128)(2,1)} %get-tuple-element.31), calls=%async_computation | async-start | bytes 131072 | tf_op jit(solution)/shard_map/all_to_all | solution.py:699
  32.7 1.2 copy-start
  42.5 105.4 %all-to-all-start.1 = ((bf16[128,240,128]{2,1,0:T(8,128)(2,1)}), bf16[128,240,128]{2,1,0:T(8,128)(2,1)}, u32[]{:S(2)}, u32[]{:S(2)}) async-start(bf16[128,240,128]{2,1,0:T(8,128)(2,1)} %pack.1), calls=%async_computation.1 | async-start | bytes 15728640 | tf_op jit(solution)/shard_map/all_to_all | solution.py:703
  52.7 2.1 %copy-start.1 = (s32[1792]{0:T(1024)}, s32[1792]{0:T(1024)S(1)}, u32[]{:S(2)}) copy-start(s32[1792]{0:T(1024)S(1)} %eq.78.rows_ref) | copy-start | bytes 21508
  149.5 3.9 %collective-permute-start.3 = (bf16[2,40,128]{2,1,0:T(8,128)(2,1)S(1)}, bf16[2,40,128]{2,1,0:T(8,128)(2,1)S(1)}, u32[]{:S(2)}, u32[]{:S(2)}) collective-permute-start(bf16[2,40,128]{2,1,0:T(8,128)(2,1)S(1)} %reduce_sum.52), channel_id=1, source_target_pairs={{0,4},{1,5},{2,6},{3,7},{4,8},{5,9},{6,10},{7,11},{8,12},{9,13},{1... | collective-permute-start | bytes 61448 | tf_op jit(solution)/shard_map/ppermute | solution.py:336
  150.1 4.1 %collective-permute-start.2 = (bf16[2,40,128]{2,1,0:T(8,128)(2,1)S(1)}, bf16[2,40,128]{2,1,0:T(8,128)(2,1)S(1)}, u32[]{:S(2)}, u32[]{:S(2)}) collective-permute-start(bf16[2,40,128]{2,1,0:T(8,128)(2,1)S(1)} %reduce_sum.52), channel_id=1, source_target_pairs={{0,8},{1,9},{2,10},{3,11},{4,12},{5,13},{6,14},{7,15},{8,0},{9,1},... | collective-permute-start | bytes 61448 | tf_op jit(solution)/shard_map/ppermute | solution.py:336
  152.9 2.6 %collective-permute-start.1 = (bf16[2,40,128]{2,1,0:T(8,128)(2,1)S(1)}, bf16[2,40,128]{2,1,0:T(8,128)(2,1)S(1)}, u32[]{:S(2)}, u32[]{:S(2)}) collective-permute-start(bf16[2,40,128]{2,1,0:T(8,128)(2,1)S(1)} %reduce_sum.52), channel_id=1, source_target_pairs={{0,12},{1,13},{2,14},{3,15},{4,0},{5,1},{6,2},{7,3},{8,4},{9,5},{1... | collective-permute-start | bytes 61448 | tf_op jit(solution)/shard_map/ppermute | solution.py:336
  155.5 5.8 %collective-permute-start.6 = (bf16[4,2,40,128]{3,2,1,0:T(8,128)(2,1)S(1)}, bf16[4,2,40,128]{3,2,1,0:T(8,128)(2,1)S(1)}, u32[]{:S(2)}, u32[]{:S(2)}) collective-permute-start(bf16[4,2,40,128]{3,2,1,0:T(8,128)(2,1)S(1)} %get-tuple-element.52), channel_id=1, source_target_pairs={{0,1},{1,2},{2,3},{3,0},{4,5},{5,6},{6,7},{7,4},{8,9},{9,10},{10,1... | collective-permute-start | bytes 245768 | tf_op jit(solution)/shard_map/ppermute | solution.py:336
  156.6 6.0 %collective-permute-start.5 = (bf16[4,2,40,128]{3,2,1,0:T(8,128)(2,1)S(1)}, bf16[4,2,40,128]{3,2,1,0:T(8,128)(2,1)S(1)}, u32[]{:S(2)}, u32[]{:S(2)}) collective-permute-start(bf16[4,2,40,128]{3,2,1,0:T(8,128)(2,1)S(1)} %get-tuple-element.52), channel_id=1, source_target_pairs={{0,2},{1,3},{2,0},{3,1},{4,6},{5,7},{6,4},{7,5},{8,10},{9,11},{10,... | collective-permute-start | bytes 245768 | tf_op jit(solution)/shard_map/ppermute | solution.py:336
  159.6 3.3 %collective-permute-start.4 = (bf16[4,2,40,128]{3,2,1,0:T(8,128)(2,1)S(1)}, bf16[4,2,40,128]{3,2,1,0:T(8,128)(2,1)S(1)}, u32[]{:S(2)}, u32[]{:S(2)}) collective-permute-start(bf16[4,2,40,128]{3,2,1,0:T(8,128)(2,1)S(1)} %get-tuple-element.52), channel_id=1, source_target_pairs={{0,3},{1,0},{2,1},{3,2},{4,7},{5,4},{6,5},{7,6},{8,11},{9,8},{10,9... | collective-permute-start | bytes 245768 | tf_op jit(solution)/shard_map/ppermute | solution.py:336
  162.9 17.5 %collective-permute-start.9 = (bf16[4,4,2,40,128]{4,3,2,1,0:T(8,128)(2,1)S(1)}, bf16[4,4,2,40,128]{4,3,2,1,0:T(8,128)(2,1)S(1)}, u32[]{:S(2)}, u32[]{:S(2)}) collective-permute-start(bf16[4,4,2,40,128]{4,3,2,1,0:T(8,128)(2,1)S(1)} %pad_maximum_fusion.1), channel_id=1, source_target_pairs={{0,32},{16,48},{32,64},{48,80},{64,96},{80,112},{96,0},{112,16},{1... | collective-permute-start | bytes 983048 | tf_op jit(solution)/shard_map/ppermute | solution.py:336
  163.0 17.4 %collective-permute-start.8 = (bf16[4,4,2,40,128]{4,3,2,1,0:T(8,128)(2,1)S(1)}, bf16[4,4,2,40,128]{4,3,2,1,0:T(8,128)(2,1)S(1)}, u32[]{:S(2)}, u32[]{:S(2)}) collective-permute-start(bf16[4,4,2,40,128]{4,3,2,1,0:T(8,128)(2,1)S(1)} %pad_maximum_fusion.1), channel_id=1, source_target_pairs={{0,64},{16,80},{32,96},{48,112},{64,0},{80,16},{96,32},{112,48},{1... | collective-permute-start | bytes 983048 | tf_op jit(solution)/shard_map/ppermute | solution.py:336
  168.3 12.1 %collective-permute-start.7 = (bf16[4,4,2,40,128]{4,3,2,1,0:T(8,128)(2,1)S(1)}, bf16[4,4,2,40,128]{4,3,2,1,0:T(8,128)(2,1)S(1)}, u32[]{:S(2)}, u32[]{:S(2)}) collective-permute-start(bf16[4,4,2,40,128]{4,3,2,1,0:T(8,128)(2,1)S(1)} %pad_maximum_fusion.1), channel_id=1, source_target_pairs={{0,96},{16,112},{32,0},{48,16},{64,32},{80,48},{96,64},{112,80},{1... | collective-permute-start | bytes 983048 | tf_op jit(solution)/shard_map/ppermute | solution.py:336
  180.4 5.5 %copy-start.2 = (f32[8,128]{1,0:T(8,128)S(1)}, f32[8,128]{1,0:T(8,128)}, u32[]{:S(2)}) copy-start(f32[8,128]{1,0:T(8,128)} %get-tuple-element.43) | copy-start | bytes 12292
  180.6 7.9 %collective-permute-start.10 = (bf16[4,4,4,2,40,128]{5,4,3,2,1,0:T(8,128)(2,1)S(1)}, bf16[4,4,4,2,40,128]{5,4,3,2,1,0:T(8,128)(2,1)S(1)}, u32[]{:S(2)}, u32[]{:S(2)}) collective-permute-start(bf16[4,4,4,2,40,128]{5,4,3,2,1,0:T(8,128)(2,1)S(1)} %pad_maximum_fusion.own_ref), channel_id=1, source_target_pairs={{0,16},{16,0},{32,48},{48,32},{64,80},{80,64},{96,112},{112,96},{1... | collective-permute-start | bytes 3932168 | tf_op jit(solution)/shard_map/ppermute | solution.py:715
